TPU v7x, 32 devices: a whole 2x2x4 slice. The times are simulated.
32 devices in a mesh: tower: 2 (over core), rows: 8 (over z, x), mp: 2 (over y).
Axes of the slice: x: 2, y: 2, z: 4, core: 2. Of those that a mesh axis runs over, the one named last changes fastest.
Arguments:
- tokens: bfloat16 [2, 8, 512, 768], P('tower', 'rows'), may hold values from -24 to 24
- segment_ids: int32 [2, 8, 512], P('tower', 'rows'), may hold values from 0 to 7, never falling along the last dimension, each value on 1 to 160 neighbouring positions
- pair_ids: int32 [64], replicated, may hold values from 0 to 63, each once
- bucket_ids: int32 [1023], replicated, may hold values from 0 to 31
- attn_gain: float32 [768], replicated, may hold values from 0.5 to 1.5
- query_weight: bfloat16 [768, 768], P(None, 'mp'), may hold values from -0.109375 to 0.109375
- key_weight: bfloat16 [768, 768], P(None, 'mp'), may hold values from -0.109375 to 0.109375
- value_weight: bfloat16 [768, 768], P(None, 'mp'), may hold values from -0.21875 to 0.21875
- output_weight: bfloat16 [768, 768], P('mp'), may hold values from -1.25 to 1.25
- bias_table: float32 [32, 12], P(None, 'mp'), may hold values from -4 to 4
- ff_gain: float32 [768], replicated, may hold values from 0.5 to 1.5
- up_weight: bfloat16 [768, 3072], P(None, 'mp'), may hold values from -0.21875 to 0.21875
- down_weight: bfloat16 [3072, 768], P('mp'), may hold values from -0.109375 to 0.109375
- final_gain: float32 [768], replicated, may hold values from 0.5 to 1.5
- proj_weight: bfloat16 [768, 768], replicated, may hold values from -6 to 6
Outputs:
- loss: float32 [], replicated
- tokens_grad: float32 [2, 8, 512, 768], P('tower', 'rows')
- attn_gain_grad: float32 [768], P(('tower', 'rows'))
- query_grad: float32 [768, 768], P(('tower', 'rows'), 'mp')
- key_grad: float32 [768, 768], P(('tower', 'rows'), 'mp')
- value_grad: float32 [768, 768], P(('tower', 'rows'), 'mp')
- output_grad: float32 [768, 768], P('mp', ('tower', 'rows'))
- bias_grad: float32 [32, 12], P(None, 'mp')
- ff_gain_grad: float32 [768], P(('tower', 'rows'))
- up_grad: float32 [768, 3072], P(('tower', 'rows'), 'mp')
- down_grad: float32 [3072, 768], P('mp', ('tower', 'rows'))
- final_gain_grad: float32 [768], P(('tower', 'rows'))
- proj_grad: float32 [768, 768], P(('tower', 'rows'))
Inputs may be any that keep to these rules, and one draw needn't show every extreme that they name: `segment_ids`: in each row the sentence numbers never fall and every one of the 8 sentences holds 1 to 160 slots, one exactly 160. A permutation; query sentence a of the query tower is paired with document sentence pair_ids[a].
All inputs are finite; a program needn't handle non-finite values.
Results may differ from a plain program's by a relative error of at most 0.022.
Values may be sent and summed in bfloat16 or wider, within the bound.
No kernel may reach another device: no remote copies, remote signals or barrier semaphores. Data moves between devices by JAX's collectives and lax.ppermute only.
A program may use at most 192 MiB of HBM per device.

v0:
```python
import functools

import jax
import jax.numpy as jnp
from jax import lax
from jax.experimental import pallas as pl
from jax.experimental.pallas import tpu as pltpu
from jax.sharding import PartitionSpec as P

SEGS_ROW = 8
BLOCK = 128

eps = 1e-06
logit_scale = 50.0
highest = lax.Precision.HIGHEST
f32 = jnp.float32
bf16 = jnp.bfloat16


def inv_rms(values):
    return lax.rsqrt(jnp.mean(values * values, -1, keepdims=True) + eps)


def dot_nn(a, b):
    return lax.dot_general(a, b, (((1,), (0,)), ((), ())), preferred_element_type=f32)


def dot_nt(a, b):
    return lax.dot_general(a, b, (((1,), (1,)), ((), ())), preferred_element_type=f32)


def dot_tn(a, b):
    return lax.dot_general(a, b, (((0,), (0,)), ((), ())), preferred_element_type=f32)


def gelu_parts(values):
    size = jnp.abs(values)
    bell = jnp.exp(-0.5 * values * values)
    t = 1.0 / (1.0 + (0.3275911 * 0.7071067811865476) * size)
    poly = t * (
        0.127414796
        + t * (-0.142248368 + t * (0.7107068705 + t * (-0.7265760135 + t * 0.5307027145)))
    )
    tail = poly * bell
    return bell, jnp.where(values >= 0, 1.0 - tail, tail)


def key_range(block, blocks):
    return max(0, block - 2), min(blocks, block + 3)


def attend_kernel(
    tok_ref, gain_ref, wq_ref, wk_ref, wv_ref, table_ref, ids_ref, seg_ref,
    n1_ref, q_ref, k_ref, v_ref, probs_ref, mix_ref,
    rel_ref, mask_ref, skew_ref,
):
    length = tok_ref.shape[0]
    blocks = length // BLOCK
    buckets = table_ref.shape[0]
    pairs = q_ref.shape[1] // BLOCK
    span = rel_ref.shape[1]
    for b in range(blocks):
        rows = slice(b * BLOCK, (b + 1) * BLOCK)
        x = tok_ref[rows, :].astype(f32)
        n1_ref[rows, :] = (x * inv_rms(x) * gain_ref[...]).astype(bf16)
    n1 = n1_ref[...]
    q_ref[...] = dot_nn(n1, wq_ref[...]).astype(bf16)
    k_ref[...] = dot_nn(n1, wk_ref[...]).astype(bf16)
    v_ref[...] = dot_nn(n1, wv_ref[...]).astype(bf16)
    hot = (lax.broadcasted_iota(jnp.int32, (buckets, span), 0) == ids_ref[...]).astype(f32)
    rel_ref[0 : table_ref.shape[1], :] = lax.dot_general(
        table_ref[...], hot, (((0,), (0,)), ((), ())), precision=highest, preferred_element_type=f32
    )
    seg_row = seg_ref[...].astype(f32)
    for b in range(blocks):
        own = jnp.broadcast_to(seg_row[:, b * BLOCK : (b + 1) * BLOCK], (BLOCK, BLOCK)).T
        for c in range(blocks):
            other = jnp.broadcast_to(seg_row[:, c * BLOCK : (c + 1) * BLOCK], (BLOCK, BLOCK))
            mask_ref[b * BLOCK : (b + 1) * BLOCK, c * BLOCK : (c + 1) * BLOCK] = jnp.where(
                own == other, 0.0, -1e30
            )
    low_lanes = lax.broadcasted_iota(jnp.int32, (BLOCK, BLOCK), 1) < BLOCK // 2
    zero = jnp.zeros((BLOCK, BLOCK), bf16)

    @pl.loop(0, pairs)
    def _(pair):
        lanes = pl.ds(pl.multiple_of(pair * BLOCK, BLOCK), BLOCK)
        for h in range(2):
            row = jnp.broadcast_to(rel_ref[pl.ds(pair * 2 + h, 1), :], (BLOCK, span))
            skew_ref[h] = pltpu.roll(row, span - (BLOCK - 1), 1, stride=1, stride_axis=0)
        for b in range(blocks):
            first, last = key_range(b, blocks)
            rows = slice(b * BLOCK, (b + 1) * BLOCK)
            keys = slice(first * BLOCK, last * BLOCK)
            shift = length - BLOCK - b * BLOCK
            q_pair = q_ref[rows, lanes]
            k_pair = k_ref[keys, lanes]
            v_pair = v_ref[keys, lanes]
            mixes = []
            for h in range(2):
                q_one = jnp.where(low_lanes if h == 0 else ~low_lanes, q_pair, zero)
                scores = (
                    dot_nt(q_one, k_pair)
                    + skew_ref[h, :, shift + first * BLOCK : shift + last * BLOCK]
                    + mask_ref[rows, keys]
                )
                most = jnp.max(scores, -1, keepdims=True)
                raised = jnp.exp(scores - most)
                probs = (raised * (1.0 / jnp.sum(raised, -1, keepdims=True))).astype(bf16)
                if first > 0:
                    probs_ref[pair * 2 + h, rows, 0 : first * BLOCK] = jnp.zeros((BLOCK, first * BLOCK), bf16)
                if last < blocks:
                    probs_ref[pair * 2 + h, rows, last * BLOCK :] = jnp.zeros(
                        (BLOCK, length - last * BLOCK), bf16
                    )
                probs_ref[pair * 2 + h, rows, keys] = probs
                mixes.append(dot_nn(probs, v_pair))
            mix_ref[rows, lanes] = jnp.where(low_lanes, mixes[0], mixes[1]).astype(bf16)


def attend_back_kernel(
    q_ref, k_ref, v_ref, probs_ref, mixg_ref, ids_ref,
    dq_ref, dk_ref, dv_ref, biasg_ref,
    ds_ref, skew_ref, rel_ref,
):
    length = q_ref.shape[0]
    blocks = length // BLOCK
    pairs = q_ref.shape[1] // BLOCK
    span = rel_ref.shape[1]
    low_lanes = lax.broadcasted_iota(jnp.int32, (BLOCK, BLOCK), 1) < BLOCK // 2
    low_all = lax.broadcasted_iota(jnp.int32, (length, BLOCK), 1) < BLOCK // 2
    zero = jnp.zeros((BLOCK, BLOCK), bf16)
    rel_ref[...] = jnp.zeros_like(rel_ref)

    @pl.loop(0, pairs)
    def _(pair):
        lanes = pl.ds(pl.multiple_of(pair * BLOCK, BLOCK), BLOCK)
        skew_ref[...] = jnp.zeros_like(skew_ref)
        for b in range(blocks):
            first, last = key_range(b, blocks)
            rows = slice(b * BLOCK, (b + 1) * BLOCK)
            keys = slice(first * BLOCK, last * BLOCK)
            shift = length - BLOCK - b * BLOCK
            g_pair = mixg_ref[rows, lanes]
            k_pair = k_ref[keys, lanes]
            v_pair = v_ref[keys, lanes]
            parts = []
            for h in range(2):
                g_one = jnp.where(low_lanes if h == 0 else ~low_lanes, g_pair, zero)
                probs = probs_ref[pair * 2 + h, rows, keys].astype(f32)
                dp = dot_nt(g_one, v_pair)
                weighted = probs * dp
                ds = weighted - probs * jnp.sum(weighted, -1, keepdims=True)
                ds_low = ds.astype(bf16)
                if first > 0:
                    ds_ref[h, rows, 0 : first * BLOCK] = jnp.zeros((BLOCK, first * BLOCK), bf16)
                if last < blocks:
                    ds_ref[h, rows, last * BLOCK :] = jnp.zeros((BLOCK, length - last * BLOCK), bf16)
                ds_ref[h, rows, keys] = ds_low
                skew_ref[h, :, shift + first * BLOCK : shift + last * BLOCK] += ds
                parts.append(dot_nn(ds_low, k_pair))
            dq_ref[rows, lanes] = jnp.where(low_lanes, parts[0], parts[1]).astype(bf16)
        q_pair = q_ref[:, lanes]
        g_pair = mixg_ref[:, lanes]
        dk_ref[:, lanes] = jnp.where(
            low_all, dot_tn(ds_ref[0], q_pair), dot_tn(ds_ref[1], q_pair)
        ).astype(bf16)
        dv_ref[:, lanes] = jnp.where(
            low_all,
            dot_tn(probs_ref[pair * 2], g_pair),
            dot_tn(probs_ref[pair * 2 + 1], g_pair),
        ).astype(bf16)
        for h in range(2):
            tiles = skew_ref[h, BLOCK - 8 :, :]
            for r in range(0, BLOCK - 8, 8):
                tiles += pltpu.roll(skew_ref[h, r : r + 8, :], BLOCK - 8 - r, 1)
            line = tiles[7:8, :]
            for r in range(7):
                line += pltpu.roll(tiles[r : r + 1, :], 7 - r, 1)
            rel_ref[pl.ds(pair * 2 + h, 1), :] = line

    hot = (lax.broadcasted_iota(jnp.int32, (biasg_ref.shape[0], span), 0) == ids_ref[...]).astype(f32)
    total = lax.dot_general(
        hot, rel_ref[...], (((1,), (1,)), ((), ())), precision=highest, preferred_element_type=f32
    )
    biasg_ref[...] = total[:, : biasg_ref.shape[1]]


def whole(kernel, out_shapes, scratch, *args):
    return pl.pallas_call(
        kernel,
        out_shape=out_shapes,
        in_specs=[pl.BlockSpec(memory_space=pltpu.VMEM)] * len(args),
        out_specs=jax.tree.map(lambda _: pl.BlockSpec(memory_space=pltpu.VMEM), out_shapes),
        scratch_shapes=scratch,
        compiler_params=pltpu.CompilerParams(vmem_limit_bytes=56 * 1024 * 1024),
    )(*args)


def swap(values, axis, bit=1):
    count = lax.axis_size(axis)
    return lax.ppermute(values, axis, [(i, i ^ bit) for i in range(count)])


def mp_sum(part):
    own = lax.optimization_barrier(part.astype(bf16))
    return own.astype(f32) + swap(own, "mp").astype(f32)


def gather_all(values):
    rows_index = lax.axis_index("rows")
    out = values[None]
    bit = 1
    while bit < lax.axis_size("rows"):
        other = swap(out, "rows", bit)
        is_high = (rows_index & bit) > 0
        out = jnp.concatenate(
            [jnp.where(is_high, other, out), jnp.where(is_high, out, other)], 0
        )
        bit *= 2
    other = swap(out, "tower")
    is_high = lax.axis_index("tower") > 0
    return jnp.concatenate([jnp.where(is_high, other, out), jnp.where(is_high, out, other)], 0)


def rows_scatter(cur, shard):
    rows_index = lax.axis_index("rows")
    bit = 1
    while bit < lax.axis_size("rows"):
        columns = cur.shape[1]
        view = cur.reshape(-1, 2, shard, columns)
        own_bit = (rows_index & bit) // bit
        keep = lax.dynamic_index_in_dim(view, own_bit, 1, False).reshape(-1, columns)
        send = lax.dynamic_index_in_dim(view, 1 - own_bit, 1, False).reshape(-1, columns)
        cur = keep.astype(f32) + swap(send, "rows", bit).astype(f32)
        bit *= 2
        if bit < lax.axis_size("rows"):
            cur = lax.optimization_barrier(cur.astype(bf16))
    return cur


def weight_scatter(left, right):
    tower_index = lax.axis_index("tower")
    half = left.shape[1] // 2
    other_left = lax.dynamic_slice_in_dim(left, (1 - tower_index) * half, half, 1)
    own_left = lax.dynamic_slice_in_dim(left, tower_index * half, half, 1)
    received = swap(dot_tn(other_left, right).astype(bf16), "tower")
    total = (dot_tn(own_left, right) + received.astype(f32)).astype(bf16)
    return rows_scatter(total, half // lax.axis_size("rows"))


def per_device(
    tokens,
    segment_ids,
    pair_ids,
    bucket_ids,
    attn_gain,
    query_weight,
    key_weight,
    value_weight,
    output_weight,
    bias_table,
    ff_gain,
    up_weight,
    down_weight,
    final_gain,
    proj_weight,
):
    length = tokens.shape[2]
    width = tokens.shape[3]
    inner = query_weight.shape[1]
    head_count = bias_table.shape[1]
    bucket_count = bias_table.shape[0]
    total_segs = pair_ids.shape[0]
    span = 2 * length
    tower_index = lax.axis_index("tower")
    device_index = tower_index * lax.axis_size("rows") + lax.axis_index("rows")
    shard = width // (2 * lax.axis_size("rows"))

    token_row = tokens.reshape(length, width)
    residual = token_row.astype(f32)
    segments = segment_ids.reshape(1, length)
    ids_row = jnp.pad(bucket_ids, (0, 1), constant_values=-1).reshape(1, span)

    def struct(shape, dtype):
        return jax.ShapeDtypeStruct(shape, dtype)

    normed_one, query, key, value, probs, attn_mix = whole(
        attend_kernel,
        (
            struct((length, width), bf16),
            struct((length, inner), bf16),
            struct((length, inner), bf16),
            struct((length, inner), bf16),
            struct((head_count, length, length), bf16),
            struct((length, inner), bf16),
        ),
        [
            pltpu.VMEM((8, span), f32),
            pltpu.VMEM((length, length), f32),
            pltpu.VMEM((2, BLOCK, span), f32),
        ],
        token_row,
        attn_gain.reshape(1, width),
        query_weight,
        key_weight,
        value_weight,
        bias_table,
        ids_row,
        segments,
    )
    hidden_one = residual + mp_sum(dot_nn(attn_mix, output_weight))
    inv_two = inv_rms(hidden_one)
    normed_two = (hidden_one * inv_two * ff_gain).astype(bf16)
    up_out = dot_nn(normed_two, up_weight)
    bell, below = gelu_parts(up_out)
    active = (up_out * below).astype(bf16)
    slope = below + up_out * bell * 0.3989422804014327
    hidden_two = hidden_one + mp_sum(dot_nn(active, down_weight))
    inv_final = inv_rms(hidden_two)
    final_out = hidden_two * inv_final * final_gain
    member = (segments == lax.broadcasted_iota(jnp.int32, (SEGS_ROW, 1), 0)).astype(f32)
    counts = jnp.sum(member, -1, keepdims=True)
    pooled = jnp.dot(member, final_out, precision=highest) / counts
    all_pooled = gather_all(pooled.astype(bf16)).reshape(2 * total_segs, width)

    embedding = dot_nn(all_pooled, proj_weight)
    inv_unit = lax.rsqrt(jnp.sum(embedding * embedding, -1, keepdims=True) + eps)
    unit_vec = embedding * inv_unit
    unit_low = unit_vec.astype(bf16)
    query_unit, doc_unit = unit_low[:total_segs], unit_low[total_segs:]
    logits = logit_scale * dot_nt(query_unit, doc_unit)
    positive = (
        pair_ids[:, None] == lax.broadcasted_iota(jnp.int32, (1, total_segs), 1)
    ).astype(f32)
    row_norm = jax.nn.logsumexp(logits, 1, keepdims=True)
    col_norm = jax.nn.logsumexp(logits, 0, keepdims=True)
    half_share = 0.5 / total_segs
    loss_value = half_share * (
        jnp.sum(row_norm) + jnp.sum(col_norm) - 2.0 * jnp.sum(logits * positive)
    )
    logit_grad = (
        half_share * (jnp.exp(logits - row_norm) + jnp.exp(logits - col_norm) - 2.0 * positive)
    ).astype(bf16)
    unit_grad = logit_scale * jnp.concatenate(
        [dot_nn(logit_grad, doc_unit), dot_tn(logit_grad, query_unit)], 0
    )
    embed_grad = (
        (unit_grad - unit_vec * jnp.sum(unit_vec * unit_grad, -1, keepdims=True)) * inv_unit
    ).astype(bf16)
    own_embed = lax.dynamic_slice_in_dim(embed_grad, device_index * SEGS_ROW, SEGS_ROW, 0)
    proj_grad = lax.dynamic_slice_in_dim(
        dot_tn(all_pooled, embed_grad), device_index * shard, shard, 0
    )
    pooled_grad = dot_nt(own_embed, proj_weight) / counts
    final_grad = lax.dot_general(
        member, pooled_grad, (((0,), (0,)), ((), ())), precision=highest, preferred_element_type=f32
    )

    def norm_back(values, inv, gain, grad):
        scaled = grad * gain
        inner_mean = jnp.mean(values * scaled, -1, keepdims=True)
        return (
            inv * scaled - values * (inv * inv * inv * inner_mean),
            jnp.sum(values * inv * grad, 0),
        )

    hidden_two_grad, final_gain_grad = norm_back(hidden_two, inv_final, final_gain, final_grad)
    ff_grad = hidden_two_grad.astype(bf16)
    up_out_grad = (dot_nt(ff_grad, down_weight) * slope).astype(bf16)
    normed_two_grad = mp_sum(dot_nt(up_out_grad, up_weight))
    down_sum = weight_scatter(ff_grad, active).T
    up_sum = weight_scatter(normed_two, up_out_grad)
    part, ff_gain_grad = norm_back(hidden_one, inv_two, ff_gain, normed_two_grad)
    hidden_one_grad = hidden_two_grad + part
    attn_grad = hidden_one_grad.astype(bf16)
    output_sum = weight_scatter(attn_grad, attn_mix).T
    mix_grad = dot_nt(attn_grad, output_weight).astype(bf16)

    query_g, key_g, value_g, bias_g = whole(
        attend_back_kernel,
        (
            struct((length, inner), bf16),
            struct((length, inner), bf16),
            struct((length, inner), bf16),
            struct((bucket_count, head_count), f32),
        ),
        [
            pltpu.VMEM((2, length, length), bf16),
            pltpu.VMEM((2, BLOCK, span), f32),
            pltpu.VMEM((8, span), f32),
        ],
        query,
        key,
        value,
        probs,
        mix_grad,
        ids_row,
    )
    normed_one_grad = mp_sum(
        dot_nt(query_g, query_weight) + dot_nt(key_g, key_weight) + dot_nt(value_g, value_weight)
    )
    qkv_sum = weight_scatter(normed_one, jnp.concatenate([query_g, key_g, value_g], 1))
    part, attn_gain_grad = norm_back(residual, inv_rms(residual), attn_gain, normed_one_grad)
    tokens_grad = (hidden_one_grad + part).reshape(tokens.shape)

    gains = jnp.stack([attn_gain_grad, ff_gain_grad, final_gain_grad], 1)
    bias_columns = -(-bucket_count * head_count // shard)
    bias_flat = jnp.pad(bias_g.reshape(-1), (0, bias_columns * shard - bucket_count * head_count))
    bias_part = jnp.tile(bias_flat.reshape(shard, bias_columns), (width // shard, 1))
    small = lax.optimization_barrier(jnp.concatenate([gains, bias_part], 1))
    halves = small.reshape(2, width // 2, -1)
    small = lax.dynamic_index_in_dim(halves, tower_index, 0, False) + swap(
        lax.dynamic_index_in_dim(halves, 1 - tower_index, 0, False), "tower"
    )
    bit = 1
    while bit < lax.axis_size("rows"):
        view = small.reshape(-1, 2, shard, small.shape[-1])
        own_bit = (lax.axis_index("rows") & bit) // bit
        small = lax.dynamic_index_in_dim(view, own_bit, 1, False) + swap(
            lax.dynamic_index_in_dim(view, 1 - own_bit, 1, False), "rows", bit
        )
        bit *= 2
    small = small.reshape(shard, -1)
    bias_total = small[:, 3:].reshape(-1)[: bucket_count * head_count].reshape(
        bucket_count, head_count
    )
    return (
        loss_value,
        tokens_grad,
        small[:, 0],
        qkv_sum[:, :inner],
        qkv_sum[:, inner : 2 * inner],
        qkv_sum[:, 2 * inner :],
        output_sum,
        bias_total,
        small[:, 1],
        up_sum,
        down_sum,
        small[:, 2],
        proj_grad,
    )


def solution(mesh):
    in_specs = (
        P("tower", "rows", None, None),
        P("tower", "rows", None),
        P(),
        P(),
        P(),
        P(None, "mp"),
        P(None, "mp"),
        P(None, "mp"),
        P("mp", None),
        P(None, "mp"),
        P(),
        P(None, "mp"),
        P("mp", None),
        P(),
        P(),
    )
    out_specs = (
        P(),
        P("tower", "rows", None, None),
        P(("tower", "rows")),
        P(("tower", "rows"), "mp"),
        P(("tower", "rows"), "mp"),
        P(("tower", "rows"), "mp"),
        P("mp", ("tower", "rows")),
        P(None, "mp"),
        P(("tower", "rows")),
        P(("tower", "rows"), "mp"),
        P("mp", ("tower", "rows")),
        P(("tower", "rows")),
        P(("tower", "rows"), None),
    )
    return jax.shard_map(
        per_device, mesh=mesh, in_specs=in_specs, out_specs=out_specs, check_vma=False
    )
```

profile of v0, /device:TPU:0, one launch (start us, length us, event | category | flops | bytes accessed | tf_op | source)
XLA Modules:
  0.0 233.4 jit_solution(12626230689533728283)
XLA Ops:
  4.8 14.0 %shard_map.246 = (bf16[512,768]{1,0:T(8,128)(2,1)}, bf16[512,384]{1,0:T(8,128)(2,1)}, bf16[512,384]{1,0:T(8,128)(2,1)}, bf16[512,384]{1,0:T(8,128)(2,1)}, bf16[6...) custom-call(bf16[512,768]{1,0:T(8,128)(2,1)} %bitcast.159, f32[1,768]{1,0:T(1,128)} %reshape.305.gain_ref, ...), custom_call_target="tpu_custom_call" | custom-call | tf_op jit(solution)/shard_map/pallas_call | solution.py:190
  20.4 3.0 %collective-permute-start = (bf16[512,768]{1,0:T(8,128)(2,1)S(1)}, bf16[512,768]{1,0:T(8,128)(2,1)S(1)}, u32[]{:S(2)}, u32[]{:S(2)}) collective-permute-start(bf16[512,768]{1,0:T(8,128)(2,1)S(1)} %convolution_convert_fusion.5), channel_id=1, source_target_pairs={{0,1},{1,0},{2,3},{3,2},{4,5},{5,4},{6,7},{7,6},{8,9},{9,8},{10,11... | collective-permute-start | bytes 2359304 | tf_op jit(solution)/shard_map/ppermute | solution.py:202
  23.4 17.5 %collective-permute-done = bf16[512,768]{1,0:T(8,128)(2,1)S(1)} collective-permute-done((bf16[512,768]{1,0:T(8,128)(2,1)S(1)}, bf16[512,768]{1,0:T(8,128)(2,1)S(1)}, u32[]{:S(2)}, u32[]{:S(2)}) %collective-permute-start) | collective-permute-done | bytes 786464 | tf_op jit(solution)/shard_map/ppermute | solution.py:202
  41.8 4.4 %multiply_convert_fusion = (bf16[512,1536]{1,0:T(8,128)(2,1)S(1)}, f32[512,1536]{1,0:T(8,128)}) fusion(bf16[512,768]{1,0:T(8,128)(2,1)S(1)} %multiply_convert_fusion.1, bf16[768,1536]{1,0:T(8,128)(2,1)S(1)} %copy-done), kind=kOutput, calls=%fused_computation.8 | convolution fusion | flops 1224474624 | bytes 7864320 | tf_op jit(solution)/shard_map/dot_general | solution.py:25
  49.6 16.8 %collective-permute-done.1 = bf16[512,768]{1,0:T(8,128)(2,1)S(1)} collective-permute-done((bf16[512,768]{1,0:T(8,128)(2,1)S(1)}, bf16[512,768]{1,0:T(8,128)(2,1)S(1)}, u32[]{:S(2)}, u32[]{:S(2)}) %collective-permute-start.1) | collective-permute-done | bytes 786464 | tf_op jit(solution)/shard_map/ppermute | solution.py:202
  70.1 2.3 collective-permute-done.2
  74.0 2.8 %collective-permute-done.3 = bf16[2,8,768]{2,1,0:T(8,128)(2,1)S(1)} collective-permute-done((bf16[2,8,768]{2,1,0:T(8,128)(2,1)S(1)}, bf16[2,8,768]{2,1,0:T(8,128)(2,1)S(1)}, u32[]{:S(2)}, u32[]{:S(2)}) %collective-permute-start.3) | collective-permute-done | bytes 24608 | tf_op jit(solution)/shard_map/ppermute | solution.py:202
  76.9 2.1 collective-permute-start.4
  78.9 3.0 %collective-permute-done.4 = bf16[4,8,768]{2,1,0:T(8,128)(2,1)S(1)} collective-permute-done((bf16[4,8,768]{2,1,0:T(8,128)(2,1)S(1)}, bf16[4,8,768]{2,1,0:T(8,128)(2,1)S(1)}, u32[]{:S(2)}, u32[]{:S(2)}) %collective-permute-start.4) | collective-permute-done | bytes 49184 | tf_op jit(solution)/shard_map/ppermute | solution.py:202
  92.6 3.6 %fusion.5 = bf16[512,1536]{1,0:T(8,128)(2,1)S(1)} fusion(f32[512,1536]{1,0:T(8,128)S(1)} %copy-done.58, bf16[512,768]{1,0:T(8,128)(2,1)S(1)} %fusion.57, bf16[1536,768]{1,0:T(8,128)(2,1)S(1)} %copy-done.52), kind=kOutput, calls=%fused_computation.14 | convolution fusion | flops 1226833920 | bytes 7864320 | tf_op jit(solution)/shard_map/dot_general | solution.py:29
  96.2 2.3 convolution_convert_fusion.3
  107.4 10.9 %collective-permute-done.6 = bf16[512,768]{1,0:T(8,128)(2,1)S(1)} collective-permute-done((bf16[512,768]{1,0:T(8,128)(2,1)}, bf16[512,768]{1,0:T(8,128)(2,1)S(1)}, u32[]{:S(2)}, u32[]{:S(2)}) %collective-permute-start.6) | collective-permute-done | bytes 786464 | tf_op jit(solution)/shard_map/ppermute | solution.py:202
  118.3 2.3 multiply_reduce_fusion.1
  120.7 3.0 %fusion.88 = (bf16[512,768]{1,0:T(8,128)(2,1)S(1)}, f32[512,768]{1,0:T(8,128)}) fusion(f32[512,768]{1,0:T(8,128)S(1)} %copy-done.3, f32[512]{0:T(512)S(1)} %fusion.83, f32[768]{0:T(1024)S(1)} %copy-done.31, bf16[512,768]{1,0:T(8,128)(2,1)S(1)} %collective-permute-done.6, bf16[512,768]{1,0:T(8,128)(2,1)} %convolution_convert_fusion.3, f32[512]{0:T(512)S(1)} %copy-done.35, ...), kind=kLoop, calls=%fused_computation.196 | loop fusion | flops 5111808 | bytes 8665088 | tf_op jit(solution)/shard_map/convert_element_type | solution.py:376
  125.1 12.3 %shard_map.247 = (bf16[512,384]{1,0:T(8,128)(2,1)}, bf16[512,384]{1,0:T(8,128)(2,1)}, bf16[512,384]{1,0:T(8,128)(2,1)}, f32[32,6]{1,0:T(8,128)}) custom-call(bf16[512,384]{1,0:T(8,128)(2,1)} %get-tuple-element.24.q_ref, bf16[512,384]{1,0:T(8,128)(2,1)} %get-tuple-element.25.k_ref, bf16[512,384]{1,0:T(8,128)(2,1)} %get-tuple-element.26.v_ref, ...), custom_call_target="tpu_custom_call" | custom-call | tf_op jit(solution)/shard_map/pallas_call | solution.py:190
  145.9 3.1 %convolution_convert_fusion.2 = bf16[384,1152]{1,0:T(8,128)(2,1)} fusion(bf16[512,1152]{1,0:T(8,128)(2,1)} %constant_dynamic-update-slice_fusion, bf16[512,768]{1,0:T(8,128)(2,1)} %get-tuple-element.32, s32[]{:T(128)S(6)} %select_n.203), kind=kOutput, calls=%fused_computation.17 | convolution fusion | flops 453427200 | bytes 2457604 | tf_op jit(solution)/shard_map/dot_general | solution.py:33
  151.7 2.1 add_convert_fusion.1
  155.8 2.1 add_convert_fusion
  162.5 2.0 fusion.12
  164.7 2.5 %collective-permute-start.19 = (bf16[48,384]{1,0:T(8,128)(2,1)S(1)}, bf16[48,384]{1,0:T(8,128)(2,1)S(1)}, u32[]{:S(2)}, u32[]{:S(2)}) collective-permute-start(bf16[48,384]{1,0:T(8,128)(2,1)S(1)} %dynamic-slice_bitcast_fusion.3), channel_id=1, source_target_pairs={{0,8},{2,10},{4,12},{6,14},{8,0},{10,2},{12,4},{14,6},{1,9},{3,11}... | collective-permute-start | bytes 110600 | tf_op jit(solution)/shard_map/ppermute | solution.py:202
  170.3 12.8 %collective-permute-done.9 = f32[4,48,7]{1,0,2:T(4,128)S(1)} collective-permute-done((f32[4,48,7]{1,0,2:T(4,128)S(1)}, f32[4,48,7]{1,0,2:T(4,128)S(1)}, u32[]{:S(2)}, u32[]{:S(2)}) %collective-permute-start.9) | collective-permute-done | bytes 5408 | tf_op jit(solution)/shard_map/ppermute | solution.py:202
  184.8 2.0 collective-permute-done.10
  186.8 2.5 %collective-permute-start.11 = (f32[1,48,7]{1,0,2:T(1,128)S(1)}, f32[1,48,7]{1,0,2:T(1,128)S(1)}, u32[]{:S(2)}, u32[]{:S(2)}) collective-permute-start(f32[1,48,7]{1,0,2:T(1,128)S(1)} %constant_dynamic-slice_fusion.17), channel_id=1, source_target_pairs={{0,8},{2,10},{4,12},{6,14},{8,0},{10,2},{12,4},{14,6},{1,9},{3,11}... | collective-permute-start | bytes 4040 | tf_op jit(solution)/shard_map/ppermute | solution.py:202
  189.3 2.8 %fusion.10 = f32[1,1,512,768]{3,2,1,0:T(8,128)} fusion(f32[512,768]{1,0:T(8,128)S(1)} %copy-done.10, bf16[512,768]{1,0:T(8,128)(2,1)} %collective-permute-done.7, bf16[512,768]{1,0:T(8,128)(2,1)S(1)} %add_convert_fusion.3, f32[512]{0:T(512)S(1)} %fusion.84, f32[768]{0:T(1024)S(1)} %copy-done.32, f32[512]{0:T(512)S(1)} %copy-done.36, ...), kind=kLoop, calls=%fused_computation.25 | loop fusion | flops 3538944 | bytes 5512192 | tf_op jit(solution)/shard_map/reshape | solution.py:405
  193.4 2.3 %add_convert_fusion.2 = bf16[384,1152]{1,0:T(8,128)(2,1)S(1)} fusion(bf16[384,1152]{1,0:T(8,128)(2,1)} %collective-permute-done.12, bf16[512,1152]{1,0:T(8,128)(2,1)} %constant_dynamic-update-slice_fusion, bf16[512,768]{1,0:T(8,128)(2,1)} %get-tuple-element.32, s32[]{:T(128)S(6)} %select_n.202), kind=kOutput, calls=%fused_computation.20 | convolution fusion | flops 454311936 | bytes 3342340 | tf_op jit(solution)/shard_map/dot_general | solution.py:33
  198.1 2.1 collective-permute-start.22
  201.6 8.1 %collective-permute-done.22 = bf16[96,1536]{1,0:T(8,128)(2,1)S(1)} collective-permute-done((bf16[96,1536]{1,0:T(8,128)(2,1)S(1)}, bf16[96,1536]{1,0:T(8,128)(2,1)S(1)}, u32[]{:S(2)}, u32[]{:S(2)}) %collective-permute-start.22) | collective-permute-done | bytes 294944 | tf_op jit(solution)/shard_map/ppermute | solution.py:202
  210.1 3.7 %collective-permute-done.26 = bf16[96,1536]{1,0:T(8,128)(2,1)S(1)} collective-permute-done((bf16[96,1536]{1,0:T(8,128)(2,1)S(1)}, bf16[96,1536]{1,0:T(8,128)(2,1)S(1)}, u32[]{:S(2)}, u32[]{:S(2)}) %collective-permute-start.26) | collective-permute-done | bytes 294944 | tf_op jit(solution)/shard_map/ppermute | solution.py:202
  214.4 2.5 %collective-permute-start.14 = (bf16[96,1152]{1,0:T(8,128)(2,1)S(1)}, bf16[96,1152]{1,0:T(8,128)(2,1)S(1)}, u32[]{:S(2)}, u32[]{:S(2)}) collective-permute-start(bf16[96,1152]{1,0:T(8,128)(2,1)S(1)} %bitcast.179), channel_id=1, source_target_pairs={{0,4},{2,6},{4,0},{6,2},{8,12},{10,14},{12,8},{14,10},{1,5},{3,7},... | collective-permute-start | bytes 663560 | tf_op jit(solution)/shard_map/ppermute | solution.py:202
  217.0 2.5 %collective-permute-done.23 = bf16[48,1536]{1,0:T(8,128)(2,1)S(1)} collective-permute-done((bf16[48,1536]{1,0:T(8,128)(2,1)S(1)}, bf16[48,1536]{1,0:T(8,128)(2,1)S(1)}, u32[]{:S(2)}, u32[]{:S(2)}) %collective-permute-start.23) | collective-permute-done | bytes 147488 | tf_op jit(solution)/shard_map/ppermute | solution.py:202
  220.3 4.3 %collective-permute-done.14 = bf16[96,1152]{1,0:T(8,128)(2,1)S(1)} collective-permute-done((bf16[96,1152]{1,0:T(8,128)(2,1)S(1)}, bf16[96,1152]{1,0:T(8,128)(2,1)S(1)}, u32[]{:S(2)}, u32[]{:S(2)}) %collective-permute-start.14) | collective-permute-done | bytes 221216 | tf_op jit(solution)/shard_map/ppermute | solution.py:202
  226.4 5.1 %collective-permute-done.15 = bf16[48,1152]{1,0:T(8,128)(2,1)S(1)} collective-permute-done((bf16[48,1152]{1,0:T(8,128)(2,1)S(1)}, bf16[48,1152]{1,0:T(8,128)(2,1)S(1)}, u32[]{:S(2)}, u32[]{:S(2)}) %collective-permute-start.15) | collective-permute-done | bytes 110624 | tf_op jit(solution)/shard_map/ppermute | solution.py:202
  (256 shorter events, 65.9 us)
Async XLA Ops:
  0.6 41.1 %copy-start = (bf16[768,1536]{1,0:T(8,128)(2,1)S(1)}, bf16[768,1536]{1,0:T(8,128)(2,1)}, u32[]{:S(2)}) copy-start(bf16[768,1536]{1,0:T(8,128)(2,1)} %param.26) | copy-start | bytes 7077892
  4.8 36.1 %copy-start.9 = (bf16[1,1,512,768]{3,2,1,0:T(8,128)(2,1)S(1)}, bf16[1,1,512,768]{3,2,1,0:T(8,128)(2,1)}, u32[]{:S(2)}) copy-start(bf16[1,1,512,768]{3,2,1,0:T(8,128)(2,1)} %param.15) | copy-start | bytes 2359300
  20.4 20.6 %collective-permute-start = (bf16[512,768]{1,0:T(8,128)(2,1)S(1)}, bf16[512,768]{1,0:T(8,128)(2,1)S(1)}, u32[]{:S(2)}, u32[]{:S(2)}) collective-permute-start(bf16[512,768]{1,0:T(8,128)(2,1)S(1)} %convolution_convert_fusion.5), channel_id=1, source_target_pairs={{0,1},{1,0},{2,3},{3,2},{4,5},{5,4},{6,7},{7,6},{8,9},{9,8},{10,11... | collective-permute-start | bytes 2359304 | tf_op jit(solution)/shard_map/ppermute | solution.py:202
  41.5 40.6 %copy-start.37 = (f32[512]{0:T(512)}, f32[512]{0:T(512)S(1)}, u32[]{:S(2)}) copy-start(f32[512]{0:T(512)S(1)} %get-tuple-element.112) | copy-start | bytes 6148
  47.6 18.8 %collective-permute-start.1 = (bf16[512,768]{1,0:T(8,128)(2,1)S(1)}, bf16[512,768]{1,0:T(8,128)(2,1)S(1)}, u32[]{:S(2)}, u32[]{:S(2)}) collective-permute-start(bf16[512,768]{1,0:T(8,128)(2,1)S(1)} %convolution_convert_fusion.4), channel_id=1, source_target_pairs={{0,1},{1,0},{2,3},{3,2},{4,5},{5,4},{6,7},{7,6},{8,9},{9,8},{10,11... | collective-permute-start | bytes 2359304 | tf_op jit(solution)/shard_map/ppermute | solution.py:202
  68.7 3.7 %collective-permute-start.2 = (bf16[1,8,768]{2,1,0:T(8,128)(2,1)S(1)}, bf16[1,8,768]{2,1,0:T(8,128)(2,1)S(1)}, u32[]{:S(2)}, u32[]{:S(2)}) collective-permute-start(bf16[1,8,768]{2,1,0:T(8,128)(2,1)S(1)} %fusion.26), channel_id=1, source_target_pairs={{0,2},{2,0},{4,6},{6,4},{8,10},{10,8},{12,14},{14,12},{1,3},{3,1},... | collective-permute-start | bytes 36872 | tf_op jit(solution)/shard_map/ppermute | solution.py:202
  72.4 4.4 %collective-permute-start.3 = (bf16[2,8,768]{2,1,0:T(8,128)(2,1)S(1)}, bf16[2,8,768]{2,1,0:T(8,128)(2,1)S(1)}, u32[]{:S(2)}, u32[]{:S(2)}) collective-permute-start(bf16[2,8,768]{2,1,0:T(8,128)(2,1)S(1)} %pad_maximum_fusion.2), channel_id=1, source_target_pairs={{0,4},{2,6},{4,0},{6,2},{8,12},{10,14},{12,8},{14,10},{1,5},{3,7},... | collective-permute-start | bytes 73736 | tf_op jit(solution)/shard_map/ppermute | solution.py:202
  76.9 5.1 %collective-permute-start.4 = (bf16[4,8,768]{2,1,0:T(8,128)(2,1)S(1)}, bf16[4,8,768]{2,1,0:T(8,128)(2,1)S(1)}, u32[]{:S(2)}, u32[]{:S(2)}) collective-permute-start(bf16[4,8,768]{2,1,0:T(8,128)(2,1)S(1)} %pad_maximum_fusion.1), channel_id=1, source_target_pairs={{0,8},{2,10},{4,12},{6,14},{8,0},{10,2},{12,4},{14,6},{1,9},{3,11}... | collective-permute-start | bytes 147464 | tf_op jit(solution)/shard_map/ppermute | solution.py:202
  82.0 1.4 collective-permute-start.5
  98.5 19.8 %collective-permute-start.6 = (bf16[512,768]{1,0:T(8,128)(2,1)}, bf16[512,768]{1,0:T(8,128)(2,1)S(1)}, u32[]{:S(2)}, u32[]{:S(2)}) collective-permute-start(bf16[512,768]{1,0:T(8,128)(2,1)} %convolution_convert_fusion.3), channel_id=1, source_target_pairs={{0,1},{1,0},{2,3},{3,2},{4,5},{5,4},{6,7},{7,6},{8,9},{9,8},{10,11... | collective-permute-start | bytes 2359304 | tf_op jit(solution)/shard_map/ppermute | solution.py:202
  101.9 49.7 %collective-permute-start.20 = (bf16[384,1536]{1,0:T(8,128)(2,1)}, bf16[384,1536]{1,0:T(8,128)(2,1)}, u32[]{:S(2)}, u32[]{:S(2)}) collective-permute-start(bf16[384,1536]{1,0:T(8,128)(2,1)} %convolution_convert_fusion.1), channel_id=1, source_target_pairs={{0,16},{16,0},{1,17},{17,1},{2,18},{18,2},{3,19},{19,3},{4,20},{20... | collective-permute-start | bytes 3538952 | tf_op jit(solution)/shard_map/ppermute | solution.py:202
  103.8 51.6 %collective-permute-start.24 = (bf16[384,1536]{1,0:T(8,128)(2,1)}, bf16[384,1536]{1,0:T(8,128)(2,1)}, u32[]{:S(2)}, u32[]{:S(2)}) collective-permute-start(bf16[384,1536]{1,0:T(8,128)(2,1)} %convolution_convert_fusion), channel_id=1, source_target_pairs={{0,16},{16,0},{1,17},{17,1},{2,18},{18,2},{3,19},{19,3},{4,20},{20... | collective-permute-start | bytes 3538952 | tf_op jit(solution)/shard_map/ppermute | solution.py:202
  140.9 21.6 %collective-permute-start.7 = (bf16[512,768]{1,0:T(8,128)(2,1)S(1)}, bf16[512,768]{1,0:T(8,128)(2,1)}, u32[]{:S(2)}, u32[]{:S(2)}) collective-permute-start(bf16[512,768]{1,0:T(8,128)(2,1)S(1)} %add_convert_fusion.3), channel_id=1, source_target_pairs={{0,1},{1,0},{2,3},{3,2},{4,5},{5,4},{6,7},{7,6},{8,9},{9,8},{10,11... | collective-permute-start | bytes 2359304 | tf_op jit(solution)/shard_map/ppermute | solution.py:202
  143.1 6.5 %collective-permute-start.16 = (bf16[384,384]{1,0:T(8,128)(2,1)}, bf16[384,384]{1,0:T(8,128)(2,1)S(1)}, u32[]{:S(2)}, u32[]{:S(2)}) collective-permute-start(bf16[384,384]{1,0:T(8,128)(2,1)} %convolution_convert_fusion.7), channel_id=1, source_target_pairs={{0,16},{16,0},{1,17},{17,1},{2,18},{18,2},{3,19},{19,3},{4,20},{20... | collective-permute-start | bytes 884744 | tf_op jit(solution)/shard_map/ppermute | solution.py:202
  149.1 44.4 %collective-permute-start.12 = (bf16[384,1152]{1,0:T(8,128)(2,1)}, bf16[384,1152]{1,0:T(8,128)(2,1)}, u32[]{:S(2)}, u32[]{:S(2)}) collective-permute-start(bf16[384,1152]{1,0:T(8,128)(2,1)} %convolution_convert_fusion.2), channel_id=1, source_target_pairs={{0,16},{16,0},{1,17},{17,1},{2,18},{18,2},{3,19},{19,3},{4,20},{20... | collective-permute-start | bytes 2654216 | tf_op jit(solution)/shard_map/ppermute | solution.py:202
  150.0 7.9 %collective-permute-start.17 = (bf16[192,384]{1,0:T(8,128)(2,1)S(1)}, bf16[192,384]{1,0:T(8,128)(2,1)S(1)}, u32[]{:S(2)}, u32[]{:S(2)}) collective-permute-start(bf16[192,384]{1,0:T(8,128)(2,1)S(1)} %bitcast.180), channel_id=1, source_target_pairs={{0,2},{2,0},{4,6},{6,4},{8,10},{10,8},{12,14},{14,12},{1,3},{3,1},... | collective-permute-start | bytes 442376 | tf_op jit(solution)/shard_map/ppermute | solution.py:202
  154.9 41.9 %collective-permute-start.21 = (bf16[192,1536]{1,0:T(8,128)(2,1)}, bf16[192,1536]{1,0:T(8,128)(2,1)}, u32[]{:S(2)}, u32[]{:S(2)}) collective-permute-start(bf16[192,1536]{1,0:T(8,128)(2,1)} %bitcast.35), channel_id=1, source_target_pairs={{0,2},{2,0},{4,6},{6,4},{8,10},{10,8},{12,14},{14,12},{1,3},{3,1},... | collective-permute-start | bytes 1769480 | tf_op jit(solution)/shard_map/ppermute | solution.py:202
  158.0 4.4 %collective-permute-start.18 = (bf16[96,384]{1,0:T(8,128)(2,1)S(1)}, bf16[96,384]{1,0:T(8,128)(2,1)S(1)}, u32[]{:S(2)}, u32[]{:S(2)}) collective-permute-start(bf16[96,384]{1,0:T(8,128)(2,1)S(1)} %bitcast.181), channel_id=1, source_target_pairs={{0,4},{2,6},{4,0},{6,2},{8,12},{10,14},{12,8},{14,10},{1,5},{3,7},... | collective-permute-start | bytes 221192 | tf_op jit(solution)/shard_map/ppermute | solution.py:202
  160.8 39.4 %collective-permute-start.25 = (bf16[192,1536]{1,0:T(8,128)(2,1)}, bf16[192,1536]{1,0:T(8,128)(2,1)}, u32[]{:S(2)}, u32[]{:S(2)}) collective-permute-start(bf16[192,1536]{1,0:T(8,128)(2,1)} %bitcast.44), channel_id=1, source_target_pairs={{0,2},{2,0},{4,6},{6,4},{8,10},{10,8},{12,14},{14,12},{1,3},{3,1},... | collective-permute-start | bytes 1769480 | tf_op jit(solution)/shard_map/ppermute | solution.py:202
  162.4 26.8 %copy-start.10 = (f32[512,768]{1,0:T(8,128)S(1)}, f32[512,768]{1,0:T(8,128)}, u32[]{:S(2)}) copy-start(f32[512,768]{1,0:T(8,128)} %get-tuple-element.97) | copy-start | bytes 4718596
  164.6 2.6 %collective-permute-start.8 = (f32[384,7]{0,1:T(8,128)S(1)}, f32[384,7]{0,1:T(8,128)S(1)}, u32[]{:S(2)}, u32[]{:S(2)}) collective-permute-start(f32[384,7]{0,1:T(8,128)S(1)} %bitcast.194), channel_id=1, source_target_pairs={{0,16},{16,0},{1,17},{17,1},{2,18},{18,2},{3,19},{19,3},{4,20},{20... | collective-permute-start | bytes 32264 | tf_op jit(solution)/shard_map/ppermute | solution.py:202
  164.7 4.9 %collective-permute-start.19 = (bf16[48,384]{1,0:T(8,128)(2,1)S(1)}, bf16[48,384]{1,0:T(8,128)(2,1)S(1)}, u32[]{:S(2)}, u32[]{:S(2)}) collective-permute-start(bf16[48,384]{1,0:T(8,128)(2,1)S(1)} %dynamic-slice_bitcast_fusion.3), channel_id=1, source_target_pairs={{0,8},{2,10},{4,12},{6,14},{8,0},{10,2},{12,4},{14,6},{1,9},{3,11}... | collective-permute-start | bytes 110600 | tf_op jit(solution)/shard_map/ppermute | solution.py:202
  167.4 15.7 %collective-permute-start.9 = (f32[4,48,7]{1,0,2:T(4,128)S(1)}, f32[4,48,7]{1,0,2:T(4,128)S(1)}, u32[]{:S(2)}, u32[]{:S(2)}) collective-permute-start(f32[4,48,7]{1,0,2:T(4,128)S(1)} %bitcast.193), channel_id=1, source_target_pairs={{0,2},{2,0},{4,6},{6,4},{8,10},{10,8},{12,14},{14,12},{1,3},{3,1},... | collective-permute-start | bytes 16136 | tf_op jit(solution)/shard_map/ppermute | solution.py:202
  183.1 3.7 %collective-permute-start.10 = (f32[2,48,7]{1,0,2:T(2,128)S(1)}, f32[2,48,7]{1,0,2:T(2,128)S(1)}, u32[]{:S(2)}, u32[]{:S(2)}) collective-permute-start(f32[2,48,7]{1,0,2:T(2,128)S(1)} %bitcast.195), channel_id=1, source_target_pairs={{0,4},{2,6},{4,0},{6,2},{8,12},{10,14},{12,8},{14,10},{1,5},{3,7},... | collective-permute-start | bytes 8072 | tf_op jit(solution)/shard_map/ppermute | solution.py:202
  186.8 5.2 %collective-permute-start.11 = (f32[1,48,7]{1,0,2:T(1,128)S(1)}, f32[1,48,7]{1,0,2:T(1,128)S(1)}, u32[]{:S(2)}, u32[]{:S(2)}) collective-permute-start(f32[1,48,7]{1,0,2:T(1,128)S(1)} %constant_dynamic-slice_fusion.17), channel_id=1, source_target_pairs={{0,8},{2,10},{4,12},{6,14},{8,0},{10,2},{12,4},{14,6},{1,9},{3,11}... | collective-permute-start | bytes 4040 | tf_op jit(solution)/shard_map/ppermute | solution.py:202
  195.9 18.3 %collective-permute-start.13 = (bf16[192,1152]{1,0:T(8,128)(2,1)S(1)}, bf16[192,1152]{1,0:T(8,128)(2,1)S(1)}, u32[]{:S(2)}, u32[]{:S(2)}) collective-permute-start(bf16[192,1152]{1,0:T(8,128)(2,1)S(1)} %bitcast.173), channel_id=1, source_target_pairs={{0,2},{2,0},{4,6},{6,4},{8,10},{10,8},{12,14},{14,12},{1,3},{3,1},... | collective-permute-start | bytes 1327112 | tf_op jit(solution)/shard_map/ppermute | solution.py:202
  198.1 11.5 %collective-permute-start.22 = (bf16[96,1536]{1,0:T(8,128)(2,1)S(1)}, bf16[96,1536]{1,0:T(8,128)(2,1)S(1)}, u32[]{:S(2)}, u32[]{:S(2)}) collective-permute-start(bf16[96,1536]{1,0:T(8,128)(2,1)S(1)} %bitcast.177), channel_id=1, source_target_pairs={{0,4},{2,6},{4,0},{6,2},{8,12},{10,14},{12,8},{14,10},{1,5},{3,7},... | collective-permute-start | bytes 884744 | tf_op jit(solution)/shard_map/ppermute | solution.py:202
  201.5 12.3 %collective-permute-start.26 = (bf16[96,1536]{1,0:T(8,128)(2,1)S(1)}, bf16[96,1536]{1,0:T(8,128)(2,1)S(1)}, u32[]{:S(2)}, u32[]{:S(2)}) collective-permute-start(bf16[96,1536]{1,0:T(8,128)(2,1)S(1)} %bitcast.178), channel_id=1, source_target_pairs={{0,4},{2,6},{4,0},{6,2},{8,12},{10,14},{12,8},{14,10},{1,5},{3,7},... | collective-permute-start | bytes 884744 | tf_op jit(solution)/shard_map/ppermute | solution.py:202
  209.8 9.7 %collective-permute-start.23 = (bf16[48,1536]{1,0:T(8,128)(2,1)S(1)}, bf16[48,1536]{1,0:T(8,128)(2,1)S(1)}, u32[]{:S(2)}, u32[]{:S(2)}) collective-permute-start(bf16[48,1536]{1,0:T(8,128)(2,1)S(1)} %dynamic-slice_bitcast_fusion.1), channel_id=1, source_target_pairs={{0,8},{2,10},{4,12},{6,14},{8,0},{10,2},{12,4},{14,6},{1,9},{3,11}... | collective-permute-start | bytes 442376 | tf_op jit(solution)/shard_map/ppermute | solution.py:202
  213.9 11.8 %collective-permute-start.27 = (bf16[48,1536]{1,0:T(8,128)(2,1)S(1)}, bf16[48,1536]{1,0:T(8,128)(2,1)S(1)}, u32[]{:S(2)}, u32[]{:S(2)}) collective-permute-start(bf16[48,1536]{1,0:T(8,128)(2,1)S(1)} %dynamic-slice_bitcast_fusion), channel_id=1, source_target_pairs={{0,8},{2,10},{4,12},{6,14},{8,0},{10,2},{12,4},{14,6},{1,9},{3,11}... | collective-permute-start | bytes 442376 | tf_op jit(solution)/shard_map/ppermute | solution.py:202
  214.4 10.1 %collective-permute-start.14 = (bf16[96,1152]{1,0:T(8,128)(2,1)S(1)}, bf16[96,1152]{1,0:T(8,128)(2,1)S(1)}, u32[]{:S(2)}, u32[]{:S(2)}) collective-permute-start(bf16[96,1152]{1,0:T(8,128)(2,1)S(1)} %bitcast.179), channel_id=1, source_target_pairs={{0,4},{2,6},{4,0},{6,2},{8,12},{10,14},{12,8},{14,10},{1,5},{3,7},... | collective-permute-start | bytes 663560 | tf_op jit(solution)/shard_map/ppermute | solution.py:202
  224.7 6.9 %collective-permute-start.15 = (bf16[48,1152]{1,0:T(8,128)(2,1)S(1)}, bf16[48,1152]{1,0:T(8,128)(2,1)S(1)}, u32[]{:S(2)}, u32[]{:S(2)}) collective-permute-start(bf16[48,1152]{1,0:T(8,128)(2,1)S(1)} %dynamic-slice_bitcast_fusion.2), channel_id=1, source_target_pairs={{0,8},{2,10},{4,12},{6,14},{8,0},{10,2},{12,4},{14,6},{1,9},{3,11}... | collective-permute-start | bytes 331784 | tf_op jit(solution)/shard_map/ppermute | solution.py:202
  (55 other events, 387.4 us)
where the time goes:
time: 234 us; the launch traced here: 233 us
  waiting for transfers between devices  94.2 us (40%)
  matrix products  37.7 us (16%)
  starting transfers between devices  33.1 us (14%)
  Pallas kernels  26.3 us (11%)
  other arithmetic  19.2 us (8%)
  local copies, waits for them, and re-layouts  18.3 us (8%)
  between operations  4.62 us (2%)
    ppermute x28, waiting for transfers between devices, swap(): return lax.ppermute(values, axis, [(i, i ^ bit) for i in range(count)])  94.2 us
    ppermute x28, starting transfers between devices, swap(): return lax.ppermute(values, axis, [(i, i ^ bit) for i in range(count)])  33.1 us
    pallas_call x2, Pallas kernels, whole(): pl.pallas_call(kernel, out_shape=out_shapes, in_specs=[pl.BlockSpec(memor...  26.3 us
    dot_general x10, matrix products, dot_tn(): lax.dot_general(a, b, (((0,), (0,)), ((), ())), preferred_element_type=f32)  15.6 us
    dot_general x8, matrix products, dot_nt(): lax.dot_general(a, b, (((1,), (1,)), ((), ())), preferred_element_type=f32)  10.8 us
    dot_general x5, matrix products, dot_nn(): lax.dot_general(a, b, (((1,), (0,)), ((), ())), preferred_element_type=f32)  9.27 us
    unnamed x124, local copies, waits for them, and re-layouts  8.99 us
  transfers between devices with their start and end apart: 28, of which 16 were waited for; matrix products, arithmetic and copies ran while one was open for 19% of the time, Pallas kernels for 5%

commit v1 on v0

v1 whole, which is shorter than its diff:
```python
import functools

import jax
import jax.numpy as jnp
from jax import lax
from jax.experimental import pallas as pl
from jax.experimental.pallas import tpu as pltpu
from jax.sharding import PartitionSpec as P

SEGS_ROW = 8
BLOCK = 128
STRIP = 32
PIECE = 384
LANES = 128
CHUNKS = 2

eps = 1e-06
logit_scale = 50.0
highest = lax.Precision.HIGHEST
f32 = jnp.float32
bf16 = jnp.bfloat16


def inv_rms(values):
    return lax.rsqrt(jnp.mean(values * values, -1, keepdims=True) + eps)


def dot_nn(a, b):
    return lax.dot_general(a, b, (((1,), (0,)), ((), ())), preferred_element_type=f32)


def dot_nt(a, b):
    return lax.dot_general(a, b, (((1,), (1,)), ((), ())), preferred_element_type=f32)


def dot_tn(a, b):
    return lax.dot_general(a, b, (((0,), (0,)), ((), ())), preferred_element_type=f32)


def gelu_parts(values):
    size = jnp.abs(values)
    bell = jnp.exp(-0.5 * values * values)
    t = 1.0 / (1.0 + (0.3275911 * 0.7071067811865476) * size)
    poly = t * (
        0.127414796
        + t * (-0.142248368 + t * (0.7107068705 + t * (-0.7265760135 + t * 0.5307027145)))
    )
    tail = poly * bell
    return bell, jnp.where(values >= 0, 1.0 - tail, tail)


def key_range(block, blocks):
    return max(0, block - 2), min(blocks, block + 3)


def split_low(values, parts):
    out = []
    for _ in range(parts):
        out.append(values.astype(bf16))
        values = values - out[-1].astype(f32)
    return out


def norm_back(values, inv, gain, grad):
    scaled = grad * gain
    inner_mean = jnp.mean(values * scaled, -1, keepdims=True)
    return inv * scaled - values * (inv * inv * inv * inner_mean)


def row_gain(gain_ref):
    return gain_ref[...].reshape(1, gain_ref.shape[0])


def attend_kernel(
    tok_hbm, wq_hbm, wk_hbm, wv_hbm, gain_hbm, table_hbm, ids_hbm, seg_hbm,
    n1_hbm, q_hbm, k_hbm, v_hbm, probs_hbm, mix_hbm, tok_ref, *rest,
):
    mix_refs = rest[:CHUNKS]
    (
        w_ref, gain_ref, table_ref, ids_ref, seg_ref, n1_ref, q_ref, k_ref, v_ref, probs_ref, mix_ref,
        rel_ref, mask_ref, skew_ref, score_ref, sems, out_sems,
    ) = rest[CHUNKS:]
    length, inner = q_ref.shape
    blocks = length // BLOCK
    heads, buckets = table_ref.shape
    pairs = inner // BLOCK
    span = rel_ref.shape[1]
    copies = start_copies(
        sems,
        (tok_hbm, tok_ref),
        (wq_hbm, w_ref.at[0]),
        (wk_hbm, w_ref.at[1]),
        (wv_hbm, w_ref.at[2]),
        (gain_hbm, gain_ref),
        (table_hbm, table_ref),
        (ids_hbm, ids_ref),
        (seg_hbm, seg_ref),
    )
    for copy in copies[4:]:
        copy.wait()
    hot = (
        lax.broadcasted_iota(jnp.int32, (buckets, span - 1), 0)
        == ids_ref[...].reshape(1, span - 1)
    ).astype(f32)
    rel_ref[...] = jnp.zeros_like(rel_ref)
    rel_ref[0:heads, 0 : span - 1] = lax.dot_general(
        table_ref[...], hot, (((1,), (0,)), ((), ())), precision=highest, preferred_element_type=f32
    )
    seg_row = seg_ref[...].astype(f32)
    for b in range(blocks):
        own = jnp.broadcast_to(seg_row[:, b * BLOCK : (b + 1) * BLOCK], (BLOCK, BLOCK)).T
        for c in range(blocks):
            other = jnp.broadcast_to(seg_row[:, c * BLOCK : (c + 1) * BLOCK], (BLOCK, BLOCK))
            mask_ref[b * BLOCK : (b + 1) * BLOCK, c * BLOCK : (c + 1) * BLOCK] = jnp.where(
                own == other, 0.0, -1e30
            )
    copies[0].wait()
    gain = row_gain(gain_ref)
    for at in range(0, length, STRIP):
        x = tok_ref[at : at + STRIP, :].astype(f32)
        n1_ref[at : at + STRIP, :] = (x * inv_rms(x) * gain).astype(bf16)
    n1 = n1_ref[...]
    for i, out_ref in enumerate((q_ref, k_ref, v_ref)):
        copies[1 + i].wait()
        out_ref[...] = dot_nn(n1, w_ref[i]).astype(bf16)
    outs = start_copies(out_sems, (n1_ref, n1_hbm), (q_ref, q_hbm), (k_ref, k_hbm), (v_ref, v_hbm))

    def probs_copy(pair):
        heads_of = pl.ds(2 * pair, 2)
        return pltpu.make_async_copy(probs_ref.at[heads_of], probs_hbm.at[heads_of], out_sems.at[4 + pair])

    low_lanes = lax.broadcasted_iota(jnp.int32, (BLOCK, BLOCK), 1) < BLOCK // 2
    zero = jnp.zeros((BLOCK, BLOCK), bf16)

    @pl.loop(0, pairs)
    def _(pair):
        lanes = pl.ds(pl.multiple_of(pair * BLOCK, BLOCK), BLOCK)
        for h in range(2):
            row = jnp.broadcast_to(rel_ref[pl.ds(pair * 2 + h, 1), :], (BLOCK, span))
            skew_ref[h] = pltpu.roll(row, span - (BLOCK - 1), 1, stride=1, stride_axis=0)
        for b in range(blocks):
            first, last = key_range(b, blocks)
            rows = slice(b * BLOCK, (b + 1) * BLOCK)
            keys = slice(first * BLOCK, last * BLOCK)
            shift = length - BLOCK - b * BLOCK
            q_pair = q_ref[rows, lanes]
            k_pair = k_ref[keys, lanes]
            v_pair = v_ref[keys, lanes]
            width = (last - first) * BLOCK
            for h in range(2):
                q_one = jnp.where(low_lanes if h == 0 else ~low_lanes, q_pair, zero)
                score_ref[h, :, :width] = dot_nt(q_one, k_pair)
            for at in range(0, BLOCK, STRIP):
                part = slice(b * BLOCK + at, b * BLOCK + at + STRIP)
                for h in range(2):
                    head = pair * 2 + h
                    scores = (
                        score_ref[h, at : at + STRIP, :width]
                        + skew_ref[h, at : at + STRIP, shift + first * BLOCK : shift + last * BLOCK]
                        + mask_ref[part, keys]
                    )
                    raised = jnp.exp(scores - jnp.max(scores, -1, keepdims=True))
                    scale = 1.0 / jnp.sum(raised, -1, keepdims=True)
                    probs_ref[head, part, keys] = (raised * scale).astype(bf16)
                    if first > 0:
                        probs_ref[head, part, 0 : first * BLOCK] = jnp.zeros((STRIP, first * BLOCK), bf16)
                    if last < blocks:
                        probs_ref[head, part, last * BLOCK :] = jnp.zeros(
                            (STRIP, length - last * BLOCK), bf16
                        )
            mix_ref[rows, lanes] = jnp.where(
                low_lanes,
                dot_nn(probs_ref[pair * 2, rows, keys], v_pair),
                dot_nn(probs_ref[pair * 2 + 1, rows, keys], v_pair),
            ).astype(bf16)
        probs_copy(pair).start()

    outs += start_copies(out_sems.at[4 + pairs :], (mix_ref, mix_hbm))
    for i, part in enumerate(mix_refs):
        part[...] = mix_ref[i * part.shape[0] : (i + 1) * part.shape[0], :]
    for copy in outs:
        copy.wait()
    for pair in range(pairs):
        probs_copy(pair).wait()


def load_kernel(
    wo_hbm, up_hbm, down_hbm, proj_hbm, fetched_hbm, fetched_too_hbm, wo_ref, up_ref, down_ref, proj_ref, sems
):
    me, tower_index = lax.axis_index("mp"), lax.axis_index("tower")
    inner = wo_hbm.shape[0]
    piece = inner // 2
    own_at = pl.multiple_of(me * inner, inner)
    other_at = (1 - me) * inner
    copies = start_copies(
        sems,
        (wo_hbm, wo_ref.at[pl.ds(own_at, inner), :]),
        (fetched_hbm, wo_ref.at[pl.ds(pl.multiple_of(other_at + tower_index * piece, piece), piece), :]),
        (fetched_too_hbm, wo_ref.at[pl.ds(pl.multiple_of(other_at + (1 - tower_index) * piece, piece), piece), :]),
        (up_hbm, up_ref),
        (down_hbm, down_ref),
        (proj_hbm, proj_ref),
    )
    for copy in copies:
        copy.wait()


def ff_kernel(
    chunk, tok_ref, wo_ref, up_ref, down_ref, mix_own, mix_other, gain_ref,
    h1_ref, n2_ref, a_ref, slope_ref, part_ref,
    mix_ref,
):
    size, width = h1_ref.shape
    inner = mix_own.shape[1]
    hidden = up_ref.shape[1]
    step = 256
    me = lax.axis_index("mp")
    mix_ref[:, pl.ds(pl.multiple_of(me * inner, inner), inner)] = mix_own[...]
    mix_ref[:, pl.ds(pl.multiple_of((1 - me) * inner, inner), inner)] = mix_other[...]
    h1_ref[...] = dot_nn(mix_ref[...], wo_ref[...])
    gain = row_gain(gain_ref)
    for at in range(0, size, STRIP):
        rows = slice(at, at + STRIP)
        h1 = tok_ref[chunk * size + at : chunk * size + at + STRIP, :].astype(f32) + h1_ref[rows, :]
        h1_ref[rows, :] = h1
        n2_ref[rows, :] = (h1 * inv_rms(h1) * gain).astype(bf16)
    n2 = n2_ref[...]
    for at in range(0, hidden, step):
        cols = slice(at, at + step)
        slope_ref[:, cols] = dot_nn(n2, up_ref[:, cols])
        for r in range(0, size, STRIP):
            rows = slice(r, r + STRIP)
            u = slope_ref[rows, cols]
            bell, below = gelu_parts(u)
            a_ref[rows, cols] = (u * below).astype(bf16)
            slope_ref[rows, cols] = below + u * bell * 0.3989422804014327
    part_ref[...] = dot_nn(a_ref[...], down_ref[...]).astype(bf16)


def pool_kernel(chunk, h1_ref, own_ref, rec_ref, gain_ref, seg_ref, *rest):
    total_ref = rest[0] if chunk > 0 else None
    h2_ref, out_ref = rest[-2:]
    size, width = h1_ref.shape
    gain = row_gain(gain_ref)
    number = lax.broadcasted_iota(jnp.int32, (SEGS_ROW, 1), 0)
    total = jnp.zeros((SEGS_ROW, width), f32)
    step = 128
    for at in range(0, size, step):
        rows = slice(at, at + step)
        h2 = h1_ref[rows, :] + (own_ref[rows, :].astype(f32) + rec_ref[rows, :].astype(f32))
        h2_ref[rows, :] = h2
        member = (seg_ref[:, chunk * size + at : chunk * size + at + step] == number).astype(f32).astype(bf16)
        for piece in split_low(h2 * inv_rms(h2) * gain, 2):
            total += dot_nn(member, piece)
    if chunk > 0:
        total += total_ref[...]
    if chunk == CHUNKS - 1:
        counts = jnp.sum((seg_ref[...] == number).astype(f32), -1, keepdims=True)
        total = total / counts
    out_ref[...] = total.astype(out_ref.dtype)


def contrast_kernel(
    total_segs, proj_ref, gathered_ref, pair_ref, loss_ref, dproj_ref, own_ref
):
    me = lax.axis_index("tower") * lax.axis_size("rows") + lax.axis_index("rows")
    count = gathered_ref.shape[0]
    row = lax.broadcasted_iota(jnp.int32, (count, count), 0)
    col = lax.broadcasted_iota(jnp.int32, (count, count), 1)
    order = (col == (row ^ (me * SEGS_ROW))).astype(f32).astype(bf16)
    pooled = dot_nn(order, gathered_ref[...]).astype(bf16)
    e = dot_nn(pooled, proj_ref[...])
    inv = lax.rsqrt(jnp.sum(e * e, -1, keepdims=True) + eps)
    unit = e * inv
    unit_low = unit.astype(bf16)
    zq, zd = unit_low[:total_segs], unit_low[total_segs:]
    logits = logit_scale * dot_nt(zd, zq)
    positive = (
        lax.broadcasted_iota(jnp.int32, (total_segs, total_segs), 0)
        == pair_ref[...].reshape(1, total_segs)
    ).astype(f32)
    norms, shares = [], []
    for axis in (0, 1):
        most = jnp.max(logits, axis, keepdims=True)
        raised = jnp.exp(logits - most)
        total = jnp.sum(raised, axis, keepdims=True)
        norms.append(jnp.log(total) + most)
        shares.append(raised / total)
    half_share = 0.5 / total_segs
    ends = jnp.sum(norms[0], 1, keepdims=True) + jnp.sum(norms[1], 0, keepdims=True)
    hits = jnp.sum(jnp.sum(logits * positive, 1, keepdims=True), 0, keepdims=True)
    loss_ref[...] = half_share * (ends - 2.0 * hits)
    grad = (half_share * (shares[0] + shares[1] - 2.0 * positive)).astype(bf16)
    dz = logit_scale * jnp.concatenate([dot_tn(grad, zd), dot_nn(grad, zq)], 0)
    de = ((dz - unit * jnp.sum(unit * dz, -1, keepdims=True)) * inv).astype(bf16)
    width, shard = proj_ref.shape[0], dproj_ref.shape[0]
    row = lax.broadcasted_iota(jnp.int32, (width, shard), 0)
    col = lax.broadcasted_iota(jnp.int32, (width, shard), 1)
    columns = (row == col + me * shard).astype(f32).astype(bf16)
    dproj_ref[...] = dot_tn(dot_nn(pooled, columns).astype(bf16), de)
    row = lax.broadcasted_iota(jnp.int32, (SEGS_ROW, count), 0)
    col = lax.broadcasted_iota(jnp.int32, (SEGS_ROW, count), 1)
    mine = (col == row + me * SEGS_ROW).astype(f32).astype(bf16)
    own_ref[...] = dot_nt(dot_nn(mine, de).astype(bf16), proj_ref[...])


def ff_back_kernel(
    chunk, down_ref, up_ref, h2_ref, slope_ref, *rest
):
    last = chunk == CHUNKS - 1
    count = 3 + (2 * CHUNKS - 1 if last else 0)
    given, outs = rest[:count], rest[count:]
    dpool_ref, seg_ref, gain_ref = given[-3:]
    part_ref, part_hbm, dh2_hbm, dgain_ref, du_ref = outs[:5]
    dh2_ref, sems = outs[-2:]
    df_ref = outs[-3] if last else outs[5]
    size, width = h2_ref.shape
    hidden = down_ref.shape[0]
    step = 256
    gain = row_gain(gain_ref)
    number = lax.broadcasted_iota(jnp.int32, (SEGS_ROW, 1), 0)
    counts = jnp.sum((seg_ref[...] == number).astype(f32), -1, keepdims=True)
    pieces = jnp.concatenate([p.astype(f32) for p in split_low(dpool_ref[...] / counts, 4)], 0).astype(bf16)
    member = (seg_ref[:, chunk * size : (chunk + 1) * size] == number).astype(f32)
    member = jnp.concatenate([member] * 4, 0).astype(bf16)
    dh2_ref[...] = dot_tn(member, pieces)
    dgain = jnp.zeros((1, width), f32)
    for at in range(0, size, STRIP):
        rows = slice(at, at + STRIP)
        h2 = h2_ref[rows, :]
        grad = dh2_ref[rows, :]
        inv = inv_rms(h2)
        dh2 = norm_back(h2, inv, gain, grad)
        dgain += jnp.sum(h2 * inv * grad, 0, keepdims=True)
        dh2_ref[rows, :] = dh2
        df_ref[rows, :] = dh2.astype(bf16)
    dgain_ref[...] = dgain
    df = df_ref[...]
    for at in range(0, hidden, step):
        cols = slice(at, at + step)
        du_ref[:, cols] = (dot_nt(df, down_ref[cols, :]) * slope_ref[:, cols]).astype(bf16)
    part_ref[...] = dot_nt(du_ref[...], up_ref[...]).astype(bf16)
    copies = start_copies(sems, (dh2_ref, dh2_hbm), (part_ref, part_hbm))
    if last:
        weight_products([*given[CHUNKS:-3], df_ref], given[:CHUNKS], outs[5:-4], outs[-4])
    for copy in copies:
        copy.wait()


def middle_back_kernel(chunk, *refs):
    first, last = chunk == 0, chunk == CHUNKS - 1
    refs = list(refs)

    def take(count):
        taken = refs[:count]
        del refs[:count]
        return taken

    own_hbm, dh2_hbm = take(2)
    ahead = take(4) if last else []
    wo_ref, h1_ref = take(2)
    lefts, rights = (take(CHUNKS), take(CHUNKS)) if first else ([], [])
    rec_ref, gain_ref = take(2)
    dh1_hbm, da_hbm, dmix_ref, dgain_ref = take(4)
    held = take(4) if last else []
    halves = take(len(refs) - 6) if first else []
    own_ref, dh2_ref, dh1_ref, da_ref, sems, out_sems = refs
    copies = start_copies(sems, (own_hbm, own_ref), (dh2_hbm, dh2_ref), *zip(ahead, held))
    if first:
        weight_products(lefts, rights, halves[:-1], halves[-1])
    for copy in copies[:2]:
        copy.wait()
    size, width = h1_ref.shape
    gain = row_gain(gain_ref)
    dgain = jnp.zeros((1, width), f32)
    for at in range(0, size, STRIP):
        rows = slice(at, at + STRIP)
        h1 = h1_ref[rows, :]
        grad = own_ref[rows, :].astype(f32) + rec_ref[rows, :].astype(f32)
        inv = inv_rms(h1)
        dh1 = dh2_ref[rows, :] + norm_back(h1, inv, gain, grad)
        dgain += jnp.sum(h1 * inv * grad, 0, keepdims=True)
        dh1_ref[rows, :] = dh1
        da_ref[rows, :] = dh1.astype(bf16)
    dgain_ref[...] = dgain
    outs = start_copies(out_sems, (dh1_ref, dh1_hbm), (da_ref, da_hbm))
    inner = dmix_ref.shape[1]
    own_at = pl.multiple_of(lax.axis_index("mp") * inner, inner)
    dmix_ref[...] = dot_nt(da_ref[...], wo_ref[pl.ds(own_at, inner), :]).astype(bf16)
    for copy in copies[2:] + outs:
        copy.wait()


def attend_back_kernel(wq_hbm, wk_hbm, wv_hbm, n1_hbm, q_ref, k_ref, v_ref, probs_ref, *rest):
    mixg_refs = rest[:CHUNKS]
    ids_ref, grads_ref, biasg_ref, w_ref, n1_ref, ds_ref, skew_ref, rel_ref, dp_ref, mixg_ref, sems = rest[CHUNKS:]
    length, inner = q_ref.shape
    blocks = length // BLOCK
    pairs = inner // BLOCK
    span = rel_ref.shape[1]
    later = start_copies(
        sems, (wq_hbm, w_ref.at[0]), (wk_hbm, w_ref.at[1]), (wv_hbm, w_ref.at[2]), (n1_hbm, n1_ref)
    )
    low_lanes = lax.broadcasted_iota(jnp.int32, (BLOCK, BLOCK), 1) < BLOCK // 2
    low_all = lax.broadcasted_iota(jnp.int32, (length, BLOCK), 1) < BLOCK // 2
    zero = jnp.zeros((BLOCK, BLOCK), bf16)
    rel_ref[...] = jnp.zeros_like(rel_ref)
    for i, part in enumerate(mixg_refs):
        mixg_ref[i * part.shape[0] : (i + 1) * part.shape[0], :] = part[...]

    @pl.loop(0, pairs)
    def _(pair):
        lanes = pl.ds(pl.multiple_of(pair * BLOCK, BLOCK), BLOCK)
        skew_ref[...] = jnp.zeros_like(skew_ref)
        for b in range(blocks):
            first, last = key_range(b, blocks)
            rows = slice(b * BLOCK, (b + 1) * BLOCK)
            keys = slice(first * BLOCK, last * BLOCK)
            shift = length - BLOCK - b * BLOCK
            g_pair = mixg_ref[rows, lanes]
            k_pair = k_ref[keys, lanes]
            v_pair = v_ref[keys, lanes]
            width = (last - first) * BLOCK
            for h in range(2):
                g_one = jnp.where(low_lanes if h == 0 else ~low_lanes, g_pair, zero)
                dp_ref[h, :, :width] = dot_nt(g_one, v_pair)
            for at in range(0, BLOCK, STRIP):
                part = slice(b * BLOCK + at, b * BLOCK + at + STRIP)
                for h in range(2):
                    probs = probs_ref[pair * 2 + h, part, keys].astype(f32)
                    weighted = probs * dp_ref[h, at : at + STRIP, :width]
                    ds = weighted - probs * jnp.sum(weighted, -1, keepdims=True)
                    ds_ref[h, part, keys] = ds.astype(bf16)
                    if first > 0:
                        ds_ref[h, part, 0 : first * BLOCK] = jnp.zeros((STRIP, first * BLOCK), bf16)
                    if last < blocks:
                        ds_ref[h, part, last * BLOCK :] = jnp.zeros((STRIP, length - last * BLOCK), bf16)
                    skew_ref[h, at : at + STRIP, shift + first * BLOCK : shift + last * BLOCK] += ds
            grads_ref[rows, lanes] = jnp.where(
                low_lanes,
                dot_nn(ds_ref[0, rows, keys], k_pair),
                dot_nn(ds_ref[1, rows, keys], k_pair),
            ).astype(bf16)
        q_pair = q_ref[:, lanes]
        g_pair = mixg_ref[:, lanes]
        k_lanes = pl.ds(pl.multiple_of(inner + pair * BLOCK, BLOCK), BLOCK)
        v_lanes = pl.ds(pl.multiple_of(2 * inner + pair * BLOCK, BLOCK), BLOCK)
        grads_ref[:, k_lanes] = jnp.where(
            low_all, dot_tn(ds_ref[0], q_pair), dot_tn(ds_ref[1], q_pair)
        ).astype(bf16)
        grads_ref[:, v_lanes] = jnp.where(
            low_all,
            dot_tn(probs_ref[pair * 2], g_pair),
            dot_tn(probs_ref[pair * 2 + 1], g_pair),
        ).astype(bf16)
        for h in range(2):
            tiles = skew_ref[h, BLOCK - 8 :, :]
            for r in range(0, BLOCK - 8, 8):
                tiles += pltpu.roll(skew_ref[h, r : r + 8, :], BLOCK - 8 - r, 1)
            line = tiles[7:8, :]
            for r in range(7):
                line += pltpu.roll(tiles[r : r + 1, :], 7 - r, 1)
            rel_ref[pl.ds(pair * 2 + h, 1), :] = line

    hot = (
        lax.broadcasted_iota(jnp.int32, (biasg_ref.shape[0], span - 1), 0)
        == ids_ref[...].reshape(1, span - 1)
    ).astype(f32)
    total = lax.dot_general(
        hot, rel_ref[:, : span - 1], (((1,), (1,)), ((), ())), precision=highest, preferred_element_type=f32
    )
    biasg_ref[...] = total[:, : biasg_ref.shape[1]]
    for copy in later:
        copy.wait()


def project_back_kernel(w_ref, tok_ref, grads_ref, *refs):
    part_refs, (part_hbm, dgain_ref, part_ref, sems) = refs[:CHUNKS], refs[CHUNKS:]
    length, width = part_ref.shape
    inner = w_ref.shape[2]
    size = length // CHUNKS
    for c in range(CHUNKS):
        rows = slice(c * size, (c + 1) * size)
        part = (
            dot_nt(grads_ref[rows, :inner], w_ref[0])
            + dot_nt(grads_ref[rows, inner : 2 * inner], w_ref[1])
            + dot_nt(grads_ref[rows, 2 * inner :], w_ref[2])
        ).astype(bf16)
        part_ref[rows, :] = part
        part_refs[c][...] = part
    (copy,) = start_copies(sems, (part_ref, part_hbm))
    dgain = jnp.zeros((1, width), f32)
    for at in range(0, length, STRIP):
        rows = slice(at, at + STRIP)
        x = tok_ref[rows, :].astype(f32)
        dgain += jnp.sum(x * inv_rms(x) * part_ref[rows, :].astype(f32), 0, keepdims=True)
    dgain_ref[...] = dgain
    copy.wait()


def last_kernel(own_hbm, *refs):
    stored_refs, (tok_ref, gain_ref), received = refs[:CHUNKS], refs[CHUNKS : CHUNKS + 2], refs[CHUNKS + 2 : 2 * CHUNKS + 2]
    out_ref, own_ref, dh1_ref, sems = refs[-4:]
    size = own_ref.shape[0] // CHUNKS
    copies = start_copies(
        sems, (own_hbm, own_ref), *[(stored_refs[c], dh1_ref.at[pl.ds(c * size, size), :]) for c in range(CHUNKS)]
    )
    gain = row_gain(gain_ref)
    for copy in copies:
        copy.wait()
    for at in range(0, CHUNKS * size, STRIP):
        rows = slice(at, at + STRIP)
        there = slice(at % size, at % size + STRIP)
        x = tok_ref[rows, :].astype(f32)
        grad = own_ref[rows, :].astype(f32) + received[at // size][there, :].astype(f32)
        out_ref[rows, :] = dh1_ref[rows, :] + norm_back(x, inv_rms(x), gain, grad)


def weight_products(lefts, rights, other_refs, own_ref, columns=0):
    tower_index = lax.axis_index("tower")
    half = lefts[0].shape[1] // 2
    for which in (1 - tower_index, tower_index):
        is_own = which is tower_index
        lanes = pl.ds(pl.multiple_of(which * half, half), half)
        turned = [left[:, lanes].T for left in lefts]
        for at in range(0, rights[0].shape[1], PIECE):
            total = None
            for left, right in zip(turned, rights):
                term = dot_nn(left, right[:, at : at + PIECE])
                total = term if total is None else total + term
            there = columns + at
            if is_own:
                own_ref[:, there : there + PIECE] = total.astype(bf16)
            else:
                other_refs[there // PIECE][...] = total.astype(bf16)


def query_key_kernel(shard, n1_ref, grads_ref, bias_ref, *refs):
    inner = grads_ref.shape[1] // 3
    count = 2 * inner // PIECE + 3
    parts, outs, all_ref = refs[:-count], refs[-count:-1], refs[-1]
    own_ref = outs[-1]
    tower_index = lax.axis_index("tower")
    width = all_ref.shape[0]
    half = width // 2
    buckets, heads = bias_ref.shape
    lane = lax.broadcasted_iota(jnp.int32, (1, LANES), 1)

    def low(values):
        return values.astype(f32).astype(bf16)

    row = lax.broadcasted_iota(jnp.int32, (width, buckets), 0) % shard
    col = lax.broadcasted_iota(jnp.int32, (width, buckets), 1)
    total = jnp.zeros((width, LANES), f32)
    for g in range(-(-buckets // shard)):
        place = lax.broadcasted_iota(jnp.int32, (heads, LANES), 0) + 3 + g * heads == lane
        total += dot_nn(low(col == row + g * shard), low(dot_nn(low(bias_ref[...]), low(place))))
    lines = [
        sum(part[...] for part in some) for some in (parts[:1], parts[1 : 1 + CHUNKS], parts[1 + CHUNKS :])
    ]
    place = lax.broadcasted_iota(jnp.int32, (3, LANES), 0) == lane
    all_ref[...] = total + dot_tn(low(jnp.concatenate(lines, 0)), low(place))
    outs[-2][...] = all_ref[pl.ds(pl.multiple_of((1 - tower_index) * half, half), half), :].astype(bf16)
    own_ref[:, 2 * inner :] = all_ref[pl.ds(pl.multiple_of(tower_index * half, half), half), :].astype(bf16)
    weight_products([n1_ref], [grads_ref.at[:, : 2 * inner]], outs[:-2], own_ref)


def value_output_kernel(*refs):
    stored_refs = refs[: CHUNKS + 1]
    n1_ref, grads_ref, *outs = refs[CHUNKS + 1 : -2 - CHUNKS]
    mix_ref, *da_refs = refs[-2 - CHUNKS : -1]
    copies = start_copies(refs[-1], *zip(stored_refs, (mix_ref, *da_refs)))
    inner = grads_ref.shape[1] // 3
    weight_products([n1_ref], [grads_ref.at[:, 2 * inner :]], outs[:-1], outs[-1])
    for copy in copies:
        copy.wait()
    size = da_refs[0].shape[0]
    pieces = [mix_ref.at[c * size : (c + 1) * size, :] for c in range(CHUNKS)]
    weight_products(da_refs, pieces, outs[:-1], outs[-1], inner)


def split_kernel(shard, bit, low, own_ref, *refs):
    rec_refs, (keep_ref, send_ref) = refs[:-2], refs[-2:]
    own_bit = lax.axis_index("rows") // bit % 2
    at = 0
    for rec_ref in rec_refs:
        cols = slice(at, at + rec_ref.shape[1])
        at = cols.stop
        for j in range(keep_ref.shape[0] // shard):
            for which, out_ref in ((own_bit, keep_ref), (1 - own_bit, send_ref)):
                start = ((j // low * 2 + which) * low + j % low) * shard
                rows = pl.ds(pl.multiple_of(start, shard), shard)
                out_ref[j * shard : (j + 1) * shard, cols] = (
                    own_ref[rows, cols].astype(f32) + rec_ref[rows, :].astype(f32)
                ).astype(bf16)


def fixed(shape, dtype):
    return pltpu.VMEM(shape, dtype)


def stored(shape, dtype):
    return pltpu.HBM(shape, dtype)


def whole(name, kernel, out_shapes, *args, scratch=(), in_hbm=0, in_vmem=0, mib=16):
    args = (
        [pltpu.with_memory_space_constraint(v, pltpu.HBM) for v in args[:in_hbm]]
        + [pltpu.with_memory_space_constraint(v, pltpu.VMEM) for v in args[in_hbm : in_hbm + in_vmem]]
        + list(args[in_hbm + in_vmem :])
    )
    vmem = pl.BlockSpec(memory_space=pltpu.VMEM)
    hbm = pl.BlockSpec(memory_space=pl.ANY)
    is_stored = lambda out: getattr(out, "memory_space", None) == pltpu.HBM
    with jax.named_scope(name):
        return pl.pallas_call(
            kernel,
            out_shape=out_shapes,
            in_specs=[hbm] * in_hbm + [vmem] * (len(args) - in_hbm),
            out_specs=jax.tree.map(lambda out: hbm if is_stored(out) else vmem, out_shapes),
            scratch_shapes=scratch,
            compiler_params=pltpu.CompilerParams(vmem_limit_bytes=mib * 1024 * 1024),
            cost_estimate=pl.CostEstimate(flops=1, bytes_accessed=1, transcendentals=0),
        )(*args)


def start_copies(sems, *pairs):
    copies = [pltpu.make_async_copy(src, dst, sems.at[i]) for i, (src, dst) in enumerate(pairs)]
    for copy in copies:
        copy.start()
    return copies


def swap(values, axis, bit=1):
    count = lax.axis_size(axis)
    return lax.ppermute(values, axis, [(i, i ^ bit) for i in range(count)])


def gather_all(values):
    bit = 1
    while bit < lax.axis_size("rows"):
        values = jnp.concatenate([values, swap(values, "rows", bit)], 0)
        bit *= 2
    return jnp.concatenate([values, swap(values, "tower")], 0)


def row_halves(cur, bit, low, shard):
    columns = cur.shape[-1]
    view = cur.reshape(-1, 2, low * shard, columns)
    own_bit = (lax.axis_index("rows") & bit) // bit
    keep = lax.dynamic_index_in_dim(view, own_bit, 1, False).reshape(-1, columns)
    send = lax.dynamic_index_in_dim(view, 1 - own_bit, 1, False).reshape(-1, columns)
    return keep, send


class RowsScatter:
    def __init__(self, name, shard, own, received, swapped=False):
        self.name, self.shard = name, shard
        self.own, self.received = own, received
        self.bits = [1 << i for i in range(lax.axis_size("rows").bit_length() - 1)]
        self.order = list(self.bits)
        if swapped and len(self.order) > 1:
            self.order[0], self.order[1] = self.order[1], self.order[0]

    def split(self):
        self.bit = self.order.pop(0)
        low = 1 << sorted(self.bits).index(self.bit)
        self.bits.remove(self.bit)
        columns = self.own.shape[1]
        if self.shard % 16 == 0:
            half = struct((self.own.shape[0] // 2, columns), bf16)
            self.own, self.send = whole(
                self.name, functools.partial(split_kernel, self.shard, self.bit, low), (half, half), self.own, *self.received
            )
        else:
            total = self.total().astype(bf16)
            self.own, self.send = row_halves(total, self.bit, low, self.shard)

    def exchange(self):
        self.received = [swap(self.send, "rows", self.bit)]

    def total(self):
        return self.own.astype(f32) + jnp.concatenate(self.received, 1).astype(f32)

    def step(self):
        self.split()
        self.exchange()

    def finish(self):
        while self.order:
            self.step()
        return self.total()


def tie(*values):
    return lax.optimization_barrier(values)


def struct(shape, dtype):
    return jax.ShapeDtypeStruct(shape, dtype)


def per_device(
    tokens,
    segment_ids,
    pair_ids,
    bucket_ids,
    attn_gain,
    query_weight,
    key_weight,
    value_weight,
    output_weight,
    bias_table,
    ff_gain,
    up_weight,
    down_weight,
    final_gain,
    proj_weight,
):
    length = tokens.shape[2]
    width = tokens.shape[3]
    inner = query_weight.shape[1]
    hidden = up_weight.shape[1]
    head_count = bias_table.shape[1]
    bucket_count = bias_table.shape[0]
    total_segs = pair_ids.shape[0]
    span = 2 * length
    size = length // CHUNKS
    chunks = range(CHUNKS)
    tower_index = lax.axis_index("tower")
    device_index = tower_index * lax.axis_size("rows") + lax.axis_index("rows")
    shard = width // (2 * lax.axis_size("rows"))

    token_row = tokens.reshape(length, width)
    segments = segment_ids.reshape(1, length)

    part_rows = inner // 2
    fetched = swap(
        lax.dynamic_slice_in_dim(output_weight, tower_index * part_rows, part_rows, 0), "mp"
    )

    normed_one, query, key, value, probs, mix_stored, tok, *mixes = whole(
        "attention",
        attend_kernel,
        (
            stored((length, width), bf16),
            stored((length, inner), bf16),
            stored((length, inner), bf16),
            stored((length, inner), bf16),
            stored((head_count, length, length), bf16),
            stored((length, inner), bf16),
            fixed((length, width), bf16),
        )
        + (fixed((size, inner), bf16),) * CHUNKS,
        token_row,
        query_weight,
        key_weight,
        value_weight,
        attn_gain,
        bias_table.T,
        bucket_ids,
        segments,
        scratch=[
            pltpu.VMEM((3, width, inner), bf16),
            pltpu.VMEM((width,), f32),
            pltpu.VMEM((head_count, bucket_count), f32),
            pltpu.VMEM((span - 1,), jnp.int32),
            pltpu.VMEM((1, length), jnp.int32),
            pltpu.VMEM((length, width), bf16),
            pltpu.VMEM((length, inner), bf16),
            pltpu.VMEM((length, inner), bf16),
            pltpu.VMEM((length, inner), bf16),
            pltpu.VMEM((head_count, length, length), bf16),
            pltpu.VMEM((length, inner), bf16),
            pltpu.VMEM((8, span), f32),
            pltpu.VMEM((length, length), f32),
            pltpu.VMEM((2, BLOCK, span), f32),
            pltpu.VMEM((2, BLOCK, length), f32),
            pltpu.SemaphoreType.DMA((8,)),
            pltpu.SemaphoreType.DMA((5 + inner // BLOCK,)),
        ],
        in_hbm=8,
        mib=24,
    )
    mix_received = [swap(mix, "mp") for mix in mixes]
    fetched, segments = tie(fetched, tie(segments, mixes[-1])[0])
    fetched_too = swap(fetched, "tower")
    output_whole, up_held, down_held, proj_held = whole(
        "load",
        load_kernel,
        (
            fixed((2 * inner, width), bf16),
            fixed((width, hidden), bf16),
            fixed((hidden, width), bf16),
            fixed((width, width), bf16),
        ),
        output_weight,
        up_weight,
        down_weight,
        proj_weight,
        fetched,
        fetched_too,
        scratch=[pltpu.SemaphoreType.DMA((6,))],
        in_hbm=4,
    )

    hidden_one, normed_two, active, slope, ff_part, ff_received = [], [], [], [], [], []
    for c in chunks:
        outs = whole(
            "feed_forward",
            functools.partial(ff_kernel, c),
            (
                fixed((size, width), f32),
                fixed((size, width), bf16),
                fixed((size, hidden), bf16),
                fixed((size, hidden), f32),
                fixed((size, width), bf16),
            ),
            tok,
            output_whole,
            up_held,
            down_held,
            mixes[c],
            mix_received[c],
            ff_gain,
            scratch=[pltpu.VMEM((size, 2 * inner), bf16)],
            in_vmem=5,
        )
        for kept, out in zip((hidden_one, normed_two, active, slope, ff_part), outs):
            kept.append(out)
        ff_received.append(swap(ff_part[c], "mp"))

    hidden_two, pooled = [], []
    for c in chunks:
        h2, total = whole(
            "pool",
            functools.partial(pool_kernel, c),
            (
                fixed((size, width), f32),
                struct((SEGS_ROW, width), bf16 if c == CHUNKS - 1 else f32),
            ),
            hidden_one[c],
            ff_part[c],
            ff_received[c],
            final_gain,
            segments,
            *pooled,
            in_vmem=2,
        )
        hidden_two.append(h2)
        pooled = [total]
    gathered = gather_all(pooled[0])
    loss, proj_grad, pooled_grad = whole(
        "contrast",
        functools.partial(contrast_kernel, total_segs),
        (
            struct((1, 1), f32),
            struct((shard, width), f32),
            struct((SEGS_ROW, width), f32),
        ),
        proj_held,
        gathered,
        pair_ids,
        in_vmem=1,
    )

    two_part, two_own, two_received, hidden_two_grad, final_gain_part = [], [], [], [], []
    ff_grad, up_out_grad = [], []
    half_shapes = (struct((width // 2, PIECE), bf16),) * (hidden // PIECE) + (struct((width // 2, hidden), bf16),)
    for c in chunks:
        last = c == CHUNKS - 1
        low_shape = ((size, width), bf16)
        outs = whole(
            "feed_forward_back",
            functools.partial(ff_back_kernel, c),
            (
                struct((size, width), bf16),
                stored((size, width), bf16),
                stored((size, width), f32),
                struct((1, width), f32),
                fixed((size, hidden), bf16),
            )
            + (half_shapes if last else (fixed(*low_shape),)),
            down_held,
            up_held,
            hidden_two[c],
            slope[c],
            *([*active, *ff_grad] if last else []),
            pooled_grad,
            segments,
            final_gain,
            scratch=([pltpu.VMEM(*low_shape)] if last else [])
            + [pltpu.VMEM((size, width), f32), pltpu.SemaphoreType.DMA((2,))],
            in_vmem=4 + (2 * CHUNKS - 1 if last else 0),
        )
        for kept, out in zip((two_part, two_own, hidden_two_grad, final_gain_part, up_out_grad), outs):
            kept.append(out)
        if not last:
            ff_grad.append(outs[5])
        two_received.append(swap(two_part[c], "mp"))
    down_scatter = RowsScatter("down_split", shard, outs[-1], [swap(v, "tower") for v in outs[5:-1]])

    hidden_one_grad, attn_grad, mix_grad, ff_gain_part = [], [], [], []
    for c in chunks:
        first, last = c == 0, c == CHUNKS - 1
        if last:
            down_scatter.split()
            up_scatter.split()
            two_received[c], down_scatter.send, up_scatter.send = tie(
                two_received[c], down_scatter.send, up_scatter.send
            )
            down_scatter.exchange()
            up_scatter.exchange()
        heads_shape = fixed((length, inner), bf16)
        outs = whole(
            "middle_back",
            functools.partial(middle_back_kernel, c),
            (
                stored((size, width), f32),
                stored((size, width), bf16),
                fixed((size, inner), bf16),
                struct((1, width), f32),
            )
            + ((heads_shape,) * 3 + (fixed((head_count, length, length), bf16),) if last else ())
            + (half_shapes if first else ()),
            two_own[c],
            hidden_two_grad[c],
            *([query, key, value, probs] if last else []),
            output_whole,
            hidden_one[c],
            *([*normed_two, *up_out_grad] if first else []),
            two_received[c],
            ff_gain,
            scratch=[
                pltpu.VMEM((size, width), bf16),
                pltpu.VMEM((size, width), f32),
                pltpu.VMEM((size, width), f32),
                pltpu.VMEM((size, width), bf16),
                pltpu.SemaphoreType.DMA((6,)),
                pltpu.SemaphoreType.DMA((2,)),
            ],
            in_hbm=6 if last else 2,
            in_vmem=2 + (2 * CHUNKS if first else 0),
        )
        for kept, out in zip((hidden_one_grad, attn_grad, mix_grad, ff_gain_part), outs):
            kept.append(out)
        if first:
            up_scatter = RowsScatter(
                "up_split", shard, outs[-1], [swap(v, "tower") for v in outs[4:-1]], swapped=True
            )
        if last:
            heads_held = outs[4:8]

    qkv_grads, bias_grad, qkv_weight, normed_held = whole(
        "attention_back",
        attend_back_kernel,
        (
            fixed((length, 3 * inner), bf16),
            struct((bucket_count, head_count), f32),
            fixed((3, width, inner), bf16),
            fixed((length, width), bf16),
        ),
        query_weight,
        key_weight,
        value_weight,
        normed_one,
        *heads_held,
        *mix_grad,
        bucket_ids,
        scratch=[
            pltpu.VMEM((2, length, length), bf16),
            pltpu.VMEM((2, BLOCK, span), f32),
            pltpu.VMEM((8, span), f32),
            pltpu.VMEM((2, BLOCK, length), f32),
            pltpu.VMEM((length, inner), bf16),
            pltpu.SemaphoreType.DMA((4,)),
        ],
        in_hbm=4,
        in_vmem=4 + CHUNKS,
    )
    *one_part, one_own, attn_gain_part = whole(
        "project_back",
        project_back_kernel,
        (struct((size, width), bf16),) * CHUNKS
        + (stored((length, width), bf16), struct((1, width), f32)),
        qkv_weight,
        tok,
        qkv_grads,
        scratch=[pltpu.VMEM((length, width), bf16), pltpu.SemaphoreType.DMA((1,))],
        in_vmem=3,
    )
    one_received = [swap(part, "mp") for part in one_part]

    piece = struct((width // 2, PIECE), bf16)
    *others, small_other, own = whole(
        "query_key_weight",
        functools.partial(query_key_kernel, shard),
        (piece,) * (2 * inner // PIECE)
        + (struct((width // 2, LANES), bf16), struct((width // 2, 2 * inner + LANES), bf16)),
        normed_held,
        qkv_grads,
        bias_grad,
        attn_gain_part,
        *ff_gain_part,
        *final_gain_part,
        scratch=[pltpu.VMEM((width, LANES), f32)],
        in_vmem=2,
    )
    first_scatter = RowsScatter("query_key_split", shard, own, [swap(v, "tower") for v in (*others, small_other)])
    *others, own = whole(
        "value_output_weight",
        value_output_kernel,
        (piece,) * (2 * inner // PIECE) + (struct((width // 2, 2 * inner), bf16),),
        mix_stored,
        *attn_grad,
        normed_held,
        qkv_grads,
        scratch=[pltpu.VMEM((length, inner), bf16)]
        + [pltpu.VMEM((size, width), bf16)] * CHUNKS
        + [pltpu.SemaphoreType.DMA((1 + CHUNKS,))],
        in_hbm=1 + CHUNKS,
        in_vmem=2,
    )
    second_scatter = RowsScatter(
        "value_output_split", shard, own, [swap(v, "tower") for v in others], swapped=True
    )
    first_scatter.split()
    second_scatter.split()
    down_scatter.split()
    up_scatter.split()
    one_received[0], first_scatter.send, second_scatter.send, down_scatter.send, up_scatter.send = tie(
        one_received[0], first_scatter.send, second_scatter.send, down_scatter.send, up_scatter.send
    )
    first_scatter.exchange()
    second_scatter.exchange()
    down_scatter.exchange()
    up_scatter.exchange()
    down_sum = down_scatter.finish()
    up_sum = up_scatter.finish()
    first_sum = first_scatter.finish()
    second_sum = second_scatter.finish()
    small = first_sum[:, 2 * inner :]
    attn_gain_sum = small[:, 0:1] + swap(small[:, 0:1], "mp")
    bias_rows = [
        small[:, 3 + g * head_count : 3 + (g + 1) * head_count]
        for g in range(-(-bucket_count // shard))
    ]
    bias_total = jnp.concatenate(bias_rows, 0)[:bucket_count]

    tokens_grad = whole(
        "last",
        last_kernel,
        struct((length, width), f32),
        one_own,
        *hidden_one_grad,
        tok,
        attn_gain,
        *one_received,
        scratch=[
            pltpu.VMEM((length, width), bf16),
            pltpu.VMEM((length, width), f32),
            pltpu.SemaphoreType.DMA((1 + CHUNKS,)),
        ],
        in_hbm=1 + CHUNKS,
        in_vmem=1,
    ).reshape(tokens.shape)
    return (
        loss[0, 0],
        tokens_grad,
        attn_gain_sum[:, 0],
        first_sum[:, :inner],
        first_sum[:, inner : 2 * inner],
        second_sum[:, :inner],
        second_sum[:, inner:].T,
        bias_total,
        small[:, 1],
        up_sum,
        down_sum.T,
        small[:, 2],
        proj_grad,
    )


def solution(mesh):
    in_specs = (
        P("tower", "rows", None, None),
        P("tower", "rows", None),
        P(),
        P(),
        P(),
        P(None, "mp"),
        P(None, "mp"),
        P(None, "mp"),
        P("mp", None),
        P(None, "mp"),
        P(),
        P(None, "mp"),
        P("mp", None),
        P(),
        P(),
    )
    out_specs = (
        P(),
        P("tower", "rows", None, None),
        P(("tower", "rows")),
        P(("tower", "rows"), "mp"),
        P(("tower", "rows"), "mp"),
        P(("tower", "rows"), "mp"),
        P("mp", ("tower", "rows")),
        P(None, "mp"),
        P(("tower", "rows")),
        P(("tower", "rows"), "mp"),
        P("mp", ("tower", "rows")),
        P(("tower", "rows")),
        P(("tower", "rows"), None),
    )
    return jax.shard_map(
        per_device, mesh=mesh, in_specs=in_specs, out_specs=out_specs, check_vma=False
    )
```

time: 234 us -> 158 us (0.68)
  matrix products: 37.7 us -> 0 us
  waiting for transfers between devices: 94.2 us -> 61.8 us
  Pallas kernels: 26.3 us -> 55.9 us
  other arithmetic: 19.2 us -> 2.28 us
  local copies, waits for them, and re-layouts: 18.3 us -> 3.11 us
  between operations: 4.62 us -> 0.99 us
    dot_general x25 -> x0, matrix products: 37.7 us -> none  [the longest x10 15.6 us: dot_tn(): lax.dot_general(a, b, (((0,), (0,)), ((), ())), preferred_element_type=f32)]
    ppermute x28 -> x40, waiting for transfers between devices: 94.2 us -> 61.8 us  [swap(): return lax.ppermute(values, axis, [(i, i ^ bit) for i in range(count)])]
    pallas_call x2 -> x28, Pallas kernels: 26.3 us -> 55.9 us  [whole(): pl.pallas_call(kernel, out_shape=out_shapes, in_specs=[hbm] * in_hbm + [v...]
    unnamed x124 -> x17, local copies, waits for them, and re-layouts: 8.99 us -> 0.71 us
    reduce_sum x8 -> x0, other arithmetic: 6.82 us -> none  [the longest x2 4.29 us: norm_back(): jnp.sum(values * inv * grad, 0)]
    convert_element_type x13 -> x0, other arithmetic: 6.67 us -> none  [the longest x1 3.03 us: per_device(): attn_grad = hidden_one_grad.astype(bf16)]
    reshape x1 -> x0, other arithmetic: 2.76 us -> none  [per_device(): tokens_grad = (hidden_one_grad + part).reshape(tokens.shape)]
    ppermute x28 -> x40, starting transfers between devices: 33.1 us -> 33.3 us  [swap(): return lax.ppermute(values, axis, [(i, i ^ bit) for i in range(count)])]
  transfers between devices with their start and end apart: 28 -> 40, of which waited for: 16 -> 26; matrix products, arithmetic and copies ran while one was open for 19% -> 2% of each run, Pallas kernels for 5% -> 24%
where the time goes in v1:
time: 158 us; the launch traced here: 157 us
  waiting for transfers between devices  61.8 us (39%)
  Pallas kernels  55.9 us (35%)
  starting transfers between devices  33.3 us (21%)
  local copies, waits for them, and re-layouts  3.11 us (2%)
  other arithmetic  2.28 us (1%)
    ppermute x40, waiting for transfers between devices, swap(): return lax.ppermute(values, axis, [(i, i ^ bit) for i in range(count)])  61.8 us
    pallas_call x28, Pallas kernels, whole(): pl.pallas_call(kernel, out_shape=out_shapes, in_specs=[hbm] * in_hbm + [v...  55.9 us
    ppermute x40, starting transfers between devices, swap(): return lax.ppermute(values, axis, [(i, i ^ bit) for i in range(count)])  33.3 us
  transfers between devices with their start and end apart: 40, of which 26 were waited for; matrix products, arithmetic and copies ran while one was open for 2% of the time, Pallas kernels for 24%

profile of v1, /device:TPU:0, one launch (start us, length us, event | category | flops | bytes accessed | tf_op | source)
XLA Modules:
  0.0 157.4 jit_solution(13377324056626583305)
XLA Ops:
  1.6 3.0 %collective-permute-start = (bf16[192,768]{1,0:T(8,128)(2,1)S(1)}, bf16[192,768]{1,0:T(8,128)(2,1)S(1)}, u32[]{:S(2)}, u32[]{:S(2)}) collective-permute-start(bf16[192,768]{1,0:T(8,128)(2,1)S(1)} %constant_dynamic-slice_fusion), channel_id=1, source_target_pairs={{0,1},{1,0},{2,3},{3,2},{4,5},{5,4},{6,7},{7,6},{8,9},{9,8},{10,11... | collective-permute-start | bytes 884744 | tf_op jit(solution)/shard_map/ppermute | solution.py:636
  4.7 10.7 %attention.1 = (bf16[512,768]{1,0:T(8,128)(2,1)}, bf16[512,384]{1,0:T(8,128)(2,1)}, bf16[512,384]{1,0:T(8,128)(2,1)}, bf16[512,384]{1,0:T(8,128)(2,1)}, bf16[6,5...) custom-call(bf16[512,768]{1,0:T(8,128)(2,1)} %bitcast.15, ...), custom_call_target="tpu_custom_call" | custom-call | flops 1 | bytes 1 | tf_op jit(solution)/shard_map/attention/pallas_call | solution.py:616
  15.6 2.0 %collective-permute-start.2 = (bf16[256,384]{1,0:T(8,128)(2,1)S(1)}, bf16[256,384]{1,0:T(8,128)(2,1)S(1)}, u32[]{:S(2)}, u32[]{:S(2)}) collective-permute-start(bf16[256,384]{1,0:T(8,128)(2,1)S(1)} %get-tuple-element.126.mix_own), channel_id=1, source_target_pairs={{0,1},{1,0},{2,3},{3,2},{4,5},{5,4},{6,7},{7,6},{8,9},{9,8},{10,11... | collective-permute-start | bytes 589832 | tf_op jit(solution)/shard_map/ppermute | solution.py:636
  17.6 3.1 %load.1 = (bf16[768,768]{1,0:T(8,128)(2,1)S(1)}, bf16[768,1536]{1,0:T(8,128)(2,1)S(1)}, bf16[1536,768]{1,0:T(8,128)(2,1)S(1)}, bf16[768,768]{1,0:T(8,128)(2,1)S(1)}) custom-call(bf16[384,768]{1,0:T(8,128)(2,1)} %wo_hbm.1, bf16[768,1536]{1,0:T(8,128)(2,1)} %up_hbm.1, bf16[1536,768]{1,0:T(8,128)(2,1)} %down_hbm.1, bf16[768,768]{1,0:T(8,128)(2,1)} %proj_hbm.1, ...), custom_call_target="tpu_custom_call" | custom-call | flops 1 | bytes 1 | tf_op jit(solution)/shard_map/load/pallas_call | solution.py:616
  20.7 2.6 %collective-permute-done.4.mix_other = bf16[256,384]{1,0:T(8,128)(2,1)S(1)} collective-permute-done((bf16[256,384]{1,0:T(8,128)(2,1)S(1)}, bf16[256,384]{1,0:T(8,128)(2,1)S(1)}, u32[]{:S(2)}, u32[]{:S(2)}) %collective-permute-start.4) | collective-permute-done | bytes 196640 | tf_op jit(solution)/shard_map/ppermute | solution.py:636
  23.3 3.3 %feed_forward.3 = (f32[256,768]{1,0:T(8,128)S(1)}, bf16[256,768]{1,0:T(8,128)(2,1)S(1)}, bf16[256,1536]{1,0:T(8,128)(2,1)S(1)}, f32[256,1536]{1,0:T(8,128)S(1)}, bf16[256,768]{1,0:T(8,128)(2,1)S(1)}) custom-call(bf16[512,768]{1,0:T(8,128)(2,1)S(1)} %get-tuple-element.130.tok_ref.refs_2_, bf16[768,768]{1,0:T(8,128)(2,1)S(1)} %get-tuple-element.131.wo_ref.refs_2_.refs_6_, ...), custom_call_target="tpu_custom_call" | custom-call | flops 1 | bytes 1 | tf_op jit(solution)/shard_map/feed_forward/pallas_call | solution.py:616
  27.0 3.3 %feed_forward.2 = (f32[256,768]{1,0:T(8,128)S(1)}, bf16[256,768]{1,0:T(8,128)(2,1)S(1)}, bf16[256,1536]{1,0:T(8,128)(2,1)S(1)}, f32[256,1536]{1,0:T(8,128)S(1)}, bf16[256,768]{1,0:T(8,128)(2,1)S(1)}) custom-call(bf16[512,768]{1,0:T(8,128)(2,1)S(1)} %get-tuple-element.130.tok_ref.refs_2_, bf16[768,768]{1,0:T(8,128)(2,1)S(1)} %get-tuple-element.131.wo_ref.refs_2_.refs_6_, ...), custom_call_target="tpu_custom_call" | custom-call | flops 1 | bytes 1 | tf_op jit(solution)/shard_map/feed_forward/pallas_call | solution.py:616
  32.1 6.7 %collective-permute-done.5.rec_ref = bf16[256,768]{1,0:T(8,128)(2,1)S(1)} collective-permute-done((bf16[256,768]{1,0:T(8,128)(2,1)S(1)}, bf16[256,768]{1,0:T(8,128)(2,1)S(1)}, u32[]{:S(2)}, u32[]{:S(2)}) %collective-permute-start.5) | collective-permute-done | bytes 393248 | tf_op jit(solution)/shard_map/ppermute | solution.py:636
  39.1 6.2 %collective-permute-done.3.rec_ref = bf16[256,768]{1,0:T(8,128)(2,1)S(1)} collective-permute-done((bf16[256,768]{1,0:T(8,128)(2,1)S(1)}, bf16[256,768]{1,0:T(8,128)(2,1)S(1)}, u32[]{:S(2)}, u32[]{:S(2)}) %collective-permute-start.3) | collective-permute-done | bytes 393248 | tf_op jit(solution)/shard_map/ppermute | solution.py:636
  47.3 2.2 %collective-permute-done.6 = bf16[8,768]{1,0:T(8,128)(2,1)S(1)} collective-permute-done((bf16[8,768]{1,0:T(8,128)(2,1)S(1)}, bf16[8,768]{1,0:T(8,128)(2,1)S(1)}, u32[]{:S(2)}, u32[]{:S(2)}) %collective-permute-start.6) | collective-permute-done | bytes 12320 | tf_op jit(solution)/shard_map/ppermute | solution.py:636
  51.1 2.8 %collective-permute-done.7 = bf16[16,768]{1,0:T(8,128)(2,1)S(1)} collective-permute-done((bf16[16,768]{1,0:T(8,128)(2,1)S(1)}, bf16[16,768]{1,0:T(8,128)(2,1)S(1)}, u32[]{:S(2)}, u32[]{:S(2)}) %collective-permute-start.7) | collective-permute-done | bytes 24608 | tf_op jit(solution)/shard_map/ppermute | solution.py:636
  53.8 2.1 %collective-permute-start.8 = (bf16[32,768]{1,0:T(8,128)(2,1)S(1)}, bf16[32,768]{1,0:T(8,128)(2,1)S(1)}, u32[]{:S(2)}, u32[]{:S(2)}) collective-permute-start(bf16[32,768]{1,0:T(8,128)(2,1)S(1)} %pad_maximum_fusion.1), channel_id=1, source_target_pairs={{0,8},{2,10},{4,12},{6,14},{8,0},{10,2},{12,4},{14,6},{1,9},{3,11}... | collective-permute-start | bytes 147464 | tf_op jit(solution)/shard_map/ppermute | solution.py:636
  55.9 2.9 %collective-permute-done.8 = bf16[32,768]{1,0:T(8,128)(2,1)S(1)} collective-permute-done((bf16[32,768]{1,0:T(8,128)(2,1)S(1)}, bf16[32,768]{1,0:T(8,128)(2,1)S(1)}, u32[]{:S(2)}, u32[]{:S(2)}) %collective-permute-start.8) | collective-permute-done | bytes 49184 | tf_op jit(solution)/shard_map/ppermute | solution.py:636
  60.2 2.0 %contrast.1 = (f32[1,1]{1,0:T(1,128)}, f32[48,768]{1,0:T(8,128)}, f32[8,768]{1,0:T(8,128)S(1)}) custom-call(bf16[768,768]{1,0:T(8,128)(2,1)S(1)} %get-tuple-element.129.proj_ref, bf16[128,768]{1,0:T(8,128)(2,1)S(1)} %constant_dynamic-update-slice_fusion.gathered_ref, s32[64]{0:T(128)S(1)} %copy-done.5), custom_call_target="tpu_custom_call" | custom-call | flops 1 | bytes 1 | tf_op jit(solution)/shard_map/contrast/pallas_call | solution.py:616
  62.2 2.9 %feed_forward_back.2 = (bf16[256,768]{1,0:T(8,128)(2,1)S(1)}, bf16[256,768]{1,0:T(8,128)(2,1)}, f32[256,768]{1,0:T(8,128)}, f32[1,768]{1,0:T(1,128)S(1)}, bf16[2...) custom-call(bf16[1536,768]{1,0:T(8,128)(2,1)S(1)} %get-tuple-element.133.down_ref, ...), custom_call_target="tpu_custom_call" | custom-call | flops 1 | bytes 1 | tf_op jit(solution)/shard_map/feed_forward_back/pallas_call | solution.py:616
  65.6 4.5 %feed_forward_back.3 = (bf16[256,768]{1,0:T(8,128)(2,1)S(1)}, bf16[256,768]{1,0:T(8,128)(2,1)}, f32[256,768]{1,0:T(8,128)}, f32[1,768]{1,0:T(1,128)S(1)}, bf16[2...) custom-call(bf16[1536,768]{1,0:T(8,128)(2,1)S(1)} %get-tuple-element, ...), custom_call_target="tpu_custom_call" | custom-call | flops 1 | bytes 1 | tf_op jit(solution)/shard_map/feed_forward_back/pallas_call | solution.py:616
  71.2 5.2 %collective-permute-done.15.refs_8_ = bf16[256,768]{1,0:T(8,128)(2,1)S(1)} collective-permute-done((bf16[256,768]{1,0:T(8,128)(2,1)S(1)}, bf16[256,768]{1,0:T(8,128)(2,1)S(1)}, u32[]{:S(2)}, u32[]{:S(2)}) %collective-permute-start.15) | collective-permute-done | bytes 393248 | tf_op jit(solution)/shard_map/ppermute | solution.py:636
  76.8 4.6 %middle_back.2 = (f32[256,768]{1,0:T(8,128)}, bf16[256,768]{1,0:T(8,128)(2,1)}, bf16[256,384]{1,0:T(8,128)(2,1)S(1)}, f32[1,768]{1,0:T(1,128)S(1)}, bf16[384,384...) custom-call(bf16[256,768]{1,0:T(8,128)(2,1)} %get-tuple-element.165., ...), custom_call_target="tpu_custom_call" | custom-call | flops 1 | bytes 1 | tf_op jit(solution)/shard_map/middle_back/pallas_call | solution.py:616
  84.6 2.1 %collective-permute-done.10.refs_8_ = bf16[256,768]{1,0:T(8,128)(2,1)S(1)} collective-permute-done((bf16[256,768]{1,0:T(8,128)(2,1)S(1)}, bf16[256,768]{1,0:T(8,128)(2,1)S(1)}, u32[]{:S(2)}, u32[]{:S(2)}) %collective-permute-start.10) | collective-permute-done | bytes 393248 | tf_op jit(solution)/shard_map/ppermute | solution.py:636
  86.7 3.0 %middle_back.3 = (f32[256,768]{1,0:T(8,128)}, bf16[256,768]{1,0:T(8,128)(2,1)}, bf16[256,384]{1,0:T(8,128)(2,1)S(1)}, f32[1,768]{1,0:T(1,128)S(1)}, bf16[512,384...) custom-call(bf16[256,768]{1,0:T(8,128)(2,1)} %get-tuple-element.152., ...), custom_call_target="tpu_custom_call" | custom-call | flops 1 | bytes 1 | tf_op jit(solution)/shard_map/middle_back/pallas_call | solution.py:616
  89.7 7.0 %attention_back.1 = (bf16[512,1152]{1,0:T(8,128)(2,1)S(1)}, f32[32,6]{1,0:T(8,128)S(1)}, bf16[3,768,384]{2,1,0:T(8,128)(2,1)S(1)}, bf16[512,768]{1,0:T(8,128)(2,1)S(1)}) custom-call(bf16[768,384]{1,0:T(8,128)(2,1)} %wq_hbm.3, bf16[768,384]{1,0:T(8,128)(2,1)} %wk_hbm.3, bf16[768,384]{1,0:T(8,128)(2,1)} %wv_hbm.3, bf16[512,768]{1,0:T(8,128)(2,1)} %get-tuple-element.143.n1_hbm, ...), custom_call_target="tpu_custom_call" | custom-call | flops 1 | bytes 1 | tf_op jit(solution)/shard_map/attention_back/pallas_call | solution.py:616
  96.7 2.1 %value_output_weight.1 = (bf16[384,384]{1,0:T(8,128)(2,1)S(1)}, bf16[384,384]{1,0:T(8,128)(2,1)S(1)}, bf16[384,768]{1,0:T(8,128)(2,1)S(1)}) custom-call(bf16[512,384]{1,0:T(8,128)(2,1)} %get-tuple-element.203.refs_0_, bf16[256,768]{1,0:T(8,128)(2,1)} %get-tuple-element.204.refs_1_, bf16[256,768]{1,0:T(8,128)(2,1)} %get-tuple-element.205.refs_2_, ...), custom_call_target="tpu_custom_call" | custom-call | flops 1 | bytes 1 | tf_op jit(solution)/shard_map/value_output_weight/pallas_call | solution.py:616
  102.1 2.3 %project_back.1 = (bf16[256,768]{1,0:T(8,128)(2,1)S(1)}, bf16[256,768]{1,0:T(8,128)(2,1)S(1)}, bf16[512,768]{1,0:T(8,128)(2,1)}, f32[1,768]{1,0:T(1,128)S(1)}) custom-call(bf16[3,768,384]{2,1,0:T(8,128)(2,1)S(1)} %get-tuple-element.185.w_ref, bf16[512,768]{1,0:T(8,128)(2,1)S(1)} %get-tuple-element.130.tok_ref.refs_2_, ...), custom_call_target="tpu_custom_call" | custom-call | flops 1 | bytes 1 | tf_op jit(solution)/shard_map/project_back/pallas_call | solution.py:616
  109.8 5.0 %collective-permute-done.26.refs_0_ = bf16[192,1536]{1,0:T(8,128)(2,1)S(1)} collective-permute-done((bf16[192,1536]{1,0:T(8,128)(2,1)S(1)}, bf16[192,1536]{1,0:T(8,128)(2,1)S(1)}, u32[]{:S(2)}, u32[]{:S(2)}) %collective-permute-start.26) | collective-permute-done | bytes 589856 | tf_op jit(solution)/shard_map/ppermute | solution.py:636
  116.1 2.1 %collective-permute-done.20.refs_4_ = bf16[256,768]{1,0:T(8,128)(2,1)S(1)} collective-permute-done((bf16[256,768]{1,0:T(8,128)(2,1)S(1)}, bf16[256,768]{1,0:T(8,128)(2,1)S(1)}, u32[]{:S(2)}, u32[]{:S(2)}) %collective-permute-start.20) | collective-permute-done | bytes 393248 | tf_op jit(solution)/shard_map/ppermute | solution.py:636
  122.8 5.3 %collective-permute-done.33.refs_0_ = bf16[192,768]{1,0:T(8,128)(2,1)S(1)} collective-permute-done((bf16[192,768]{1,0:T(8,128)(2,1)S(1)}, bf16[192,768]{1,0:T(8,128)(2,1)S(1)}, u32[]{:S(2)}, u32[]{:S(2)}) %collective-permute-start.33) | collective-permute-done | bytes 294944 | tf_op jit(solution)/shard_map/ppermute | solution.py:636
  129.1 2.8 %collective-permute-start.37 = (bf16[48,1536]{1,0:T(8,128)(2,1)S(1)}, bf16[48,1536]{1,0:T(8,128)(2,1)S(1)}, u32[]{:S(2)}, u32[]{:S(2)}) collective-permute-start(bf16[48,1536]{1,0:T(8,128)(2,1)S(1)} %get-tuple-element.233), channel_id=1, source_target_pairs={{0,8},{2,10},{4,12},{6,14},{8,0},{10,2},{12,4},{14,6},{1,9},{3,11}... | collective-permute-start | bytes 442376 | tf_op jit(solution)/shard_map/ppermute | solution.py:636
  131.9 3.5 %last.1 = f32[512,768]{1,0:T(8,128)} custom-call(bf16[512,768]{1,0:T(8,128)(2,1)} %get-tuple-element.187.own_hbm, f32[256,768]{1,0:T(8,128)} %get-tuple-element.188.refs_0_, f32[256,768]{1,0:T(8,128)} %get-tuple-element.189.refs_1_, bf16[512,768]{1,0:T(8,128)(2,1)S(1)} %get-tuple-element.130.tok_ref.refs_2_, f32[768]{0:T(1024)S(1)} %copy-done.4, ...), custom_call_target="tpu_custom_call" | custom-call | flops 1 | bytes 1 | tf_op jit(solution)/shard_map/last/pallas_call | solution.py:616
  137.9 2.4 %collective-permute-start.35 = (bf16[48,768]{1,0:T(8,128)(2,1)S(1)}, bf16[48,768]{1,0:T(8,128)(2,1)S(1)}, u32[]{:S(2)}, u32[]{:S(2)}) collective-permute-start(bf16[48,768]{1,0:T(8,128)(2,1)S(1)} %get-tuple-element.229), channel_id=1, source_target_pairs={{0,8},{2,10},{4,12},{6,14},{8,0},{10,2},{12,4},{14,6},{1,9},{3,11}... | collective-permute-start | bytes 221192 | tf_op jit(solution)/shard_map/ppermute | solution.py:636
  141.1 4.5 %collective-permute-done.39 = bf16[48,1536]{1,0:T(8,128)(2,1)S(1)} collective-permute-done((bf16[48,1536]{1,0:T(8,128)(2,1)S(1)}, bf16[48,1536]{1,0:T(8,128)(2,1)S(1)}, u32[]{:S(2)}, u32[]{:S(2)}) %collective-permute-start.39) | collective-permute-done | bytes 147488 | tf_op jit(solution)/shard_map/ppermute | solution.py:636
  148.4 4.3 %collective-permute-done.31 = bf16[48,896]{1,0:T(8,128)(2,1)S(1)} collective-permute-done((bf16[48,896]{1,0:T(8,128)(2,1)S(1)}, bf16[48,896]{1,0:T(8,128)(2,1)S(1)}, u32[]{:S(2)}, u32[]{:S(2)}) %collective-permute-start.31) | collective-permute-done | bytes 86048 | tf_op jit(solution)/shard_map/ppermute | solution.py:636
  154.8 1.9 %collective-permute-done.32 = f32[48,1]{1,0:T(8,128)S(1)} collective-permute-done((f32[48,1]{1,0:T(8,128)S(1)}, f32[48,1]{1,0:T(8,128)S(1)}, u32[]{:S(2)}, u32[]{:S(2)}) %collective-permute-start.32) | collective-permute-done | bytes 224 | tf_op jit(solution)/shard_map/ppermute | solution.py:636
  (107 shorter events, 38.0 us)
Async XLA Ops:
  1.6 13.8 %collective-permute-start = (bf16[192,768]{1,0:T(8,128)(2,1)S(1)}, bf16[192,768]{1,0:T(8,128)(2,1)S(1)}, u32[]{:S(2)}, u32[]{:S(2)}) collective-permute-start(bf16[192,768]{1,0:T(8,128)(2,1)S(1)} %constant_dynamic-slice_fusion), channel_id=1, source_target_pairs={{0,1},{1,0},{2,3},{3,2},{4,5},{5,4},{6,7},{7,6},{8,9},{9,8},{10,11... | collective-permute-start | bytes 884744 | tf_op jit(solution)/shard_map/ppermute | solution.py:636
  15.5 7.8 %collective-permute-start.4 = (bf16[256,384]{1,0:T(8,128)(2,1)S(1)}, bf16[256,384]{1,0:T(8,128)(2,1)S(1)}, u32[]{:S(2)}, u32[]{:S(2)}) collective-permute-start(bf16[256,384]{1,0:T(8,128)(2,1)S(1)} %get-tuple-element.137.mix_own), channel_id=1, source_target_pairs={{0,1},{1,0},{2,3},{3,2},{4,5},{5,4},{6,7},{7,6},{8,9},{9,8},{10,11... | collective-permute-start | bytes 589832 | tf_op jit(solution)/shard_map/ppermute | solution.py:636
  15.6 11.4 %collective-permute-start.2 = (bf16[256,384]{1,0:T(8,128)(2,1)S(1)}, bf16[256,384]{1,0:T(8,128)(2,1)S(1)}, u32[]{:S(2)}, u32[]{:S(2)}) collective-permute-start(bf16[256,384]{1,0:T(8,128)(2,1)S(1)} %get-tuple-element.126.mix_own), channel_id=1, source_target_pairs={{0,1},{1,0},{2,3},{3,2},{4,5},{5,4},{6,7},{7,6},{8,9},{9,8},{10,11... | collective-permute-start | bytes 589832 | tf_op jit(solution)/shard_map/ppermute | solution.py:636
  26.6 12.1 %collective-permute-start.5 = (bf16[256,768]{1,0:T(8,128)(2,1)S(1)}, bf16[256,768]{1,0:T(8,128)(2,1)S(1)}, u32[]{:S(2)}, u32[]{:S(2)}) collective-permute-start(bf16[256,768]{1,0:T(8,128)(2,1)S(1)} %get-tuple-element.139.own_ref), channel_id=1, source_target_pairs={{0,1},{1,0},{2,3},{3,2},{4,5},{5,4},{6,7},{7,6},{8,9},{9,8},{10,11... | collective-permute-start | bytes 1179656 | tf_op jit(solution)/shard_map/ppermute | solution.py:636
  30.3 15.0 %collective-permute-start.3 = (bf16[256,768]{1,0:T(8,128)(2,1)S(1)}, bf16[256,768]{1,0:T(8,128)(2,1)S(1)}, u32[]{:S(2)}, u32[]{:S(2)}) collective-permute-start(bf16[256,768]{1,0:T(8,128)(2,1)S(1)} %get-tuple-element.135.own_ref), channel_id=1, source_target_pairs={{0,1},{1,0},{2,3},{3,2},{4,5},{5,4},{6,7},{7,6},{8,9},{9,8},{10,11... | collective-permute-start | bytes 1179656 | tf_op jit(solution)/shard_map/ppermute | solution.py:636
  45.7 3.8 %collective-permute-start.6 = (bf16[8,768]{1,0:T(8,128)(2,1)S(1)}, bf16[8,768]{1,0:T(8,128)(2,1)S(1)}, u32[]{:S(2)}, u32[]{:S(2)}) collective-permute-start(bf16[8,768]{1,0:T(8,128)(2,1)S(1)} %get-tuple-element.141), channel_id=1, source_target_pairs={{0,2},{2,0},{4,6},{6,4},{8,10},{10,8},{12,14},{14,12},{1,3},{3,1},... | collective-permute-start | bytes 36872 | tf_op jit(solution)/shard_map/ppermute | solution.py:636
  49.5 4.4 %collective-permute-start.7 = (bf16[16,768]{1,0:T(8,128)(2,1)S(1)}, bf16[16,768]{1,0:T(8,128)(2,1)S(1)}, u32[]{:S(2)}, u32[]{:S(2)}) collective-permute-start(bf16[16,768]{1,0:T(8,128)(2,1)S(1)} %pad_maximum_fusion.2), channel_id=1, source_target_pairs={{0,4},{2,6},{4,0},{6,2},{8,12},{10,14},{12,8},{14,10},{1,5},{3,7},... | collective-permute-start | bytes 73736 | tf_op jit(solution)/shard_map/ppermute | solution.py:636
  53.8 5.0 %collective-permute-start.8 = (bf16[32,768]{1,0:T(8,128)(2,1)S(1)}, bf16[32,768]{1,0:T(8,128)(2,1)S(1)}, u32[]{:S(2)}, u32[]{:S(2)}) collective-permute-start(bf16[32,768]{1,0:T(8,128)(2,1)S(1)} %pad_maximum_fusion.1), channel_id=1, source_target_pairs={{0,8},{2,10},{4,12},{6,14},{8,0},{10,2},{12,4},{14,6},{1,9},{3,11}... | collective-permute-start | bytes 147464 | tf_op jit(solution)/shard_map/ppermute | solution.py:636
  65.1 11.2 %collective-permute-start.15 = (bf16[256,768]{1,0:T(8,128)(2,1)S(1)}, bf16[256,768]{1,0:T(8,128)(2,1)S(1)}, u32[]{:S(2)}, u32[]{:S(2)}) collective-permute-start(bf16[256,768]{1,0:T(8,128)(2,1)S(1)} %get-tuple-element.171), channel_id=1, source_target_pairs={{0,1},{1,0},{2,3},{3,2},{4,5},{5,4},{6,7},{7,6},{8,9},{9,8},{10,11... | collective-permute-start | bytes 1179656 | tf_op jit(solution)/shard_map/ppermute | solution.py:636
  70.1 11.3 %collective-permute-start.11 = (bf16[384,384]{1,0:T(8,128)(2,1)S(1)}, bf16[384,384]{1,0:T(8,128)(2,1)S(1)}, u32[]{:S(2)}, u32[]{:S(2)}) collective-permute-start(bf16[384,384]{1,0:T(8,128)(2,1)S(1)} %get-tuple-element.160), channel_id=1, source_target_pairs={{0,16},{16,0},{1,17},{17,1},{2,18},{18,2},{3,19},{19,3},{4,20},{20... | collective-permute-start | bytes 884744 | tf_op jit(solution)/shard_map/ppermute | solution.py:636
  70.2 11.3 %collective-permute-start.12 = (bf16[384,384]{1,0:T(8,128)(2,1)S(1)}, bf16[384,384]{1,0:T(8,128)(2,1)S(1)}, u32[]{:S(2)}, u32[]{:S(2)}) collective-permute-start(bf16[384,384]{1,0:T(8,128)(2,1)S(1)} %get-tuple-element.161), channel_id=1, source_target_pairs={{0,16},{16,0},{1,17},{17,1},{2,18},{18,2},{3,19},{19,3},{4,20},{20... | collective-permute-start | bytes 884744 | tf_op jit(solution)/shard_map/ppermute | solution.py:636
  70.7 11.3 %collective-permute-start.13 = (bf16[384,384]{1,0:T(8,128)(2,1)S(1)}, bf16[384,384]{1,0:T(8,128)(2,1)S(1)}, u32[]{:S(2)}, u32[]{:S(2)}) collective-permute-start(bf16[384,384]{1,0:T(8,128)(2,1)S(1)} %get-tuple-element.162), channel_id=1, source_target_pairs={{0,16},{16,0},{1,17},{17,1},{2,18},{18,2},{3,19},{19,3},{4,20},{20... | collective-permute-start | bytes 884744 | tf_op jit(solution)/shard_map/ppermute | solution.py:636
  70.7 11.3 %collective-permute-start.14 = (bf16[384,384]{1,0:T(8,128)(2,1)S(1)}, bf16[384,384]{1,0:T(8,128)(2,1)S(1)}, u32[]{:S(2)}, u32[]{:S(2)}) collective-permute-start(bf16[384,384]{1,0:T(8,128)(2,1)S(1)} %get-tuple-element.163), channel_id=1, source_target_pairs={{0,16},{16,0},{1,17},{17,1},{2,18},{18,2},{3,19},{19,3},{4,20},{20... | collective-permute-start | bytes 884744 | tf_op jit(solution)/shard_map/ppermute | solution.py:636
  76.3 10.3 %collective-permute-start.10 = (bf16[256,768]{1,0:T(8,128)(2,1)S(1)}, bf16[256,768]{1,0:T(8,128)(2,1)S(1)}, u32[]{:S(2)}, u32[]{:S(2)}) collective-permute-start(bf16[256,768]{1,0:T(8,128)(2,1)S(1)} %get-tuple-element.158), channel_id=1, source_target_pairs={{0,1},{1,0},{2,3},{3,2},{4,5},{5,4},{6,7},{7,6},{8,9},{9,8},{10,11... | collective-permute-start | bytes 1179656 | tf_op jit(solution)/shard_map/ppermute | solution.py:636
  82.1 2.2 %collective-permute-start.19 = (bf16[384,384]{1,0:T(8,128)(2,1)S(1)}, bf16[384,384]{1,0:T(8,128)(2,1)S(1)}, u32[]{:S(2)}, u32[]{:S(2)}) collective-permute-start(bf16[384,384]{1,0:T(8,128)(2,1)S(1)} %get-tuple-element.176), channel_id=1, source_target_pairs={{0,16},{16,0},{1,17},{17,1},{2,18},{18,2},{3,19},{19,3},{4,20},{20... | collective-permute-start | bytes 884744 | tf_op jit(solution)/shard_map/ppermute | solution.py:636
  98.8 8.7 %collective-permute-start.24 = (bf16[384,384]{1,0:T(8,128)(2,1)S(1)}, bf16[384,384]{1,0:T(8,128)(2,1)S(1)}, u32[]{:S(2)}, u32[]{:S(2)}) collective-permute-start(bf16[384,384]{1,0:T(8,128)(2,1)S(1)} %get-tuple-element.207), channel_id=1, source_target_pairs={{0,16},{16,0},{1,17},{17,1},{2,18},{18,2},{3,19},{19,3},{4,20},{20... | collective-permute-start | bytes 884744 | tf_op jit(solution)/shard_map/ppermute | solution.py:636
  98.9 8.7 %collective-permute-start.25 = (bf16[384,384]{1,0:T(8,128)(2,1)S(1)}, bf16[384,384]{1,0:T(8,128)(2,1)S(1)}, u32[]{:S(2)}, u32[]{:S(2)}) collective-permute-start(bf16[384,384]{1,0:T(8,128)(2,1)S(1)} %get-tuple-element.208), channel_id=1, source_target_pairs={{0,16},{16,0},{1,17},{17,1},{2,18},{18,2},{3,19},{19,3},{4,20},{20... | collective-permute-start | bytes 884744 | tf_op jit(solution)/shard_map/ppermute | solution.py:636
  99.4 15.3 %collective-permute-start.26 = (bf16[192,1536]{1,0:T(8,128)(2,1)S(1)}, bf16[192,1536]{1,0:T(8,128)(2,1)S(1)}, u32[]{:S(2)}, u32[]{:S(2)}) collective-permute-start(bf16[192,1536]{1,0:T(8,128)(2,1)S(1)} %get-tuple-element.211), channel_id=1, source_target_pairs={{0,2},{2,0},{4,6},{6,4},{8,10},{10,8},{12,14},{14,12},{1,3},{3,1},... | collective-permute-start | bytes 1769480 | tf_op jit(solution)/shard_map/ppermute | solution.py:636
  100.9 15.0 %collective-permute-start.27 = (bf16[192,1536]{1,0:T(8,128)(2,1)S(1)}, bf16[192,1536]{1,0:T(8,128)(2,1)S(1)}, u32[]{:S(2)}, u32[]{:S(2)}) collective-permute-start(bf16[192,1536]{1,0:T(8,128)(2,1)S(1)} %get-tuple-element.214), channel_id=1, source_target_pairs={{0,4},{2,6},{4,0},{6,2},{8,12},{10,14},{12,8},{14,10},{1,5},{3,7},... | collective-permute-start | bytes 1769480 | tf_op jit(solution)/shard_map/ppermute | solution.py:636
  107.0 11.2 %collective-permute-start.20 = (bf16[256,768]{1,0:T(8,128)(2,1)S(1)}, bf16[256,768]{1,0:T(8,128)(2,1)S(1)}, u32[]{:S(2)}, u32[]{:S(2)}) collective-permute-start(bf16[256,768]{1,0:T(8,128)(2,1)S(1)} %get-tuple-element.190), channel_id=1, source_target_pairs={{0,1},{1,0},{2,3},{3,2},{4,5},{5,4},{6,7},{7,6},{8,9},{9,8},{10,11... | collective-permute-start | bytes 1179656 | tf_op jit(solution)/shard_map/ppermute | solution.py:636
  118.2 9.9 %collective-permute-start.33 = (bf16[192,768]{1,0:T(8,128)(2,1)S(1)}, bf16[192,768]{1,0:T(8,128)(2,1)S(1)}, u32[]{:S(2)}, u32[]{:S(2)}) collective-permute-start(bf16[192,768]{1,0:T(8,128)(2,1)S(1)} %get-tuple-element.225), channel_id=1, source_target_pairs={{0,4},{2,6},{4,0},{6,2},{8,12},{10,14},{12,8},{14,10},{1,5},{3,7},... | collective-permute-start | bytes 884744 | tf_op jit(solution)/shard_map/ppermute | solution.py:636
  119.1 9.9 %collective-permute-start.36 = (bf16[96,1536]{1,0:T(8,128)(2,1)S(1)}, bf16[96,1536]{1,0:T(8,128)(2,1)S(1)}, u32[]{:S(2)}, u32[]{:S(2)}) collective-permute-start(bf16[96,1536]{1,0:T(8,128)(2,1)S(1)} %get-tuple-element.231), channel_id=1, source_target_pairs={{0,2},{2,0},{4,6},{6,4},{8,10},{10,8},{12,14},{14,12},{1,3},{3,1},... | collective-permute-start | bytes 884744 | tf_op jit(solution)/shard_map/ppermute | solution.py:636
  119.6 12.3 %collective-permute-start.28 = (bf16[256,768]{1,0:T(8,128)(2,1)S(1)}, bf16[256,768]{1,0:T(8,128)(2,1)S(1)}, u32[]{:S(2)}, u32[]{:S(2)}) collective-permute-start(bf16[256,768]{1,0:T(8,128)(2,1)S(1)} %get-tuple-element.217), channel_id=1, source_target_pairs={{0,1},{1,0},{2,3},{3,2},{4,5},{5,4},{6,7},{7,6},{8,9},{9,8},{10,11... | collective-permute-start | bytes 1179656 | tf_op jit(solution)/shard_map/ppermute | solution.py:636
  120.1 17.4 %collective-permute-start.29 = (bf16[192,896]{1,0:T(8,128)(2,1)S(1)}, bf16[192,896]{1,0:T(8,128)(2,1)S(1)}, u32[]{:S(2)}, u32[]{:S(2)}) collective-permute-start(bf16[192,896]{1,0:T(8,128)(2,1)S(1)} %get-tuple-element.219), channel_id=1, source_target_pairs={{0,2},{2,0},{4,6},{6,4},{8,10},{10,8},{12,14},{14,12},{1,3},{3,1},... | collective-permute-start | bytes 1032200 | tf_op jit(solution)/shard_map/ppermute | solution.py:636
  121.6 13.8 %collective-permute-start.38 = (bf16[96,1536]{1,0:T(8,128)(2,1)S(1)}, bf16[96,1536]{1,0:T(8,128)(2,1)S(1)}, u32[]{:S(2)}, u32[]{:S(2)}) collective-permute-start(bf16[96,1536]{1,0:T(8,128)(2,1)S(1)} %get-tuple-element.235), channel_id=1, source_target_pairs={{0,4},{2,6},{4,0},{6,2},{8,12},{10,14},{12,8},{14,10},{1,5},{3,7},... | collective-permute-start | bytes 884744 | tf_op jit(solution)/shard_map/ppermute | solution.py:636
  128.2 9.6 %collective-permute-start.34 = (bf16[96,768]{1,0:T(8,128)(2,1)S(1)}, bf16[96,768]{1,0:T(8,128)(2,1)S(1)}, u32[]{:S(2)}, u32[]{:S(2)}) collective-permute-start(bf16[96,768]{1,0:T(8,128)(2,1)S(1)} %get-tuple-element.227), channel_id=1, source_target_pairs={{0,2},{2,0},{4,6},{6,4},{8,10},{10,8},{12,14},{14,12},{1,3},{3,1},... | collective-permute-start | bytes 442376 | tf_op jit(solution)/shard_map/ppermute | solution.py:636
  129.1 11.2 %collective-permute-start.37 = (bf16[48,1536]{1,0:T(8,128)(2,1)S(1)}, bf16[48,1536]{1,0:T(8,128)(2,1)S(1)}, u32[]{:S(2)}, u32[]{:S(2)}) collective-permute-start(bf16[48,1536]{1,0:T(8,128)(2,1)S(1)} %get-tuple-element.233), channel_id=1, source_target_pairs={{0,8},{2,10},{4,12},{6,14},{8,0},{10,2},{12,4},{14,6},{1,9},{3,11}... | collective-permute-start | bytes 442376 | tf_op jit(solution)/shard_map/ppermute | solution.py:636
  135.6 10.1 %collective-permute-start.39 = (bf16[48,1536]{1,0:T(8,128)(2,1)S(1)}, bf16[48,1536]{1,0:T(8,128)(2,1)S(1)}, u32[]{:S(2)}, u32[]{:S(2)}) collective-permute-start(bf16[48,1536]{1,0:T(8,128)(2,1)S(1)} %get-tuple-element.237), channel_id=1, source_target_pairs={{0,8},{2,10},{4,12},{6,14},{8,0},{10,2},{12,4},{14,6},{1,9},{3,11}... | collective-permute-start | bytes 442376 | tf_op jit(solution)/shard_map/ppermute | solution.py:636
  137.5 8.9 %collective-permute-start.30 = (bf16[96,896]{1,0:T(8,128)(2,1)S(1)}, bf16[96,896]{1,0:T(8,128)(2,1)S(1)}, u32[]{:S(2)}, u32[]{:S(2)}) collective-permute-start(bf16[96,896]{1,0:T(8,128)(2,1)S(1)} %get-tuple-element.221), channel_id=1, source_target_pairs={{0,4},{2,6},{4,0},{6,2},{8,12},{10,14},{12,8},{14,10},{1,5},{3,7},... | collective-permute-start | bytes 516104 | tf_op jit(solution)/shard_map/ppermute | solution.py:636
  137.9 9.9 %collective-permute-start.35 = (bf16[48,768]{1,0:T(8,128)(2,1)S(1)}, bf16[48,768]{1,0:T(8,128)(2,1)S(1)}, u32[]{:S(2)}, u32[]{:S(2)}) collective-permute-start(bf16[48,768]{1,0:T(8,128)(2,1)S(1)} %get-tuple-element.229), channel_id=1, source_target_pairs={{0,8},{2,10},{4,12},{6,14},{8,0},{10,2},{12,4},{14,6},{1,9},{3,11}... | collective-permute-start | bytes 221192 | tf_op jit(solution)/shard_map/ppermute | solution.py:636
  146.4 6.4 %collective-permute-start.31 = (bf16[48,896]{1,0:T(8,128)(2,1)S(1)}, bf16[48,896]{1,0:T(8,128)(2,1)S(1)}, u32[]{:S(2)}, u32[]{:S(2)}) collective-permute-start(bf16[48,896]{1,0:T(8,128)(2,1)S(1)} %get-tuple-element.223), channel_id=1, source_target_pairs={{0,8},{2,10},{4,12},{6,14},{8,0},{10,2},{12,4},{14,6},{1,9},{3,11}... | collective-permute-start | bytes 258056 | tf_op jit(solution)/shard_map/ppermute | solution.py:636
  152.8 3.9 %collective-permute-start.32 = (f32[48,1]{1,0:T(8,128)S(1)}, f32[48,1]{1,0:T(8,128)S(1)}, u32[]{:S(2)}, u32[]{:S(2)}) collective-permute-start(f32[48,1]{1,0:T(8,128)S(1)} %slice.40), channel_id=1, source_target_pairs={{0,1},{1,0},{2,3},{3,2},{4,5},{5,4},{6,7},{7,6},{8,9},{9,8},{10,11... | collective-permute-start | bytes 584 | tf_op jit(solution)/shard_map/ppermute | solution.py:636
  (14 other events, 87.8 us)

commit v2 on v1

--- a/solution.py
+++ b/solution.py
@@ -10,8 +10,9 @@
 SEGS_ROW = 8
 BLOCK = 128
 STRIP = 32
-PIECE = 384
+STEP = 384
 LANES = 128
+FF_SENDS, QK_SENDS, VO_SENDS = 4, 2, 2
 CHUNKS = 2
 
 eps = 1e-06
@@ -304,30 +305,24 @@
     own_ref[...] = dot_nt(dot_nn(mine, de).astype(bf16), proj_ref[...])
 
 
-def ff_back_kernel(
-    chunk, down_ref, up_ref, h2_ref, slope_ref, *rest
-):
-    last = chunk == CHUNKS - 1
-    count = 3 + (2 * CHUNKS - 1 if last else 0)
-    given, outs = rest[:count], rest[count:]
-    dpool_ref, seg_ref, gain_ref = given[-3:]
-    part_ref, part_hbm, dh2_hbm, dgain_ref, du_ref = outs[:5]
-    dh2_ref, sems = outs[-2:]
-    df_ref = outs[-3] if last else outs[5]
-    size, width = h2_ref.shape
+def ff_back_kernel(down_ref, up_ref, *refs):
+    h2_refs, slope_refs, refs = refs[:CHUNKS], refs[CHUNKS : 2 * CHUNKS], refs[2 * CHUNKS :]
+    dpool_ref, seg_ref, gain_ref, part_ref, dh2_ref, df_ref, du_ref, dgain_ref = refs
+    length, width = dh2_ref.shape
+    size = length // CHUNKS
     hidden = down_ref.shape[0]
     step = 256
     gain = row_gain(gain_ref)
     number = lax.broadcasted_iota(jnp.int32, (SEGS_ROW, 1), 0)
     counts = jnp.sum((seg_ref[...] == number).astype(f32), -1, keepdims=True)
     pieces = jnp.concatenate([p.astype(f32) for p in split_low(dpool_ref[...] / counts, 4)], 0).astype(bf16)
-    member = (seg_ref[:, chunk * size : (chunk + 1) * size] == number).astype(f32)
+    member = (seg_ref[...] == number).astype(f32)
     member = jnp.concatenate([member] * 4, 0).astype(bf16)
     dh2_ref[...] = dot_tn(member, pieces)
     dgain = jnp.zeros((1, width), f32)
-    for at in range(0, size, STRIP):
+    for at in range(0, length, STRIP):
         rows = slice(at, at + STRIP)
-        h2 = h2_ref[rows, :]
+        h2 = h2_refs[at // size][at % size : at % size + STRIP, :]
         grad = dh2_ref[rows, :]
         inv = inv_rms(h2)
         dh2 = norm_back(h2, inv, gain, grad)
@@ -338,44 +333,37 @@
     df = df_ref[...]
     for at in range(0, hidden, step):
         cols = slice(at, at + step)
-        du_ref[:, cols] = (dot_nt(df, down_ref[cols, :]) * slope_ref[:, cols]).astype(bf16)
+        da = dot_nt(df, down_ref[cols, :])
+        for c in range(CHUNKS):
+            rows = slice(c * size, (c + 1) * size)
+            du_ref[rows, cols] = (da[rows, :] * slope_refs[c][:, cols]).astype(bf16)
     part_ref[...] = dot_nt(du_ref[...], up_ref[...]).astype(bf16)
-    copies = start_copies(sems, (dh2_ref, dh2_hbm), (part_ref, part_hbm))
-    if last:
-        weight_products([*given[CHUNKS:-3], df_ref], given[:CHUNKS], outs[5:-4], outs[-4])
-    for copy in copies:
-        copy.wait()
-
-
-def middle_back_kernel(chunk, *refs):
-    first, last = chunk == 0, chunk == CHUNKS - 1
-    refs = list(refs)
-
-    def take(count):
-        taken = refs[:count]
-        del refs[:count]
-        return taken
-
-    own_hbm, dh2_hbm = take(2)
-    ahead = take(4) if last else []
-    wo_ref, h1_ref = take(2)
-    lefts, rights = (take(CHUNKS), take(CHUNKS)) if first else ([], [])
-    rec_ref, gain_ref = take(2)
-    dh1_hbm, da_hbm, dmix_ref, dgain_ref = take(4)
-    held = take(4) if last else []
-    halves = take(len(refs) - 6) if first else []
-    own_ref, dh2_ref, dh1_ref, da_ref, sems, out_sems = refs
-    copies = start_copies(sems, (own_hbm, own_ref), (dh2_hbm, dh2_ref), *zip(ahead, held))
-    if first:
-        weight_products(lefts, rights, halves[:-1], halves[-1])
-    for copy in copies[:2]:
-        copy.wait()
-    size, width = h1_ref.shape
+
+
+def down_weight_kernel(df_ref, *refs):
+    size = refs[0].shape[0]
+    weight_products([df_ref.at[c * size : (c + 1) * size, :] for c in range(CHUNKS)], refs[:CHUNKS], refs[CHUNKS:-1], refs[-1])
+
+
+def up_weight_kernel(du_ref, *refs):
+    size = refs[0].shape[0]
+    weight_products(refs[:CHUNKS], [du_ref.at[c * size : (c + 1) * size, :] for c in range(CHUNKS)], refs[CHUNKS:-1], refs[-1])
+
+
+def middle_back_kernel(*refs):
+    ahead, refs = refs[:4], refs[4:]
+    wo_ref, own_ref, dh2_ref, *refs = refs
+    h1_refs, refs = refs[:CHUNKS], refs[CHUNKS:]
+    rec_ref, gain_ref, dh1_hbm, da_hbm, dmix_ref, dgain_ref, *refs = refs
+    held, (dh1_ref, da_ref, sems, out_sems) = refs[:4], refs[4:]
+    copies = start_copies(sems, *zip(ahead, held))
+    length, width = dh1_ref.shape
+    size = length // CHUNKS
     gain = row_gain(gain_ref)
     dgain = jnp.zeros((1, width), f32)
-    for at in range(0, size, STRIP):
+    for at in range(0, length, STRIP):
         rows = slice(at, at + STRIP)
-        h1 = h1_ref[rows, :]
+        h1 = h1_refs[at // size][at % size : at % size + STRIP, :]
         grad = own_ref[rows, :].astype(f32) + rec_ref[rows, :].astype(f32)
         inv = inv_rms(h1)
         dh1 = dh2_ref[rows, :] + norm_back(h1, inv, gain, grad)
@@ -383,17 +371,17 @@
         dh1_ref[rows, :] = dh1
         da_ref[rows, :] = dh1.astype(bf16)
     dgain_ref[...] = dgain
-    outs = start_copies(out_sems, (dh1_ref, dh1_hbm), (da_ref, da_hbm))
+    copies += start_copies(out_sems, (dh1_ref, dh1_hbm), (da_ref, da_hbm))
     inner = dmix_ref.shape[1]
     own_at = pl.multiple_of(lax.axis_index("mp") * inner, inner)
     dmix_ref[...] = dot_nt(da_ref[...], wo_ref[pl.ds(own_at, inner), :]).astype(bf16)
-    for copy in copies[2:] + outs:
+    for copy in copies:
         copy.wait()
 
 
 def attend_back_kernel(wq_hbm, wk_hbm, wv_hbm, n1_hbm, q_ref, k_ref, v_ref, probs_ref, *rest):
-    mixg_refs = rest[:CHUNKS]
-    ids_ref, grads_ref, biasg_ref, w_ref, n1_ref, ds_ref, skew_ref, rel_ref, dp_ref, mixg_ref, sems = rest[CHUNKS:]
+    mixg_ref, ids_ref, grads_ref, biasg_ref, n1_ref, w_ref, *halves = rest[:-5]
+    ds_ref, skew_ref, rel_ref, dp_ref, sems = rest[-5:]
     length, inner = q_ref.shape
     blocks = length // BLOCK
     pairs = inner // BLOCK
@@ -405,8 +393,6 @@
     low_all = lax.broadcasted_iota(jnp.int32, (length, BLOCK), 1) < BLOCK // 2
     zero = jnp.zeros((BLOCK, BLOCK), bf16)
     rel_ref[...] = jnp.zeros_like(rel_ref)
-    for i, part in enumerate(mixg_refs):
-        mixg_ref[i * part.shape[0] : (i + 1) * part.shape[0], :] = part[...]
 
     @pl.loop(0, pairs)
     def _(pair):
@@ -472,77 +458,74 @@
     biasg_ref[...] = total[:, : biasg_ref.shape[1]]
     for copy in later:
         copy.wait()
-
-
-def project_back_kernel(w_ref, tok_ref, grads_ref, *refs):
-    part_refs, (part_hbm, dgain_ref, part_ref, sems) = refs[:CHUNKS], refs[CHUNKS:]
+    weight_products([n1_ref], [grads_ref.at[:, : 2 * inner]], halves[:-1], halves[-1])
+
+
+def project_back_kernel(shard, *refs):
+    mix_hbm, da_hbm, w_ref, tok_ref, n1_ref, grads_ref, bias_ref, ff_gain, final_gain, part_ref, part_hbm, *refs = refs
+    *others, small_ref, own_ref, all_ref, mix_ref, da_ref, sems = refs
+    copies = start_copies(sems, (mix_hbm, mix_ref), (da_hbm, da_ref))
     length, width = part_ref.shape
     inner = w_ref.shape[2]
-    size = length // CHUNKS
-    for c in range(CHUNKS):
-        rows = slice(c * size, (c + 1) * size)
-        part = (
-            dot_nt(grads_ref[rows, :inner], w_ref[0])
-            + dot_nt(grads_ref[rows, inner : 2 * inner], w_ref[1])
-            + dot_nt(grads_ref[rows, 2 * inner :], w_ref[2])
-        ).astype(bf16)
-        part_ref[rows, :] = part
-        part_refs[c][...] = part
-    (copy,) = start_copies(sems, (part_ref, part_hbm))
+    part_ref[...] = (
+        dot_nt(grads_ref[:, :inner], w_ref[0])
+        + dot_nt(grads_ref[:, inner : 2 * inner], w_ref[1])
+        + dot_nt(grads_ref[:, 2 * inner :], w_ref[2])
+    ).astype(bf16)
+    copies += start_copies(sems.at[2:], (part_ref, part_hbm))
     dgain = jnp.zeros((1, width), f32)
     for at in range(0, length, STRIP):
         rows = slice(at, at + STRIP)
         x = tok_ref[rows, :].astype(f32)
         dgain += jnp.sum(x * inv_rms(x) * part_ref[rows, :].astype(f32), 0, keepdims=True)
-    dgain_ref[...] = dgain
-    copy.wait()
-
-
-def last_kernel(own_hbm, *refs):
-    stored_refs, (tok_ref, gain_ref), received = refs[:CHUNKS], refs[CHUNKS : CHUNKS + 2], refs[CHUNKS + 2 : 2 * CHUNKS + 2]
-    out_ref, own_ref, dh1_ref, sems = refs[-4:]
-    size = own_ref.shape[0] // CHUNKS
-    copies = start_copies(
-        sems, (own_hbm, own_ref), *[(stored_refs[c], dh1_ref.at[pl.ds(c * size, size), :]) for c in range(CHUNKS)]
-    )
+    weight_products([n1_ref], [grads_ref.at[:, 2 * inner :]], others, own_ref)
+    small_columns(shard, bias_ref, [dgain, ff_gain[...], final_gain[...]], all_ref)
+    tower_index = lax.axis_index("tower")
+    half = small_ref.shape[0]
+    small_ref[...] = all_ref[pl.ds(pl.multiple_of((1 - tower_index) * half, half), half), :].astype(bf16)
+    own_ref[:, 2 * inner :] = all_ref[pl.ds(pl.multiple_of(tower_index * half, half), half), :].astype(bf16)
+    for copy in copies:
+        copy.wait()
+    weight_products([da_ref], [mix_ref], others, own_ref, inner)
+
+
+def last_kernel(own_hbm, dh1_hbm, tok_ref, gain_ref, rec_ref, out_ref, own_ref, dh1_ref, sems):
+    copies = start_copies(sems, (own_hbm, own_ref), (dh1_hbm, dh1_ref))
     gain = row_gain(gain_ref)
     for copy in copies:
         copy.wait()
-    for at in range(0, CHUNKS * size, STRIP):
+    for at in range(0, own_ref.shape[0], STRIP):
         rows = slice(at, at + STRIP)
-        there = slice(at % size, at % size + STRIP)
         x = tok_ref[rows, :].astype(f32)
-        grad = own_ref[rows, :].astype(f32) + received[at // size][there, :].astype(f32)
+        grad = own_ref[rows, :].astype(f32) + rec_ref[rows, :].astype(f32)
         out_ref[rows, :] = dh1_ref[rows, :] + norm_back(x, inv_rms(x), gain, grad)
 
 
 def weight_products(lefts, rights, other_refs, own_ref, columns=0):
     tower_index = lax.axis_index("tower")
     half = lefts[0].shape[1] // 2
+    each = other_refs[0].shape[1]
     for which in (1 - tower_index, tower_index):
-        is_own = which is tower_index
         lanes = pl.ds(pl.multiple_of(which * half, half), half)
         turned = [left[:, lanes].T for left in lefts]
-        for at in range(0, rights[0].shape[1], PIECE):
+        for at in range(0, rights[0].shape[1], STEP):
             total = None
             for left, right in zip(turned, rights):
-                term = dot_nn(left, right[:, at : at + PIECE])
+                term = dot_nn(left, right[:, at : at + STEP])
                 total = term if total is None else total + term
+            total = total.astype(bf16)
             there = columns + at
-            if is_own:
-                own_ref[:, there : there + PIECE] = total.astype(bf16)
-            else:
-                other_refs[there // PIECE][...] = total.astype(bf16)
-
-
-def query_key_kernel(shard, n1_ref, grads_ref, bias_ref, *refs):
-    inner = grads_ref.shape[1] // 3
-    count = 2 * inner // PIECE + 3
-    parts, outs, all_ref = refs[:-count], refs[-count:-1], refs[-1]
-    own_ref = outs[-1]
-    tower_index = lax.axis_index("tower")
+            if which is tower_index:
+                own_ref[:, there : there + STEP] = total
+                continue
+            for i, other_ref in enumerate(other_refs):
+                begin, end = max(there, i * each), min(there + STEP, (i + 1) * each)
+                if begin < end:
+                    other_ref[:, begin - i * each : end - i * each] = total[:, begin - there : end - there]
+
+
+def small_columns(shard, bias_ref, lines, all_ref):
     width = all_ref.shape[0]
-    half = width // 2
     buckets, heads = bias_ref.shape
     lane = lax.broadcasted_iota(jnp.int32, (1, LANES), 1)
 
@@ -555,44 +538,59 @@
     for g in range(-(-buckets // shard)):
         place = lax.broadcasted_iota(jnp.int32, (heads, LANES), 0) + 3 + g * heads == lane
         total += dot_nn(low(col == row + g * shard), low(dot_nn(low(bias_ref[...]), low(place))))
-    lines = [
-        sum(part[...] for part in some) for some in (parts[:1], parts[1 : 1 + CHUNKS], parts[1 + CHUNKS :])
-    ]
     place = lax.broadcasted_iota(jnp.int32, (3, LANES), 0) == lane
     all_ref[...] = total + dot_tn(low(jnp.concatenate(lines, 0)), low(place))
-    outs[-2][...] = all_ref[pl.ds(pl.multiple_of((1 - tower_index) * half, half), half), :].astype(bf16)
-    own_ref[:, 2 * inner :] = all_ref[pl.ds(pl.multiple_of(tower_index * half, half), half), :].astype(bf16)
-    weight_products([n1_ref], [grads_ref.at[:, : 2 * inner]], outs[:-2], own_ref)
-
-
-def value_output_kernel(*refs):
-    stored_refs = refs[: CHUNKS + 1]
-    n1_ref, grads_ref, *outs = refs[CHUNKS + 1 : -2 - CHUNKS]
-    mix_ref, *da_refs = refs[-2 - CHUNKS : -1]
-    copies = start_copies(refs[-1], *zip(stored_refs, (mix_ref, *da_refs)))
-    inner = grads_ref.shape[1] // 3
-    weight_products([n1_ref], [grads_ref.at[:, 2 * inner :]], outs[:-1], outs[-1])
-    for copy in copies:
-        copy.wait()
-    size = da_refs[0].shape[0]
-    pieces = [mix_ref.at[c * size : (c + 1) * size, :] for c in range(CHUNKS)]
-    weight_products(da_refs, pieces, outs[:-1], outs[-1], inner)
-
-
-def split_kernel(shard, bit, low, own_ref, *refs):
-    rec_refs, (keep_ref, send_ref) = refs[:-2], refs[-2:]
+
+
+def finish_kernel(pieces, own_ref, *refs):
+    rec_refs, out_refs = refs[:pieces], refs[pieces:]
+    at = 0
+    for out_ref, rec_ref in zip(out_refs, rec_refs if pieces > 1 else [rec_refs[0]] * len(out_refs)):
+        cols = slice(at, at + out_ref.shape[1])
+        at = cols.stop
+        out_ref[...] = own_ref[:, cols].astype(f32) + rec_ref[:, cols].astype(f32)
+
+
+def small_finish_kernel(own_ref, rec_ref, mp_own_ref, mp_rec_ref, *out_refs):
+    finish_kernel(1, own_ref, rec_ref, *out_refs[:-4])
+    *gain_refs, bias_ref = out_refs[-4:]
+    at = own_ref.shape[1] - LANES
+    values = own_ref[:, at:].astype(f32) + rec_ref[:, at:].astype(f32)
+    others = mp_own_ref[...].astype(f32) + mp_rec_ref[...].astype(f32)
+    lane = lax.broadcasted_iota(jnp.int32, (1, LANES), 1)
+    values += jnp.where(lane == 0, others, 0.0)
+    eye = (lax.broadcasted_iota(jnp.int32, (LANES, LANES), 0) == lane).astype(f32)
+    turned = lax.dot_general(
+        eye, values, (((1,), (1,)), ((), ())), precision=highest, preferred_element_type=f32
+    )
+    for i, gain_ref in enumerate(gain_refs):
+        gain_ref[...] = turned[i, :]
+    bias_ref[...] = turned[3 : 3 + bias_ref.shape[0], : bias_ref.shape[1]]
+
+
+def split_kernel(shard, bit, low, sends, own_ref, *refs):
+    rec_refs, keep_ref, send_refs = refs[: -1 - sends], refs[-1 - sends], refs[-sends:]
     own_bit = lax.axis_index("rows") // bit % 2
+    each = send_refs[0].shape[1]
     at = 0
     for rec_ref in rec_refs:
-        cols = slice(at, at + rec_ref.shape[1])
-        at = cols.stop
+        columns = rec_ref.shape[1]
         for j in range(keep_ref.shape[0] // shard):
-            for which, out_ref in ((own_bit, keep_ref), (1 - own_bit, send_ref)):
+            there = slice(j * shard, (j + 1) * shard)
+            for which in (own_bit, 1 - own_bit):
                 start = ((j // low * 2 + which) * low + j % low) * shard
                 rows = pl.ds(pl.multiple_of(start, shard), shard)
-                out_ref[j * shard : (j + 1) * shard, cols] = (
-                    own_ref[rows, cols].astype(f32) + rec_ref[rows, :].astype(f32)
+                total = (
+                    own_ref[rows, at : at + columns].astype(f32) + rec_ref[rows, :].astype(f32)
                 ).astype(bf16)
+                if which is own_bit:
+                    keep_ref[there, at : at + columns] = total
+                    continue
+                for i, send_ref in enumerate(send_refs):
+                    begin, end = max(at, i * each), min(at + columns, (i + 1) * each)
+                    if begin < end:
+                        send_ref[there, begin - i * each : end - i * each] = total[:, begin - at : end - at]
+        at += columns
 
 
 def fixed(shape, dtype):
@@ -637,10 +635,11 @@
 
 
 def gather_all(values):
-    bit = 1
-    while bit < lax.axis_size("rows"):
-        values = jnp.concatenate([values, swap(values, "rows", bit)], 0)
-        bit *= 2
+    bits = [1 << i for i in range(lax.axis_size("rows").bit_length() - 1)]
+    steps = [bits[:1]] + [bits[i : i + 2] for i in range(1, len(bits), 2)]
+    for step in steps:
+        masks = step + ([step[0] | step[1]] if len(step) > 1 else [])
+        values = jnp.concatenate([values] + [swap(values, "rows", mask) for mask in masks], 0)
     return jnp.concatenate([values, swap(values, "tower")], 0)
 
 
@@ -662,38 +661,60 @@
         if swapped and len(self.order) > 1:
             self.order[0], self.order[1] = self.order[1], self.order[0]
 
-    def split(self):
+    def split(self, sends=1):
         self.bit = self.order.pop(0)
         low = 1 << sorted(self.bits).index(self.bit)
         self.bits.remove(self.bit)
-        columns = self.own.shape[1]
+        rows, columns = self.own.shape[0] // 2, self.own.shape[1]
         if self.shard % 16 == 0:
-            half = struct((self.own.shape[0] // 2, columns), bf16)
-            self.own, self.send = whole(
-                self.name, functools.partial(split_kernel, self.shard, self.bit, low), (half, half), self.own, *self.received
+            self.own, *self.send = whole(
+                self.name,
+                functools.partial(split_kernel, self.shard, self.bit, low, sends),
+                (struct((rows, columns), bf16),) + (struct((rows, columns // sends), bf16),) * sends,
+                self.own,
+                *self.received,
             )
         else:
-            total = self.total().astype(bf16)
-            self.own, self.send = row_halves(total, self.bit, low, self.shard)
+            self.own, send = row_halves(self.total().astype(bf16), self.bit, low, self.shard)
+            self.send = jnp.split(send, sends, 1)
 
     def exchange(self):
-        self.received = [swap(self.send, "rows", self.bit)]
+        self.received = [swap(v, "rows", self.bit) for v in self.send]
+
+    def step(self, sends=1):
+        self.split(sends)
+        self.exchange()
 
     def total(self):
         return self.own.astype(f32) + jnp.concatenate(self.received, 1).astype(f32)
 
-    def step(self):
-        self.split()
-        self.exchange()
-
-    def finish(self):
+    def finish(self, *columns):
         while self.order:
             self.step()
-        return self.total()
+        outs = tuple(struct((self.own.shape[0], n), f32) for n in columns)
+        kernel = functools.partial(finish_kernel, len(self.received))
+        return whole(self.name + "_finish", kernel, outs, self.own, *self.received)
+
+    def small_finish(self, bias_shape, *columns):
+        while self.order:
+            self.step()
+        rows = self.own.shape[0]
+        outs = tuple(struct((rows, n), f32) for n in columns)
+        outs += (struct((rows,), f32),) * 3 + (struct(bias_shape, f32),)
+        across = [(i, i ^ 1 ^ (2 * self.bit)) for i in range(2 * lax.axis_size("rows"))]
+        return whole(
+            self.name + "_finish",
+            small_finish_kernel,
+            outs,
+            self.own,
+            *self.received,
+            swap(self.own[:, -LANES:], "mp"),
+            lax.ppermute(self.send[0][:, -LANES:], ("rows", "mp"), across),
+        )
 
 
 def tie(*values):
-    return lax.optimization_barrier(values)
+    return list(lax.optimization_barrier(values))
 
 
 def struct(shape, dtype):
@@ -864,219 +885,190 @@
         in_vmem=1,
     )
 
-    two_part, two_own, two_received, hidden_two_grad, final_gain_part = [], [], [], [], []
-    ff_grad, up_out_grad = [], []
-    half_shapes = (struct((width // 2, PIECE), bf16),) * (hidden // PIECE) + (struct((width // 2, hidden), bf16),)
-    for c in chunks:
-        last = c == CHUNKS - 1
-        low_shape = ((size, width), bf16)
-        outs = whole(
-            "feed_forward_back",
-            functools.partial(ff_back_kernel, c),
-            (
-                struct((size, width), bf16),
-                stored((size, width), bf16),
-                stored((size, width), f32),
-                struct((1, width), f32),
-                fixed((size, hidden), bf16),
-            )
-            + (half_shapes if last else (fixed(*low_shape),)),
-            down_held,
-            up_held,
-            hidden_two[c],
-            slope[c],
-            *([*active, *ff_grad] if last else []),
-            pooled_grad,
-            segments,
-            final_gain,
-            scratch=([pltpu.VMEM(*low_shape)] if last else [])
-            + [pltpu.VMEM((size, width), f32), pltpu.SemaphoreType.DMA((2,))],
-            in_vmem=4 + (2 * CHUNKS - 1 if last else 0),
+    two_part, hidden_two_grad, ff_grad, up_out_grad, final_gain_part = whole(
+        "feed_forward_back",
+        ff_back_kernel,
+        (
+            fixed((length, width), bf16),
+            fixed((length, width), f32),
+            fixed((length, width), bf16),
+            fixed((length, hidden), bf16),
+            struct((1, width), f32),
+        ),
+        down_held,
+        up_held,
+        *hidden_two,
+        *slope,
+        pooled_grad,
+        segments,
+        final_gain,
+        in_vmem=2 + 2 * CHUNKS,
+    )
+    two_received = swap(two_part, "mp")
+    half_shapes = (struct((width // 2, hidden // FF_SENDS), bf16),) * FF_SENDS + (struct((width // 2, hidden), bf16),)
+    *halves, own = whole("down_weight", down_weight_kernel, half_shapes, ff_grad, *active, in_vmem=1 + CHUNKS)
+    down_scatter = RowsScatter("down_split", shard, own, [swap(v, "tower") for v in halves])
+    *halves, own = whole("up_weight", up_weight_kernel, half_shapes, up_out_grad, *normed_two, in_vmem=1 + CHUNKS)
+    up_scatter = RowsScatter("up_split", shard, own, [swap(v, "tower") for v in halves], swapped=True)
+    down_scatter.step()
+    up_scatter.split()
+    two_received, down_send, up_scatter.send = tie(
+        two_received, down_scatter.send, up_scatter.send
+    )
+    up_scatter.exchange()
+    hidden_one_grad, attn_grad, mix_grad, ff_gain_part, *heads_held = whole(
+        "middle_back",
+        middle_back_kernel,
+        (
+            stored((length, width), f32),
+            stored((length, width), bf16),
+            fixed((length, inner), bf16),
+            struct((1, width), f32),
         )
-        for kept, out in zip((two_part, two_own, hidden_two_grad, final_gain_part, up_out_grad), outs):
-            kept.append(out)
-        if not last:
-            ff_grad.append(outs[5])
-        two_received.append(swap(two_part[c], "mp"))
-    down_scatter = RowsScatter("down_split", shard, outs[-1], [swap(v, "tower") for v in outs[5:-1]])
-
-    hidden_one_grad, attn_grad, mix_grad, ff_gain_part = [], [], [], []
-    for c in chunks:
-        first, last = c == 0, c == CHUNKS - 1
-        if last:
-            down_scatter.split()
-            up_scatter.split()
-            two_received[c], down_scatter.send, up_scatter.send = tie(
-                two_received[c], down_scatter.send, up_scatter.send
-            )
-            down_scatter.exchange()
-            up_scatter.exchange()
-        heads_shape = fixed((length, inner), bf16)
-        outs = whole(
-            "middle_back",
-            functools.partial(middle_back_kernel, c),
-            (
-                stored((size, width), f32),
-                stored((size, width), bf16),
-                fixed((size, inner), bf16),
-                struct((1, width), f32),
-            )
-            + ((heads_shape,) * 3 + (fixed((head_count, length, length), bf16),) if last else ())
-            + (half_shapes if first else ()),
-            two_own[c],
-            hidden_two_grad[c],
-            *([query, key, value, probs] if last else []),
-            output_whole,
-            hidden_one[c],
-            *([*normed_two, *up_out_grad] if first else []),
-            two_received[c],
-            ff_gain,
-            scratch=[
-                pltpu.VMEM((size, width), bf16),
-                pltpu.VMEM((size, width), f32),
-                pltpu.VMEM((size, width), f32),
-                pltpu.VMEM((size, width), bf16),
-                pltpu.SemaphoreType.DMA((6,)),
-                pltpu.SemaphoreType.DMA((2,)),
-            ],
-            in_hbm=6 if last else 2,
-            in_vmem=2 + (2 * CHUNKS if first else 0),
-        )
-        for kept, out in zip((hidden_one_grad, attn_grad, mix_grad, ff_gain_part), outs):
-            kept.append(out)
-        if first:
-            up_scatter = RowsScatter(
-                "up_split", shard, outs[-1], [swap(v, "tower") for v in outs[4:-1]], swapped=True
-            )
-        if last:
-            heads_held = outs[4:8]
-
-    qkv_grads, bias_grad, qkv_weight, normed_held = whole(
+        + (fixed((length, inner), bf16),) * 3
+        + (fixed((head_count, length, length), bf16),),
+        query,
+        key,
+        value,
+        probs,
+        output_whole,
+        two_part,
+        hidden_two_grad,
+        *hidden_one,
+        two_received,
+        ff_gain,
+        scratch=[
+            pltpu.VMEM((length, width), f32),
+            pltpu.VMEM((length, width), bf16),
+            pltpu.SemaphoreType.DMA((4,)),
+            pltpu.SemaphoreType.DMA((2,)),
+        ],
+        in_hbm=4,
+        in_vmem=3 + CHUNKS,
+    )
+
+    qkv_grads, bias_grad, normed_held, qkv_weight, *halves = whole(
         "attention_back",
         attend_back_kernel,
         (
             fixed((length, 3 * inner), bf16),
             struct((bucket_count, head_count), f32),
+            fixed((length, width), bf16),
             fixed((3, width, inner), bf16),
-            fixed((length, width), bf16),
-        ),
+        )
+        + (struct((width // 2, 2 * inner // QK_SENDS), bf16),) * QK_SENDS
+        + (struct((width // 2, 2 * inner), bf16),),
         query_weight,
         key_weight,
         value_weight,
         normed_one,
         *heads_held,
-        *mix_grad,
+        mix_grad,
         bucket_ids,
         scratch=[
             pltpu.VMEM((2, length, length), bf16),
             pltpu.VMEM((2, BLOCK, span), f32),
             pltpu.VMEM((8, span), f32),
             pltpu.VMEM((2, BLOCK, length), f32),
-            pltpu.VMEM((length, inner), bf16),
             pltpu.SemaphoreType.DMA((4,)),
         ],
         in_hbm=4,
-        in_vmem=4 + CHUNKS,
-    )
-    *one_part, one_own, attn_gain_part = whole(
+        in_vmem=5,
+    )
+    first_scatter = RowsScatter("query_key_split", shard, halves[-1], [swap(v, "tower") for v in halves[:-1]])
+    qkv_grads, down_scatter.received, up_scatter.received = tie(
+        qkv_grads, down_scatter.received, up_scatter.received
+    )
+    down_scatter.split()
+    up_scatter.split()
+    first_scatter.split()
+    qkv_grads = tie(qkv_grads, down_scatter.send, up_scatter.send, first_scatter.send)[0]
+    down_scatter.exchange()
+    up_scatter.exchange()
+    first_scatter.exchange()
+    one_part, one_own, *halves, own = whole(
         "project_back",
-        project_back_kernel,
-        (struct((size, width), bf16),) * CHUNKS
-        + (stored((length, width), bf16), struct((1, width), f32)),
+        functools.partial(project_back_kernel, shard),
+        (struct((length, width), bf16), stored((length, width), bf16))
+        + (struct((width // 2, 2 * inner // VO_SENDS), bf16),) * VO_SENDS
+        + (struct((width // 2, LANES), bf16), struct((width // 2, 2 * inner + LANES), bf16)),
+        mix_stored,
+        attn_grad,
         qkv_weight,
         tok,
-        qkv_grads,
-        scratch=[pltpu.VMEM((length, width), bf16), pltpu.SemaphoreType.DMA((1,))],
-        in_vmem=3,
-    )
-    one_received = [swap(part, "mp") for part in one_part]
-
-    piece = struct((width // 2, PIECE), bf16)
-    *others, small_other, own = whole(
-        "query_key_weight",
-        functools.partial(query_key_kernel, shard),
-        (piece,) * (2 * inner // PIECE)
-        + (struct((width // 2, LANES), bf16), struct((width // 2, 2 * inner + LANES), bf16)),
         normed_held,
         qkv_grads,
         bias_grad,
-        attn_gain_part,
-        *ff_gain_part,
-        *final_gain_part,
-        scratch=[pltpu.VMEM((width, LANES), f32)],
-        in_vmem=2,
-    )
-    first_scatter = RowsScatter("query_key_split", shard, own, [swap(v, "tower") for v in (*others, small_other)])
-    *others, own = whole(
-        "value_output_weight",
-        value_output_kernel,
-        (piece,) * (2 * inner // PIECE) + (struct((width // 2, 2 * inner), bf16),),
-        mix_stored,
-        *attn_grad,
-        normed_held,
-        qkv_grads,
-        scratch=[pltpu.VMEM((length, inner), bf16)]
-        + [pltpu.VMEM((size, width), bf16)] * CHUNKS
-        + [pltpu.SemaphoreType.DMA((1 + CHUNKS,))],
-        in_hbm=1 + CHUNKS,
-        in_vmem=2,
-    )
-    second_scatter = RowsScatter(
-        "value_output_split", shard, own, [swap(v, "tower") for v in others], swapped=True
-    )
-    first_scatter.split()
-    second_scatter.split()
+        ff_gain_part,
+        final_gain_part,
+        scratch=[
+            pltpu.VMEM((width, LANES), f32),
+            pltpu.VMEM((length, inner), bf16),
+            pltpu.VMEM((length, width), bf16),
+            pltpu.SemaphoreType.DMA((3,)),
+        ],
+        in_hbm=2,
+        in_vmem=4,
+    )
+    one_received = swap(one_part, "mp")
     down_scatter.split()
     up_scatter.split()
-    one_received[0], first_scatter.send, second_scatter.send, down_scatter.send, up_scatter.send = tie(
-        one_received[0], first_scatter.send, second_scatter.send, down_scatter.send, up_scatter.send
-    )
-    first_scatter.exchange()
-    second_scatter.exchange()
+    halves = tie(halves, down_scatter.send, up_scatter.send)[0]
     down_scatter.exchange()
     up_scatter.exchange()
-    down_sum = down_scatter.finish()
-    up_sum = up_scatter.finish()
-    first_sum = first_scatter.finish()
-    second_sum = second_scatter.finish()
-    small = first_sum[:, 2 * inner :]
-    attn_gain_sum = small[:, 0:1] + swap(small[:, 0:1], "mp")
-    bias_rows = [
-        small[:, 3 + g * head_count : 3 + (g + 1) * head_count]
-        for g in range(-(-bucket_count // shard))
-    ]
-    bias_total = jnp.concatenate(bias_rows, 0)[:bucket_count]
-
+    second_scatter = RowsScatter(
+        "value_output_split", shard, own, [swap(v, "tower") for v in halves], swapped=True
+    )
+    second_scatter.step()
+    first_scatter.received, second_scatter.received, down_scatter.received = tie(
+        first_scatter.received, second_scatter.received, down_scatter.received
+    )
+    first_scatter.step()
+    second_scatter.step()
     tokens_grad = whole(
         "last",
         last_kernel,
         struct((length, width), f32),
         one_own,
-        *hidden_one_grad,
+        hidden_one_grad,
         tok,
         attn_gain,
-        *one_received,
+        one_received,
         scratch=[
             pltpu.VMEM((length, width), bf16),
             pltpu.VMEM((length, width), f32),
-            pltpu.SemaphoreType.DMA((1 + CHUNKS,)),
+            pltpu.SemaphoreType.DMA((2,)),
         ],
-        in_hbm=1 + CHUNKS,
+        in_hbm=2,
         in_vmem=1,
-    ).reshape(tokens.shape)
+    )
+    first_scatter.received, second_scatter.received, down_scatter.received, up_scatter.received, tokens_grad = tie(
+        first_scatter.received, second_scatter.received, down_scatter.received, up_scatter.received, tokens_grad
+    )
+    first_scatter.step()
+    second_scatter.step()
+    (down_sum,) = down_scatter.finish(hidden)
+    (up_sum,) = up_scatter.finish(hidden)
+    bias_pieces = -(-bucket_count // shard)
+    value_sum, output_sum, attn_gain_sum, ff_gain_sum, final_gain_sum, turned = second_scatter.small_finish(
+        (head_count * bias_pieces, min(shard, bucket_count)), inner, inner
+    )
+    query_sum, key_sum = first_scatter.finish(inner, inner)
+    bias_rows = [turned[g * head_count : (g + 1) * head_count, :] for g in range(bias_pieces)]
+    bias_total = jnp.concatenate(bias_rows, 1)[:, :bucket_count].T
     return (
         loss[0, 0],
-        tokens_grad,
-        attn_gain_sum[:, 0],
-        first_sum[:, :inner],
-        first_sum[:, inner : 2 * inner],
-        second_sum[:, :inner],
-        second_sum[:, inner:].T,
+        tokens_grad.reshape(tokens.shape),
+        attn_gain_sum,
+        query_sum,
+        key_sum,
+        value_sum,
+        output_sum.T,
         bias_total,
-        small[:, 1],
+        ff_gain_sum,
         up_sum,
         down_sum.T,
-        small[:, 2],
+        final_gain_sum,
         proj_grad,
     )
 

time: 158 us -> 147 us (0.930)
  waiting for transfers between devices: 61.8 us -> 58 us
  other arithmetic: 2.28 us -> 0 us
  local copies, waits for them, and re-layouts: 3.11 us -> 1.05 us
    ppermute x40 -> x39, waiting for transfers between devices: 61.8 us -> 57.6 us  [swap(): return lax.ppermute(values, axis, [(i, i ^ bit) for i in range(count)])]
    ppermute x40 -> x39, starting transfers between devices: 33.3 us -> 30.3 us  [swap(): return lax.ppermute(values, axis, [(i, i ^ bit) for i in range(count)])]
    ppermute x0 -> x1, starting transfers between devices: none -> 1.59 us  [small_finish(): lax.ppermute(self.send[0][:, -LANES:], ('rows', 'mp'), across)]
    pallas_call x28 -> x30, Pallas kernels: 55.9 us -> 54.6 us  [whole(): pl.pallas_call(kernel, out_shape=out_shapes, in_specs=[hbm] * in_hbm + [v...]
  transfers between devices with their start and end apart: 40 -> 40, of which waited for: 26 -> 21; matrix products, arithmetic and copies ran while one was open for 2% -> 0% of each run, Pallas kernels for 24% -> 32%
where the time goes in v2:
time: 147 us
  waiting for transfers between devices  58 us (39%)
  Pallas kernels  54.6 us (37%)
  starting transfers between devices  31.9 us (22%)
    ppermute x39, waiting for transfers between devices, swap(): return lax.ppermute(values, axis, [(i, i ^ bit) for i in range(count)])  57.6 us
    pallas_call x30, Pallas kernels, whole(): pl.pallas_call(kernel, out_shape=out_shapes, in_specs=[hbm] * in_hbm + [v...  54.6 us
    ppermute x39, starting transfers between devices, swap(): return lax.ppermute(values, axis, [(i, i ^ bit) for i in range(count)])  30.3 us
  transfers between devices with their start and end apart: 40, of which 21 were waited for; matrix products, arithmetic and copies ran while one was open for 0% of the time, Pallas kernels for 32%

profile of v2, /device:TPU:0, one launch (start us, length us, event | category | flops | bytes accessed | tf_op | source)
XLA Modules:
  0.0 146.6 jit_solution(11929076963076607233)
XLA Ops:
  1.6 3.0 %collective-permute-start = (bf16[192,768]{1,0:T(8,128)(2,1)S(1)}, bf16[192,768]{1,0:T(8,128)(2,1)S(1)}, u32[]{:S(2)}, u32[]{:S(2)}) collective-permute-start(bf16[192,768]{1,0:T(8,128)(2,1)S(1)} %constant_dynamic-slice_fusion), channel_id=1, source_target_pairs={{0,1},{1,0},{2,3},{3,2},{4,5},{5,4},{6,7},{7,6},{8,9},{9,8},{10,11... | collective-permute-start | bytes 884744 | tf_op jit(solution)/shard_map/ppermute | solution.py:634
  4.7 10.8 %attention.1 = (bf16[512,768]{1,0:T(8,128)(2,1)}, bf16[512,384]{1,0:T(8,128)(2,1)}, bf16[512,384]{1,0:T(8,128)(2,1)}, bf16[512,384]{1,0:T(8,128)(2,1)}, bf16[6,5...) custom-call(bf16[512,768]{1,0:T(8,128)(2,1)} %bitcast.13, ...), custom_call_target="tpu_custom_call" | custom-call | flops 1 | bytes 1 | tf_op jit(solution)/shard_map/attention/pallas_call | solution.py:614
  15.6 2.0 %collective-permute-start.2 = (bf16[256,384]{1,0:T(8,128)(2,1)S(1)}, bf16[256,384]{1,0:T(8,128)(2,1)S(1)}, u32[]{:S(2)}, u32[]{:S(2)}) collective-permute-start(bf16[256,384]{1,0:T(8,128)(2,1)S(1)} %get-tuple-element.131.mix_own), channel_id=1, source_target_pairs={{0,1},{1,0},{2,3},{3,2},{4,5},{5,4},{6,7},{7,6},{8,9},{9,8},{10,11... | collective-permute-start | bytes 589832 | tf_op jit(solution)/shard_map/ppermute | solution.py:634
  17.6 3.1 %load.1 = (bf16[768,768]{1,0:T(8,128)(2,1)S(1)}, bf16[768,1536]{1,0:T(8,128)(2,1)S(1)}, bf16[1536,768]{1,0:T(8,128)(2,1)S(1)}, bf16[768,768]{1,0:T(8,128)(2,1)S(1)}) custom-call(bf16[384,768]{1,0:T(8,128)(2,1)} %wo_hbm.1, bf16[768,1536]{1,0:T(8,128)(2,1)} %up_hbm.1, bf16[1536,768]{1,0:T(8,128)(2,1)} %down_hbm.1, bf16[768,768]{1,0:T(8,128)(2,1)} %proj_hbm.1, ...), custom_call_target="tpu_custom_call" | custom-call | flops 1 | bytes 1 | tf_op jit(solution)/shard_map/load/pallas_call | solution.py:614
  20.7 2.6 %collective-permute-done.4.mix_other = bf16[256,384]{1,0:T(8,128)(2,1)S(1)} collective-permute-done((bf16[256,384]{1,0:T(8,128)(2,1)S(1)}, bf16[256,384]{1,0:T(8,128)(2,1)S(1)}, u32[]{:S(2)}, u32[]{:S(2)}) %collective-permute-start.4) | collective-permute-done | bytes 196640 | tf_op jit(solution)/shard_map/ppermute | solution.py:634
  23.3 3.3 %feed_forward.3 = (f32[256,768]{1,0:T(8,128)S(1)}, bf16[256,768]{1,0:T(8,128)(2,1)S(1)}, bf16[256,1536]{1,0:T(8,128)(2,1)S(1)}, f32[256,1536]{1,0:T(8,128)S(1)}, bf16[256,768]{1,0:T(8,128)(2,1)S(1)}) custom-call(bf16[512,768]{1,0:T(8,128)(2,1)S(1)} %get-tuple-element.135.tok_ref.refs_3_, bf16[768,768]{1,0:T(8,128)(2,1)S(1)} %get-tuple-element.136.wo_ref.refs_4_, ...), custom_call_target="tpu_custom_call" | custom-call | flops 1 | bytes 1 | tf_op jit(solution)/shard_map/feed_forward/pallas_call | solution.py:614
  27.1 3.3 %feed_forward.2 = (f32[256,768]{1,0:T(8,128)S(1)}, bf16[256,768]{1,0:T(8,128)(2,1)S(1)}, bf16[256,1536]{1,0:T(8,128)(2,1)S(1)}, f32[256,1536]{1,0:T(8,128)S(1)}, bf16[256,768]{1,0:T(8,128)(2,1)S(1)}) custom-call(bf16[512,768]{1,0:T(8,128)(2,1)S(1)} %get-tuple-element.135.tok_ref.refs_3_, bf16[768,768]{1,0:T(8,128)(2,1)S(1)} %get-tuple-element.136.wo_ref.refs_4_, ...), custom_call_target="tpu_custom_call" | custom-call | flops 1 | bytes 1 | tf_op jit(solution)/shard_map/feed_forward/pallas_call | solution.py:614
  30.4 1.7 %collective-permute-start.3 = (bf16[256,768]{1,0:T(8,128)(2,1)S(1)}, bf16[256,768]{1,0:T(8,128)(2,1)S(1)}, u32[]{:S(2)}, u32[]{:S(2)}) collective-permute-start(bf16[256,768]{1,0:T(8,128)(2,1)S(1)} %get-tuple-element.140.own_ref), channel_id=1, source_target_pairs={{0,1},{1,0},{2,3},{3,2},{4,5},{5,4},{6,7},{7,6},{8,9},{9,8},{10,11... | collective-permute-start | bytes 1179656 | tf_op jit(solution)/shard_map/ppermute | solution.py:634
  32.1 6.7 %collective-permute-done.5.rec_ref = bf16[256,768]{1,0:T(8,128)(2,1)S(1)} collective-permute-done((bf16[256,768]{1,0:T(8,128)(2,1)S(1)}, bf16[256,768]{1,0:T(8,128)(2,1)S(1)}, u32[]{:S(2)}, u32[]{:S(2)}) %collective-permute-start.5) | collective-permute-done | bytes 393248 | tf_op jit(solution)/shard_map/ppermute | solution.py:634
  39.1 6.2 %collective-permute-done.3.rec_ref = bf16[256,768]{1,0:T(8,128)(2,1)S(1)} collective-permute-done((bf16[256,768]{1,0:T(8,128)(2,1)S(1)}, bf16[256,768]{1,0:T(8,128)(2,1)S(1)}, u32[]{:S(2)}, u32[]{:S(2)}) %collective-permute-start.3) | collective-permute-done | bytes 393248 | tf_op jit(solution)/shard_map/ppermute | solution.py:634
  45.7 1.6 %collective-permute-start.6 = (bf16[8,768]{1,0:T(8,128)(2,1)S(1)}, bf16[8,768]{1,0:T(8,128)(2,1)S(1)}, u32[]{:S(2)}, u32[]{:S(2)}) collective-permute-start(bf16[8,768]{1,0:T(8,128)(2,1)S(1)} %get-tuple-element.146), channel_id=1, source_target_pairs={{0,2},{2,0},{4,6},{6,4},{8,10},{10,8},{12,14},{14,12},{1,3},{3,1},... | collective-permute-start | bytes 36872 | tf_op jit(solution)/shard_map/ppermute | solution.py:634
  47.3 2.2 %collective-permute-done.6 = bf16[8,768]{1,0:T(8,128)(2,1)S(1)} collective-permute-done((bf16[8,768]{1,0:T(8,128)(2,1)S(1)}, bf16[8,768]{1,0:T(8,128)(2,1)S(1)}, u32[]{:S(2)}, u32[]{:S(2)}) %collective-permute-start.6) | collective-permute-done | bytes 12320 | tf_op jit(solution)/shard_map/ppermute | solution.py:634
  49.5 1.6 %collective-permute-start.7 = (bf16[16,768]{1,0:T(8,128)(2,1)S(1)}, bf16[16,768]{1,0:T(8,128)(2,1)S(1)}, u32[]{:S(2)}, u32[]{:S(2)}) collective-permute-start(bf16[16,768]{1,0:T(8,128)(2,1)S(1)} %get-tuple-element.257), channel_id=1, source_target_pairs={{0,4},{2,6},{4,0},{6,2},{8,12},{10,14},{12,8},{14,10},{1,5},{3,7},... | collective-permute-start | bytes 73736 | tf_op jit(solution)/shard_map/ppermute | solution.py:634
  51.1 2.5 %collective-permute-start.9 = (bf16[16,768]{1,0:T(8,128)(2,1)S(1)}, bf16[16,768]{1,0:T(8,128)(2,1)S(1)}, u32[]{:S(2)}, u32[]{:S(2)}) collective-permute-start(bf16[16,768]{1,0:T(8,128)(2,1)S(1)} %get-tuple-element.257), channel_id=1, source_target_pairs={{0,12},{2,14},{4,8},{6,10},{8,4},{10,6},{12,0},{14,2},{1,13},{3,15... | collective-permute-start | bytes 73736 | tf_op jit(solution)/shard_map/ppermute | solution.py:634
  53.7 4.9 %collective-permute-done.8 = bf16[16,768]{1,0:T(8,128)(2,1)S(1)} collective-permute-done((bf16[16,768]{1,0:T(8,128)(2,1)S(1)}, bf16[16,768]{1,0:T(8,128)(2,1)S(1)}, u32[]{:S(2)}, u32[]{:S(2)}) %collective-permute-start.8) | collective-permute-done | bytes 24608 | tf_op jit(solution)/shard_map/ppermute | solution.py:634
  60.0 2.0 %contrast.1 = (f32[1,1]{1,0:T(1,128)}, f32[48,768]{1,0:T(8,128)}, f32[8,768]{1,0:T(8,128)S(1)}) custom-call(bf16[768,768]{1,0:T(8,128)(2,1)S(1)} %get-tuple-element.134.proj_ref, bf16[128,768]{1,0:T(8,128)(2,1)S(1)} %constant_dynamic-update-slice_fusion.7.gathered_ref, s32[64]{0:T(128)S(1)} %copy-done.5), custom_call_target="tpu_custom_call" | custom-call | flops 1 | bytes 1 | tf_op jit(solution)/shard_map/contrast/pallas_call | solution.py:614
  62.0 3.9 %feed_forward_back.1 = (bf16[512,768]{1,0:T(8,128)(2,1)S(1)}, f32[512,768]{1,0:T(8,128)S(1)}, bf16[512,768]{1,0:T(8,128)(2,1)S(1)}, bf16[512,1536]{1,0:T(8,128)(2,1)S(1)}, f32[1,768]{1,0:T(1,128)S(1)}) custom-call(bf16[1536,768]{1,0:T(8,128)(2,1)S(1)} %get-tuple-element.138.down_ref, bf16[768,1536]{1,0:T(8,128)(2,1)S(1)} %get-tuple-element.137.up_ref, ...), custom_call_target="tpu_custom_call" | custom-call | flops 1 | bytes 1 | tf_op jit(solution)/shard_map/feed_forward_back/pallas_call | solution.py:614
  66.5 1.8 %down_weight.1 = (bf16[384,384]{1,0:T(8,128)(2,1)S(1)}, bf16[384,384]{1,0:T(8,128)(2,1)S(1)}, bf16[384,384]{1,0:T(8,128)(2,1)S(1)}, bf16[384,384]{1,0:T(8,128)(2,1)S(1)}, bf16[384,1536]{1,0:T(8,128)(2,1)S(1)}) custom-call(bf16[512,768]{1,0:T(8,128)(2,1)S(1)} %get-tuple-element.160.df_ref, bf16[256,1536]{1,0:T(8,128)(2,1)S(1)} %get-tuple-element.161.refs_0_, ...), custom_call_target="tpu_custom_call" | custom-call | flops 1 | bytes 1 | tf_op jit(solution)/shard_map/down_weight/pallas_call | solution.py:614
  69.4 1.8 %up_weight.1 = (bf16[384,384]{1,0:T(8,128)(2,1)S(1)}, bf16[384,384]{1,0:T(8,128)(2,1)S(1)}, bf16[384,384]{1,0:T(8,128)(2,1)S(1)}, bf16[384,384]{1,0:T(8,128)(2,1)S(1)}, bf16[384,1536]{1,0:T(8,128)(2,1)S(1)}) custom-call(bf16[512,1536]{1,0:T(8,128)(2,1)S(1)} %get-tuple-element.169.du_ref, bf16[256,768]{1,0:T(8,128)(2,1)S(1)} %get-tuple-element.170.refs_0_, ...), custom_call_target="tpu_custom_call" | custom-call | flops 1 | bytes 1 | tf_op jit(solution)/shard_map/up_weight/pallas_call | solution.py:614
  74.7 10.8 %collective-permute-done.11.refs_9_ = bf16[512,768]{1,0:T(8,128)(2,1)S(1)} collective-permute-done((bf16[512,768]{1,0:T(8,128)(2,1)S(1)}, bf16[512,768]{1,0:T(8,128)(2,1)S(1)}, u32[]{:S(2)}, u32[]{:S(2)}) %collective-permute-start.11) | collective-permute-done | bytes 786464 | tf_op jit(solution)/shard_map/ppermute | solution.py:634
  86.1 3.7 %middle_back.1 = (f32[512,768]{1,0:T(8,128)}, bf16[512,768]{1,0:T(8,128)(2,1)}, bf16[512,384]{1,0:T(8,128)(2,1)S(1)}, f32[1,768]{1,0:T(1,128)S(1)}, bf16[512,384...) custom-call(bf16[512,384]{1,0:T(8,128)(2,1)} %get-tuple-element.149., ...), custom_call_target="tpu_custom_call" | custom-call | flops 1 | bytes 1 | tf_op jit(solution)/shard_map/middle_back/pallas_call | solution.py:614
  89.8 8.1 %attention_back.1 = (bf16[512,1152]{1,0:T(8,128)(2,1)S(1)}, f32[32,6]{1,0:T(8,128)S(1)}, bf16[512,768]{1,0:T(8,128)(2,1)S(1)}, bf16[3,768,384]{2,1,0:T(8,128)(2,...) custom-call(bf16[768,384]{1,0:T(8,128)(2,1)} %wq_hbm.3, ...), custom_call_target="tpu_custom_call" | custom-call | flops 1 | bytes 1 | tf_op jit(solution)/shard_map/attention_back/pallas_call | solution.py:614
  98.5 1.6 %collective-permute-done.24.refs_0_ = bf16[192,1536]{1,0:T(8,128)(2,1)S(1)} collective-permute-done((bf16[192,1536]{1,0:T(8,128)(2,1)S(1)}, bf16[192,1536]{1,0:T(8,128)(2,1)S(1)}, u32[]{:S(2)}, u32[]{:S(2)}) %collective-permute-start.24) | collective-permute-done | bytes 589856 | tf_op jit(solution)/shard_map/ppermute | solution.py:634
  102.7 4.0 %project_back.1 = (bf16[512,768]{1,0:T(8,128)(2,1)S(1)}, bf16[512,768]{1,0:T(8,128)(2,1)}, bf16[384,384]{1,0:T(8,128)(2,1)S(1)}, bf16[384,384]{1,0:T(8,128)(2,1)...) custom-call(bf16[512,384]{1,0:T(8,128)(2,1)} %get-tuple-element.189.refs_0_, ...), custom_call_target="tpu_custom_call" | custom-call | flops 1 | bytes 1 | tf_op jit(solution)/shard_map/project_back/pallas_call | solution.py:614
  114.0 8.1 %collective-permute-done.22.refs_0_ = bf16[192,768]{1,0:T(8,128)(2,1)S(1)} collective-permute-done((bf16[192,768]{1,0:T(8,128)(2,1)S(1)}, bf16[192,768]{1,0:T(8,128)(2,1)S(1)}, u32[]{:S(2)}, u32[]{:S(2)}) %collective-permute-start.22) | collective-permute-done | bytes 294944 | tf_op jit(solution)/shard_map/ppermute | solution.py:634
  122.1 2.0 %collective-permute-done.31.refs_0_ = bf16[48,1536]{1,0:T(8,128)(2,1)S(1)} collective-permute-done((bf16[48,1536]{1,0:T(8,128)(2,1)S(1)}, bf16[48,1536]{1,0:T(8,128)(2,1)S(1)}, u32[]{:S(2)}, u32[]{:S(2)}) %collective-permute-start.31) | collective-permute-done | bytes 147488 | tf_op jit(solution)/shard_map/ppermute | solution.py:634
  125.8 2.4 %collective-permute-start.34 = (bf16[48,1536]{1,0:T(8,128)(2,1)S(1)}, bf16[48,1536]{1,0:T(8,128)(2,1)S(1)}, u32[]{:S(2)}, u32[]{:S(2)}) collective-permute-start(bf16[48,1536]{1,0:T(8,128)(2,1)S(1)} %get-tuple-element.213), channel_id=1, source_target_pairs={{0,8},{2,10},{4,12},{6,14},{8,0},{10,2},{12,4},{14,6},{1,9},{3,11}... | collective-permute-start | bytes 442376 | tf_op jit(solution)/shard_map/ppermute | solution.py:634
  129.3 3.5 %last.1 = f32[512,768]{1,0:T(8,128)} custom-call(bf16[512,768]{1,0:T(8,128)(2,1)} %get-tuple-element.224.own_hbm, f32[512,768]{1,0:T(8,128)} %get-tuple-element.225.dh1_hbm, bf16[512,768]{1,0:T(8,128)(2,1)S(1)} %get-tuple-element.135.tok_ref.refs_3_, f32[768]{0:T(1024)S(1)} %copy-done.4, bf16[512,768]{1,0:T(8,128)(2,1)S(1)} %collective-permute-done.35.rec_ref), custom_call_target="tpu_custom_call" | custom-call | flops 1 | bytes 1 | tf_op jit(solution)/shard_map/last/pallas_call | solution.py:614
  132.9 1.9 %collective-permute-done.34.refs_0_ = bf16[48,1536]{1,0:T(8,128)(2,1)S(1)} collective-permute-done((bf16[48,1536]{1,0:T(8,128)(2,1)S(1)}, bf16[48,1536]{1,0:T(8,128)(2,1)S(1)}, u32[]{:S(2)}, u32[]{:S(2)}) %collective-permute-start.34) | collective-permute-done | bytes 147488 | tf_op jit(solution)/shard_map/ppermute | solution.py:634
  136.1 2.4 %collective-permute-start.39 = (bf16[48,768]{1,0:T(8,128)(2,1)S(1)}, bf16[48,768]{1,0:T(8,128)(2,1)S(1)}, u32[]{:S(2)}, u32[]{:S(2)}) collective-permute-start(bf16[48,768]{1,0:T(8,128)(2,1)S(1)} %get-tuple-element.236), channel_id=1, source_target_pairs={{0,8},{2,10},{4,12},{6,14},{8,0},{10,2},{12,4},{14,6},{1,9},{3,11}... | collective-permute-start | bytes 221192 | tf_op jit(solution)/shard_map/ppermute | solution.py:634
  138.5 1.6 %collective-permute-start.38 = (bf16[48,128]{1,0:T(8,128)(2,1)S(1)}, bf16[48,128]{1,0:T(8,128)(2,1)S(1)}, u32[]{:S(2)}, u32[]{:S(2)}) collective-permute-start(bf16[48,128]{1,0:T(8,128)(2,1)S(1)} %slice.7), channel_id=1, source_target_pairs={{0,9},{1,8},{2,11},{3,10},{4,13},{5,12},{6,15},{7,14},{8,1},{9,0},... | collective-permute-start | bytes 36872 | tf_op jit(solution)/shard_map/ppermute | solution.py:712
  142.0 2.6 %collective-permute-done.39.refs_0_ = bf16[48,768]{1,0:T(8,128)(2,1)S(1)} collective-permute-done((bf16[48,768]{1,0:T(8,128)(2,1)S(1)}, bf16[48,768]{1,0:T(8,128)(2,1)S(1)}, u32[]{:S(2)}, u32[]{:S(2)}) %collective-permute-start.39) | collective-permute-done | bytes 73760 | tf_op jit(solution)/shard_map/ppermute | solution.py:634
  (99 shorter events, 28.0 us)
Async XLA Ops:
  1.6 13.8 %collective-permute-start = (bf16[192,768]{1,0:T(8,128)(2,1)S(1)}, bf16[192,768]{1,0:T(8,128)(2,1)S(1)}, u32[]{:S(2)}, u32[]{:S(2)}) collective-permute-start(bf16[192,768]{1,0:T(8,128)(2,1)S(1)} %constant_dynamic-slice_fusion), channel_id=1, source_target_pairs={{0,1},{1,0},{2,3},{3,2},{4,5},{5,4},{6,7},{7,6},{8,9},{9,8},{10,11... | collective-permute-start | bytes 884744 | tf_op jit(solution)/shard_map/ppermute | solution.py:634
  15.5 7.8 %collective-permute-start.4 = (bf16[256,384]{1,0:T(8,128)(2,1)S(1)}, bf16[256,384]{1,0:T(8,128)(2,1)S(1)}, u32[]{:S(2)}, u32[]{:S(2)}) collective-permute-start(bf16[256,384]{1,0:T(8,128)(2,1)S(1)} %get-tuple-element.142.mix_own), channel_id=1, source_target_pairs={{0,1},{1,0},{2,3},{3,2},{4,5},{5,4},{6,7},{7,6},{8,9},{9,8},{10,11... | collective-permute-start | bytes 589832 | tf_op jit(solution)/shard_map/ppermute | solution.py:634
  15.6 11.4 %collective-permute-start.2 = (bf16[256,384]{1,0:T(8,128)(2,1)S(1)}, bf16[256,384]{1,0:T(8,128)(2,1)S(1)}, u32[]{:S(2)}, u32[]{:S(2)}) collective-permute-start(bf16[256,384]{1,0:T(8,128)(2,1)S(1)} %get-tuple-element.131.mix_own), channel_id=1, source_target_pairs={{0,1},{1,0},{2,3},{3,2},{4,5},{5,4},{6,7},{7,6},{8,9},{9,8},{10,11... | collective-permute-start | bytes 589832 | tf_op jit(solution)/shard_map/ppermute | solution.py:634
  26.6 12.1 %collective-permute-start.5 = (bf16[256,768]{1,0:T(8,128)(2,1)S(1)}, bf16[256,768]{1,0:T(8,128)(2,1)S(1)}, u32[]{:S(2)}, u32[]{:S(2)}) collective-permute-start(bf16[256,768]{1,0:T(8,128)(2,1)S(1)} %get-tuple-element.144.own_ref), channel_id=1, source_target_pairs={{0,1},{1,0},{2,3},{3,2},{4,5},{5,4},{6,7},{7,6},{8,9},{9,8},{10,11... | collective-permute-start | bytes 1179656 | tf_op jit(solution)/shard_map/ppermute | solution.py:634
  30.4 15.0 %collective-permute-start.3 = (bf16[256,768]{1,0:T(8,128)(2,1)S(1)}, bf16[256,768]{1,0:T(8,128)(2,1)S(1)}, u32[]{:S(2)}, u32[]{:S(2)}) collective-permute-start(bf16[256,768]{1,0:T(8,128)(2,1)S(1)} %get-tuple-element.140.own_ref), channel_id=1, source_target_pairs={{0,1},{1,0},{2,3},{3,2},{4,5},{5,4},{6,7},{7,6},{8,9},{9,8},{10,11... | collective-permute-start | bytes 1179656 | tf_op jit(solution)/shard_map/ppermute | solution.py:634
  45.7 3.8 %collective-permute-start.6 = (bf16[8,768]{1,0:T(8,128)(2,1)S(1)}, bf16[8,768]{1,0:T(8,128)(2,1)S(1)}, u32[]{:S(2)}, u32[]{:S(2)}) collective-permute-start(bf16[8,768]{1,0:T(8,128)(2,1)S(1)} %get-tuple-element.146), channel_id=1, source_target_pairs={{0,2},{2,0},{4,6},{6,4},{8,10},{10,8},{12,14},{14,12},{1,3},{3,1},... | collective-permute-start | bytes 36872 | tf_op jit(solution)/shard_map/ppermute | solution.py:634
  49.5 4.2 %collective-permute-start.7 = (bf16[16,768]{1,0:T(8,128)(2,1)S(1)}, bf16[16,768]{1,0:T(8,128)(2,1)S(1)}, u32[]{:S(2)}, u32[]{:S(2)}) collective-permute-start(bf16[16,768]{1,0:T(8,128)(2,1)S(1)} %get-tuple-element.257), channel_id=1, source_target_pairs={{0,4},{2,6},{4,0},{6,2},{8,12},{10,14},{12,8},{14,10},{1,5},{3,7},... | collective-permute-start | bytes 73736 | tf_op jit(solution)/shard_map/ppermute | solution.py:634
  51.1 7.5 %collective-permute-start.9 = (bf16[16,768]{1,0:T(8,128)(2,1)S(1)}, bf16[16,768]{1,0:T(8,128)(2,1)S(1)}, u32[]{:S(2)}, u32[]{:S(2)}) collective-permute-start(bf16[16,768]{1,0:T(8,128)(2,1)S(1)} %get-tuple-element.257), channel_id=1, source_target_pairs={{0,12},{2,14},{4,8},{6,10},{8,4},{10,6},{12,0},{14,2},{1,13},{3,15... | collective-permute-start | bytes 73736 | tf_op jit(solution)/shard_map/ppermute | solution.py:634
  53.6 5.0 %collective-permute-start.8 = (bf16[16,768]{1,0:T(8,128)(2,1)S(1)}, bf16[16,768]{1,0:T(8,128)(2,1)S(1)}, u32[]{:S(2)}, u32[]{:S(2)}) collective-permute-start(bf16[16,768]{1,0:T(8,128)(2,1)S(1)} %get-tuple-element.257), channel_id=1, source_target_pairs={{0,8},{2,10},{4,12},{6,14},{8,0},{10,2},{12,4},{14,6},{1,9},{3,11}... | collective-permute-start | bytes 73736 | tf_op jit(solution)/shard_map/ppermute | solution.py:634
  65.9 19.7 %collective-permute-start.11 = (bf16[512,768]{1,0:T(8,128)(2,1)S(1)}, bf16[512,768]{1,0:T(8,128)(2,1)S(1)}, u32[]{:S(2)}, u32[]{:S(2)}) collective-permute-start(bf16[512,768]{1,0:T(8,128)(2,1)S(1)} %get-tuple-element.158.refs_5_), channel_id=1, source_target_pairs={{0,1},{1,0},{2,3},{3,2},{4,5},{5,4},{6,7},{7,6},{8,9},{9,8},{10,11... | collective-permute-start | bytes 2359304 | tf_op jit(solution)/shard_map/ppermute | solution.py:634
  68.3 2.9 %collective-permute-start.12 = (bf16[384,384]{1,0:T(8,128)(2,1)S(1)}, bf16[384,384]{1,0:T(8,128)(2,1)S(1)}, u32[]{:S(2)}, u32[]{:S(2)}) collective-permute-start(bf16[384,384]{1,0:T(8,128)(2,1)S(1)} %get-tuple-element.164), channel_id=1, source_target_pairs={{0,16},{16,0},{1,17},{17,1},{2,18},{18,2},{3,19},{19,3},{4,20},{20... | collective-permute-start | bytes 884744 | tf_op jit(solution)/shard_map/ppermute | solution.py:634
  68.4 3.0 %collective-permute-start.13 = (bf16[384,384]{1,0:T(8,128)(2,1)S(1)}, bf16[384,384]{1,0:T(8,128)(2,1)S(1)}, u32[]{:S(2)}, u32[]{:S(2)}) collective-permute-start(bf16[384,384]{1,0:T(8,128)(2,1)S(1)} %get-tuple-element.165), channel_id=1, source_target_pairs={{0,16},{16,0},{1,17},{17,1},{2,18},{18,2},{3,19},{19,3},{4,20},{20... | collective-permute-start | bytes 884744 | tf_op jit(solution)/shard_map/ppermute | solution.py:634
  68.9 2.9 %collective-permute-start.14 = (bf16[384,384]{1,0:T(8,128)(2,1)S(1)}, bf16[384,384]{1,0:T(8,128)(2,1)S(1)}, u32[]{:S(2)}, u32[]{:S(2)}) collective-permute-start(bf16[384,384]{1,0:T(8,128)(2,1)S(1)} %get-tuple-element.166), channel_id=1, source_target_pairs={{0,16},{16,0},{1,17},{17,1},{2,18},{18,2},{3,19},{19,3},{4,20},{20... | collective-permute-start | bytes 884744 | tf_op jit(solution)/shard_map/ppermute | solution.py:634
  69.0 3.0 %collective-permute-start.15 = (bf16[384,384]{1,0:T(8,128)(2,1)S(1)}, bf16[384,384]{1,0:T(8,128)(2,1)S(1)}, u32[]{:S(2)}, u32[]{:S(2)}) collective-permute-start(bf16[384,384]{1,0:T(8,128)(2,1)S(1)} %get-tuple-element.167), channel_id=1, source_target_pairs={{0,16},{16,0},{1,17},{17,1},{2,18},{18,2},{3,19},{19,3},{4,20},{20... | collective-permute-start | bytes 884744 | tf_op jit(solution)/shard_map/ppermute | solution.py:634
  71.4 3.0 %collective-permute-start.17 = (bf16[384,384]{1,0:T(8,128)(2,1)S(1)}, bf16[384,384]{1,0:T(8,128)(2,1)S(1)}, u32[]{:S(2)}, u32[]{:S(2)}) collective-permute-start(bf16[384,384]{1,0:T(8,128)(2,1)S(1)} %get-tuple-element.174), channel_id=1, source_target_pairs={{0,16},{16,0},{1,17},{17,1},{2,18},{18,2},{3,19},{19,3},{4,20},{20... | collective-permute-start | bytes 884744 | tf_op jit(solution)/shard_map/ppermute | solution.py:634
  72.9 25.6 %collective-permute-start.23 = (bf16[192,1536]{1,0:T(8,128)(2,1)S(1)}, bf16[192,1536]{1,0:T(8,128)(2,1)S(1)}, u32[]{:S(2)}, u32[]{:S(2)}) collective-permute-start(bf16[192,1536]{1,0:T(8,128)(2,1)S(1)} %get-tuple-element.168), channel_id=1, source_target_pairs={{0,2},{2,0},{4,6},{6,4},{8,10},{10,8},{12,14},{14,12},{1,3},{3,1},... | collective-permute-start | bytes 1769480 | tf_op jit(solution)/shard_map/ppermute | solution.py:634
  85.6 14.6 %collective-permute-start.24 = (bf16[192,1536]{1,0:T(8,128)(2,1)S(1)}, bf16[192,1536]{1,0:T(8,128)(2,1)S(1)}, u32[]{:S(2)}, u32[]{:S(2)}) collective-permute-start(bf16[192,1536]{1,0:T(8,128)(2,1)S(1)} %get-tuple-element.194), channel_id=1, source_target_pairs={{0,4},{2,6},{4,0},{6,2},{8,12},{10,14},{12,8},{14,10},{1,5},{3,7},... | collective-permute-start | bytes 1769480 | tf_op jit(solution)/shard_map/ppermute | solution.py:634
  97.9 4.6 %collective-permute-start.20 = (bf16[384,384]{1,0:T(8,128)(2,1)S(1)}, bf16[384,384]{1,0:T(8,128)(2,1)S(1)}, u32[]{:S(2)}, u32[]{:S(2)}) collective-permute-start(bf16[384,384]{1,0:T(8,128)(2,1)S(1)} %get-tuple-element.185), channel_id=1, source_target_pairs={{0,16},{16,0},{1,17},{17,1},{2,18},{18,2},{3,19},{19,3},{4,20},{20... | collective-permute-start | bytes 884744 | tf_op jit(solution)/shard_map/ppermute | solution.py:634
  98.0 4.5 %collective-permute-start.21 = (bf16[384,384]{1,0:T(8,128)(2,1)S(1)}, bf16[384,384]{1,0:T(8,128)(2,1)S(1)}, u32[]{:S(2)}, u32[]{:S(2)}) collective-permute-start(bf16[384,384]{1,0:T(8,128)(2,1)S(1)} %get-tuple-element.186), channel_id=1, source_target_pairs={{0,16},{16,0},{1,17},{17,1},{2,18},{18,2},{3,19},{19,3},{4,20},{20... | collective-permute-start | bytes 884744 | tf_op jit(solution)/shard_map/ppermute | solution.py:634
  100.3 7.4 %collective-permute-start.26 = (bf16[96,1536]{1,0:T(8,128)(2,1)S(1)}, bf16[96,1536]{1,0:T(8,128)(2,1)S(1)}, u32[]{:S(2)}, u32[]{:S(2)}) collective-permute-start(bf16[96,1536]{1,0:T(8,128)(2,1)S(1)} %get-tuple-element.201), channel_id=1, source_target_pairs={{0,2},{2,0},{4,6},{6,4},{8,10},{10,8},{12,14},{14,12},{1,3},{3,1},... | collective-permute-start | bytes 884744 | tf_op jit(solution)/shard_map/ppermute | solution.py:634
  102.0 7.2 %collective-permute-start.25 = (bf16[96,1536]{1,0:T(8,128)(2,1)S(1)}, bf16[96,1536]{1,0:T(8,128)(2,1)S(1)}, u32[]{:S(2)}, u32[]{:S(2)}) collective-permute-start(bf16[96,1536]{1,0:T(8,128)(2,1)S(1)} %get-tuple-element.198), channel_id=1, source_target_pairs={{0,4},{2,6},{4,0},{6,2},{8,12},{10,14},{12,8},{14,10},{1,5},{3,7},... | collective-permute-start | bytes 884744 | tf_op jit(solution)/shard_map/ppermute | solution.py:634
  109.8 19.5 %collective-permute-start.35 = (bf16[512,768]{1,0:T(8,128)(2,1)S(1)}, bf16[512,768]{1,0:T(8,128)(2,1)S(1)}, u32[]{:S(2)}, u32[]{:S(2)}) collective-permute-start(bf16[512,768]{1,0:T(8,128)(2,1)S(1)} %get-tuple-element.226), channel_id=1, source_target_pairs={{0,1},{1,0},{2,3},{3,2},{4,5},{5,4},{6,7},{7,6},{8,9},{9,8},{10,11... | collective-permute-start | bytes 2359304 | tf_op jit(solution)/shard_map/ppermute | solution.py:634
  111.8 13.3 %collective-permute-start.30 = (bf16[192,896]{1,0:T(8,128)(2,1)S(1)}, bf16[192,896]{1,0:T(8,128)(2,1)S(1)}, u32[]{:S(2)}, u32[]{:S(2)}) collective-permute-start(bf16[192,896]{1,0:T(8,128)(2,1)S(1)} %get-tuple-element.217), channel_id=1, source_target_pairs={{0,4},{2,6},{4,0},{6,2},{8,12},{10,14},{12,8},{14,10},{1,5},{3,7},... | collective-permute-start | bytes 1032200 | tf_op jit(solution)/shard_map/ppermute | solution.py:634
  113.4 8.8 %collective-permute-start.22 = (bf16[192,768]{1,0:T(8,128)(2,1)S(1)}, bf16[192,768]{1,0:T(8,128)(2,1)S(1)}, u32[]{:S(2)}, u32[]{:S(2)}) collective-permute-start(bf16[192,768]{1,0:T(8,128)(2,1)S(1)} %get-tuple-element.188), channel_id=1, source_target_pairs={{0,2},{2,0},{4,6},{6,4},{8,10},{10,8},{12,14},{14,12},{1,3},{3,1},... | collective-permute-start | bytes 884744 | tf_op jit(solution)/shard_map/ppermute | solution.py:634
  113.9 10.3 %collective-permute-start.31 = (bf16[48,1536]{1,0:T(8,128)(2,1)S(1)}, bf16[48,1536]{1,0:T(8,128)(2,1)S(1)}, u32[]{:S(2)}, u32[]{:S(2)}) collective-permute-start(bf16[48,1536]{1,0:T(8,128)(2,1)S(1)} %get-tuple-element.211), channel_id=1, source_target_pairs={{0,8},{2,10},{4,12},{6,14},{8,0},{10,2},{12,4},{14,6},{1,9},{3,11}... | collective-permute-start | bytes 442376 | tf_op jit(solution)/shard_map/ppermute | solution.py:634
  125.2 10.1 %collective-permute-start.33 = (bf16[96,896]{1,0:T(8,128)(2,1)S(1)}, bf16[96,896]{1,0:T(8,128)(2,1)S(1)}, u32[]{:S(2)}, u32[]{:S(2)}) collective-permute-start(bf16[96,896]{1,0:T(8,128)(2,1)S(1)} %get-tuple-element.222), channel_id=1, source_target_pairs={{0,2},{2,0},{4,6},{6,4},{8,10},{10,8},{12,14},{14,12},{1,3},{3,1},... | collective-permute-start | bytes 516104 | tf_op jit(solution)/shard_map/ppermute | solution.py:634
  125.8 8.9 %collective-permute-start.34 = (bf16[48,1536]{1,0:T(8,128)(2,1)S(1)}, bf16[48,1536]{1,0:T(8,128)(2,1)S(1)}, u32[]{:S(2)}, u32[]{:S(2)}) collective-permute-start(bf16[48,1536]{1,0:T(8,128)(2,1)S(1)} %get-tuple-element.213), channel_id=1, source_target_pairs={{0,8},{2,10},{4,12},{6,14},{8,0},{10,2},{12,4},{14,6},{1,9},{3,11}... | collective-permute-start | bytes 442376 | tf_op jit(solution)/shard_map/ppermute | solution.py:634
  128.3 7.0 %collective-permute-start.32 = (bf16[96,768]{1,0:T(8,128)(2,1)S(1)}, bf16[96,768]{1,0:T(8,128)(2,1)S(1)}, u32[]{:S(2)}, u32[]{:S(2)}) collective-permute-start(bf16[96,768]{1,0:T(8,128)(2,1)S(1)} %get-tuple-element.219), channel_id=1, source_target_pairs={{0,4},{2,6},{4,0},{6,2},{8,12},{10,14},{12,8},{14,10},{1,5},{3,7},... | collective-permute-start | bytes 442376 | tf_op jit(solution)/shard_map/ppermute | solution.py:634
  135.4 10.4 %collective-permute-start.36 = (bf16[48,896]{1,0:T(8,128)(2,1)S(1)}, bf16[48,896]{1,0:T(8,128)(2,1)S(1)}, u32[]{:S(2)}, u32[]{:S(2)}) collective-permute-start(bf16[48,896]{1,0:T(8,128)(2,1)S(1)} %get-tuple-element.231), channel_id=1, source_target_pairs={{0,8},{2,10},{4,12},{6,14},{8,0},{10,2},{12,4},{14,6},{1,9},{3,11}... | collective-permute-start | bytes 258056 | tf_op jit(solution)/shard_map/ppermute | solution.py:634
  136.1 8.6 %collective-permute-start.39 = (bf16[48,768]{1,0:T(8,128)(2,1)S(1)}, bf16[48,768]{1,0:T(8,128)(2,1)S(1)}, u32[]{:S(2)}, u32[]{:S(2)}) collective-permute-start(bf16[48,768]{1,0:T(8,128)(2,1)S(1)} %get-tuple-element.236), channel_id=1, source_target_pairs={{0,8},{2,10},{4,12},{6,14},{8,0},{10,2},{12,4},{14,6},{1,9},{3,11}... | collective-permute-start | bytes 221192 | tf_op jit(solution)/shard_map/ppermute | solution.py:634
  138.5 7.3 %collective-permute-start.38 = (bf16[48,128]{1,0:T(8,128)(2,1)S(1)}, bf16[48,128]{1,0:T(8,128)(2,1)S(1)}, u32[]{:S(2)}, u32[]{:S(2)}) collective-permute-start(bf16[48,128]{1,0:T(8,128)(2,1)S(1)} %slice.7), channel_id=1, source_target_pairs={{0,9},{1,8},{2,11},{3,10},{4,13},{5,12},{6,15},{7,14},{8,1},{9,0},... | collective-permute-start | bytes 36872 | tf_op jit(solution)/shard_map/ppermute | solution.py:712
  140.0 5.7 %collective-permute-start.37 = (bf16[48,128]{1,0:T(8,128)(2,1)S(1)}, bf16[48,128]{1,0:T(8,128)(2,1)S(1)}, u32[]{:S(2)}, u32[]{:S(2)}) collective-permute-start(bf16[48,128]{1,0:T(8,128)(2,1)S(1)} %slice.6), channel_id=1, source_target_pairs={{0,1},{1,0},{2,3},{3,2},{4,5},{5,4},{6,7},{7,6},{8,9},{9,8},{10,11... | collective-permute-start | bytes 36872 | tf_op jit(solution)/shard_map/ppermute | solution.py:634
  (14 other events, 93.4 us)

commit v3 on v2

--- a/solution.py
+++ b/solution.py
@@ -12,7 +12,7 @@
 STRIP = 32
 STEP = 384
 LANES = 128
-FF_SENDS, QK_SENDS, VO_SENDS = 4, 2, 2
+DOWN_SENDS, UP_SENDS = 4, 8
 CHUNKS = 2
 
 eps = 1e-06
@@ -354,8 +354,8 @@
     ahead, refs = refs[:4], refs[4:]
     wo_ref, own_ref, dh2_ref, *refs = refs
     h1_refs, refs = refs[:CHUNKS], refs[CHUNKS:]
-    rec_ref, gain_ref, dh1_hbm, da_hbm, dmix_ref, dgain_ref, *refs = refs
-    held, (dh1_ref, da_ref, sems, out_sems) = refs[:4], refs[4:]
+    rec_ref, gain_ref, dh1_ref, da_hbm, dmix_ref, dgain_ref, *refs = refs
+    held, (da_ref, sems, out_sems) = refs[:4], refs[4:]
     copies = start_copies(sems, *zip(ahead, held))
     length, width = dh1_ref.shape
     size = length // CHUNKS
@@ -371,7 +371,7 @@
         dh1_ref[rows, :] = dh1
         da_ref[rows, :] = dh1.astype(bf16)
     dgain_ref[...] = dgain
-    copies += start_copies(out_sems, (dh1_ref, dh1_hbm), (da_ref, da_hbm))
+    copies += start_copies(out_sems, (da_ref, da_hbm))
     inner = dmix_ref.shape[1]
     own_at = pl.multiple_of(lax.axis_index("mp") * inner, inner)
     dmix_ref[...] = dot_nt(da_ref[...], wo_ref[pl.ds(own_at, inner), :]).astype(bf16)
@@ -379,15 +379,24 @@
         copy.wait()
 
 
-def attend_back_kernel(wq_hbm, wk_hbm, wv_hbm, n1_hbm, q_ref, k_ref, v_ref, probs_ref, *rest):
-    mixg_ref, ids_ref, grads_ref, biasg_ref, n1_ref, w_ref, *halves = rest[:-5]
-    ds_ref, skew_ref, rel_ref, dp_ref, sems = rest[-5:]
+def attend_back_kernel(
+    shard, wq_hbm, wk_hbm, wv_hbm, n1_hbm, mix_hbm, da_hbm, q_ref, k_ref, v_ref, probs_ref, mixg_ref, tok_ref,
+    ids_ref, ff_gain, final_gain,
+    part_ref, qk_other, qk_own, vo_other, vo_own,
+    grads_ref, n1_ref, w_ref, mix_ref, da_ref, all_ref, biasg_ref, ds_ref, skew_ref, rel_ref, dp_ref, sems,
+):
     length, inner = q_ref.shape
     blocks = length // BLOCK
     pairs = inner // BLOCK
     span = rel_ref.shape[1]
     later = start_copies(
-        sems, (wq_hbm, w_ref.at[0]), (wk_hbm, w_ref.at[1]), (wv_hbm, w_ref.at[2]), (n1_hbm, n1_ref)
+        sems,
+        (wq_hbm, w_ref.at[0]),
+        (wk_hbm, w_ref.at[1]),
+        (wv_hbm, w_ref.at[2]),
+        (n1_hbm, n1_ref),
+        (mix_hbm, mix_ref),
+        (da_hbm, da_ref),
     )
     low_lanes = lax.broadcasted_iota(jnp.int32, (BLOCK, BLOCK), 1) < BLOCK // 2
     low_all = lax.broadcasted_iota(jnp.int32, (length, BLOCK), 1) < BLOCK // 2
@@ -458,47 +467,42 @@
     biasg_ref[...] = total[:, : biasg_ref.shape[1]]
     for copy in later:
         copy.wait()
-    weight_products([n1_ref], [grads_ref.at[:, : 2 * inner]], halves[:-1], halves[-1])
-
-
-def project_back_kernel(shard, *refs):
-    mix_hbm, da_hbm, w_ref, tok_ref, n1_ref, grads_ref, bias_ref, ff_gain, final_gain, part_ref, part_hbm, *refs = refs
-    *others, small_ref, own_ref, all_ref, mix_ref, da_ref, sems = refs
-    copies = start_copies(sems, (mix_hbm, mix_ref), (da_hbm, da_ref))
-    length, width = part_ref.shape
-    inner = w_ref.shape[2]
     part_ref[...] = (
         dot_nt(grads_ref[:, :inner], w_ref[0])
         + dot_nt(grads_ref[:, inner : 2 * inner], w_ref[1])
         + dot_nt(grads_ref[:, 2 * inner :], w_ref[2])
     ).astype(bf16)
-    copies += start_copies(sems.at[2:], (part_ref, part_hbm))
+    weight_products([n1_ref], [grads_ref.at[:, : 2 * inner]], [qk_other], qk_own)
+    width = n1_ref.shape[1]
     dgain = jnp.zeros((1, width), f32)
     for at in range(0, length, STRIP):
         rows = slice(at, at + STRIP)
         x = tok_ref[rows, :].astype(f32)
         dgain += jnp.sum(x * inv_rms(x) * part_ref[rows, :].astype(f32), 0, keepdims=True)
-    weight_products([n1_ref], [grads_ref.at[:, 2 * inner :]], others, own_ref)
-    small_columns(shard, bias_ref, [dgain, ff_gain[...], final_gain[...]], all_ref)
+    weight_products([n1_ref], [grads_ref.at[:, 2 * inner :]], [vo_other], vo_own)
+    weight_products([da_ref], [mix_ref], [vo_other], vo_own, inner)
+    small_columns(shard, biasg_ref, [dgain, ff_gain[...], final_gain[...]], all_ref)
     tower_index = lax.axis_index("tower")
-    half = small_ref.shape[0]
-    small_ref[...] = all_ref[pl.ds(pl.multiple_of((1 - tower_index) * half, half), half), :].astype(bf16)
-    own_ref[:, 2 * inner :] = all_ref[pl.ds(pl.multiple_of(tower_index * half, half), half), :].astype(bf16)
-    for copy in copies:
-        copy.wait()
-    weight_products([da_ref], [mix_ref], others, own_ref, inner)
-
-
-def last_kernel(own_hbm, dh1_hbm, tok_ref, gain_ref, rec_ref, out_ref, own_ref, dh1_ref, sems):
-    copies = start_copies(sems, (own_hbm, own_ref), (dh1_hbm, dh1_ref))
+    half = width // 2
+    for which, out_ref in ((1 - tower_index, qk_other), (tower_index, qk_own)):
+        rows = pl.ds(pl.multiple_of(which * half, half), half)
+        out_ref[:, 2 * inner :] = all_ref[rows, :].astype(bf16)
+
+
+def last_kernel(tok_ref, own_ref, dh1_ref, gain_ref, rec_ref, out_hbm, out_ref, sems):
     gain = row_gain(gain_ref)
-    for copy in copies:
-        copy.wait()
-    for at in range(0, own_ref.shape[0], STRIP):
+    length = own_ref.shape[0]
+    copies = []
+    for at in range(0, length, STRIP):
         rows = slice(at, at + STRIP)
         x = tok_ref[rows, :].astype(f32)
         grad = own_ref[rows, :].astype(f32) + rec_ref[rows, :].astype(f32)
         out_ref[rows, :] = dh1_ref[rows, :] + norm_back(x, inv_rms(x), gain, grad)
+        if (at + STRIP) % BLOCK == 0:
+            done = pl.ds(at + STRIP - BLOCK, BLOCK)
+            copies += start_copies(sems.at[len(copies) :], (out_ref.at[done, :], out_hbm.at[done, :]))
+    for copy in copies:
+        copy.wait()
 
 
 def weight_products(lefts, rights, other_refs, own_ref, columns=0):
@@ -551,21 +555,30 @@
         out_ref[...] = own_ref[:, cols].astype(f32) + rec_ref[:, cols].astype(f32)
 
 
-def small_finish_kernel(own_ref, rec_ref, mp_own_ref, mp_rec_ref, *out_refs):
+def small_finish_kernel(own_ref, rec_ref, *out_refs):
     finish_kernel(1, own_ref, rec_ref, *out_refs[:-4])
     *gain_refs, bias_ref = out_refs[-4:]
     at = own_ref.shape[1] - LANES
     values = own_ref[:, at:].astype(f32) + rec_ref[:, at:].astype(f32)
-    others = mp_own_ref[...].astype(f32) + mp_rec_ref[...].astype(f32)
-    lane = lax.broadcasted_iota(jnp.int32, (1, LANES), 1)
-    values += jnp.where(lane == 0, others, 0.0)
-    eye = (lax.broadcasted_iota(jnp.int32, (LANES, LANES), 0) == lane).astype(f32)
+    eye = (
+        lax.broadcasted_iota(jnp.int32, (LANES, LANES), 0) == lax.broadcasted_iota(jnp.int32, (LANES, LANES), 1)
+    ).astype(f32)
     turned = lax.dot_general(
         eye, values, (((1,), (1,)), ((), ())), precision=highest, preferred_element_type=f32
     )
     for i, gain_ref in enumerate(gain_refs):
         gain_ref[...] = turned[i, :]
     bias_ref[...] = turned[3 : 3 + bias_ref.shape[0], : bias_ref.shape[1]]
+
+
+def gain_finish_kernel(own_ref, rec_ref, gain_own, gain_rec, *out_refs):
+    finish_kernel(1, own_ref, rec_ref, *out_refs[:-1])
+    out_refs[-1][...] = gain_own[...] + gain_rec[...]
+
+
+def two_finish_kernel(own_ref, rec_ref, own_too, rec_too, out_ref, out_too):
+    finish_kernel(1, own_ref, rec_ref, out_ref)
+    finish_kernel(1, own_too, rec_too, out_too)
 
 
 def split_kernel(shard, bit, low, sends, own_ref, *refs):
@@ -701,16 +714,24 @@
         rows = self.own.shape[0]
         outs = tuple(struct((rows, n), f32) for n in columns)
         outs += (struct((rows,), f32),) * 3 + (struct(bias_shape, f32),)
-        across = [(i, i ^ 1 ^ (2 * self.bit)) for i in range(2 * lax.axis_size("rows"))]
+        return whole(self.name + "_finish", small_finish_kernel, outs, self.own, *self.received)
+
+    def gain_finish(self, gain, *columns):
+        while self.order:
+            self.step()
+        outs = tuple(struct((self.own.shape[0], n), f32) for n in columns) + (struct(gain.shape, f32),)
         return whole(
-            self.name + "_finish",
-            small_finish_kernel,
-            outs,
-            self.own,
-            *self.received,
-            swap(self.own[:, -LANES:], "mp"),
-            lax.ppermute(self.send[0][:, -LANES:], ("rows", "mp"), across),
+            self.name + "_finish", gain_finish_kernel, outs, self.own, *self.received, gain, swap(gain, "mp")
         )
+
+
+def finish_two(first, second):
+    while first.order or second.order:
+        for scatter in (first, second):
+            if scatter.order:
+                scatter.step()
+    outs = tuple(struct(v.own.shape, f32) for v in (first, second))
+    return whole("finish", two_finish_kernel, outs, first.own, *first.received, second.own, *second.received)
 
 
 def tie(*values):
@@ -905,11 +926,15 @@
         in_vmem=2 + 2 * CHUNKS,
     )
     two_received = swap(two_part, "mp")
-    half_shapes = (struct((width // 2, hidden // FF_SENDS), bf16),) * FF_SENDS + (struct((width // 2, hidden), bf16),)
-    *halves, own = whole("down_weight", down_weight_kernel, half_shapes, ff_grad, *active, in_vmem=1 + CHUNKS)
+
+    def half_shapes(sends):
+        half = struct((width // 2, hidden), bf16)
+        return (struct((width // 2, hidden // sends), bf16),) * sends + (half,)
+
+    *halves, own = whole("down_weight", down_weight_kernel, half_shapes(DOWN_SENDS), ff_grad, *active, in_vmem=1 + CHUNKS)
     down_scatter = RowsScatter("down_split", shard, own, [swap(v, "tower") for v in halves])
-    *halves, own = whole("up_weight", up_weight_kernel, half_shapes, up_out_grad, *normed_two, in_vmem=1 + CHUNKS)
-    up_scatter = RowsScatter("up_split", shard, own, [swap(v, "tower") for v in halves], swapped=True)
+    *halves, own = whole("up_weight", up_weight_kernel, half_shapes(UP_SENDS), up_out_grad, *normed_two, in_vmem=1 + CHUNKS)
+    up_scatter = RowsScatter("up_split", shard, own, [swap(v, "tower") for v in halves])
     down_scatter.step()
     up_scatter.split()
     two_received, down_send, up_scatter.send = tie(
@@ -920,7 +945,7 @@
         "middle_back",
         middle_back_kernel,
         (
-            stored((length, width), f32),
+            fixed((length, width), f32),
             stored((length, width), bf16),
             fixed((length, inner), bf16),
             struct((1, width), f32),
@@ -938,122 +963,104 @@
         two_received,
         ff_gain,
         scratch=[
-            pltpu.VMEM((length, width), f32),
             pltpu.VMEM((length, width), bf16),
             pltpu.SemaphoreType.DMA((4,)),
-            pltpu.SemaphoreType.DMA((2,)),
+            pltpu.SemaphoreType.DMA((1,)),
         ],
         in_hbm=4,
         in_vmem=3 + CHUNKS,
     )
 
-    qkv_grads, bias_grad, normed_held, qkv_weight, *halves = whole(
+    down_scatter.received, mix_grad = tie(down_scatter.received, mix_grad)
+    down_scatter.split()
+    mix_grad = tie(mix_grad, down_scatter.send)[0]
+    down_scatter.exchange()
+
+    pair_shape = struct((width // 2, 2 * inner), bf16)
+    more_shape = struct((width // 2, 2 * inner + LANES), bf16)
+    one_part, first_other, first_own, second_other, second_own = whole(
         "attention_back",
-        attend_back_kernel,
+        functools.partial(attend_back_kernel, shard),
         (
-            fixed((length, 3 * inner), bf16),
-            struct((bucket_count, head_count), f32),
             fixed((length, width), bf16),
-            fixed((3, width, inner), bf16),
-        )
-        + (struct((width // 2, 2 * inner // QK_SENDS), bf16),) * QK_SENDS
-        + (struct((width // 2, 2 * inner), bf16),),
+            more_shape,
+            more_shape,
+            pair_shape,
+            pair_shape,
+        ),
         query_weight,
         key_weight,
         value_weight,
         normed_one,
+        mix_stored,
+        attn_grad,
         *heads_held,
         mix_grad,
+        tok,
         bucket_ids,
+        ff_gain_part,
+        final_gain_part,
         scratch=[
+            pltpu.VMEM((length, 3 * inner), bf16),
+            pltpu.VMEM((length, width), bf16),
+            pltpu.VMEM((3, width, inner), bf16),
+            pltpu.VMEM((length, inner), bf16),
+            pltpu.VMEM((length, width), bf16),
+            pltpu.VMEM((width, LANES), f32),
+            pltpu.VMEM((bucket_count, head_count), f32),
             pltpu.VMEM((2, length, length), bf16),
             pltpu.VMEM((2, BLOCK, span), f32),
             pltpu.VMEM((8, span), f32),
             pltpu.VMEM((2, BLOCK, length), f32),
-            pltpu.SemaphoreType.DMA((4,)),
+            pltpu.SemaphoreType.DMA((6,)),
         ],
-        in_hbm=4,
-        in_vmem=5,
-    )
-    first_scatter = RowsScatter("query_key_split", shard, halves[-1], [swap(v, "tower") for v in halves[:-1]])
-    qkv_grads, down_scatter.received, up_scatter.received = tie(
-        qkv_grads, down_scatter.received, up_scatter.received
-    )
-    down_scatter.split()
-    up_scatter.split()
-    first_scatter.split()
-    qkv_grads = tie(qkv_grads, down_scatter.send, up_scatter.send, first_scatter.send)[0]
-    down_scatter.exchange()
-    up_scatter.exchange()
-    first_scatter.exchange()
-    one_part, one_own, *halves, own = whole(
-        "project_back",
-        functools.partial(project_back_kernel, shard),
-        (struct((length, width), bf16), stored((length, width), bf16))
-        + (struct((width // 2, 2 * inner // VO_SENDS), bf16),) * VO_SENDS
-        + (struct((width // 2, LANES), bf16), struct((width // 2, 2 * inner + LANES), bf16)),
-        mix_stored,
-        attn_grad,
-        qkv_weight,
-        tok,
-        normed_held,
-        qkv_grads,
-        bias_grad,
-        ff_gain_part,
-        final_gain_part,
-        scratch=[
-            pltpu.VMEM((width, LANES), f32),
-            pltpu.VMEM((length, inner), bf16),
-            pltpu.VMEM((length, width), bf16),
-            pltpu.SemaphoreType.DMA((3,)),
-        ],
-        in_hbm=2,
-        in_vmem=4,
+        in_hbm=6,
+        in_vmem=6,
+        mib=24,
     )
     one_received = swap(one_part, "mp")
-    down_scatter.split()
-    up_scatter.split()
-    halves = tie(halves, down_scatter.send, up_scatter.send)[0]
-    down_scatter.exchange()
-    up_scatter.exchange()
-    second_scatter = RowsScatter(
-        "value_output_split", shard, own, [swap(v, "tower") for v in halves], swapped=True
-    )
+    first_other, second_other, down_scatter.received, up_scatter.received = tie(
+        first_other, second_other, down_scatter.received, up_scatter.received
+    )
+    first_scatter = RowsScatter("query_key_split", shard, first_own, [swap(first_other, "tower")])
+    second_scatter = RowsScatter("value_output_split", shard, second_own, [swap(second_other, "tower")])
+    up_scatter.step()
+    down_scatter.step()
+    first_scatter.received = tie(first_scatter.received, up_scatter.send, down_scatter.send)[0]
+    first_scatter.step()
     second_scatter.step()
+    first_scatter.received, up_scatter.received, down_scatter.received = tie(
+        first_scatter.received, up_scatter.received, down_scatter.received
+    )
+    first_scatter.step()
+    up_scatter.step()
     first_scatter.received, second_scatter.received, down_scatter.received = tie(
         first_scatter.received, second_scatter.received, down_scatter.received
     )
+    second_scatter.step()
     first_scatter.step()
-    second_scatter.step()
+    down_sum, up_sum = finish_two(down_scatter, up_scatter)
     tokens_grad = whole(
         "last",
         last_kernel,
-        struct((length, width), f32),
-        one_own,
+        stored((length, width), f32),
+        tok,
+        one_part,
         hidden_one_grad,
-        tok,
         attn_gain,
         one_received,
-        scratch=[
-            pltpu.VMEM((length, width), bf16),
-            pltpu.VMEM((length, width), f32),
-            pltpu.SemaphoreType.DMA((2,)),
-        ],
-        in_hbm=2,
-        in_vmem=1,
-    )
-    first_scatter.received, second_scatter.received, down_scatter.received, up_scatter.received, tokens_grad = tie(
-        first_scatter.received, second_scatter.received, down_scatter.received, up_scatter.received, tokens_grad
-    )
-    first_scatter.step()
+        scratch=[pltpu.VMEM((length, width), f32), pltpu.SemaphoreType.DMA((length // BLOCK,))],
+        in_vmem=3,
+    )
+    second_scatter.received, first_scatter.received, tokens_grad, down_sum, up_sum = tie(
+        second_scatter.received, first_scatter.received, tokens_grad, down_sum, up_sum
+    )
     second_scatter.step()
-    (down_sum,) = down_scatter.finish(hidden)
-    (up_sum,) = up_scatter.finish(hidden)
     bias_pieces = -(-bucket_count // shard)
-    value_sum, output_sum, attn_gain_sum, ff_gain_sum, final_gain_sum, turned = second_scatter.small_finish(
+    query_sum, key_sum, attn_gain_sum, ff_gain_sum, final_gain_sum, turned = first_scatter.small_finish(
         (head_count * bias_pieces, min(shard, bucket_count)), inner, inner
     )
-    query_sum, key_sum = first_scatter.finish(inner, inner)
+    value_sum, output_sum, attn_gain_sum = second_scatter.gain_finish(attn_gain_sum, inner, inner)
     bias_rows = [turned[g * head_count : (g + 1) * head_count, :] for g in range(bias_pieces)]
     bias_total = jnp.concatenate(bias_rows, 1)[:, :bucket_count].T
     return (

time: 147 us -> 139 us (0.946)
  Pallas kernels: 54.6 us -> 49.8 us
  waiting for transfers between devices: 58 us -> 55.7 us
    pallas_call x30 -> x28, Pallas kernels: 54.6 us -> 49.8 us  [whole(): pl.pallas_call(kernel, out_shape=out_shapes, in_specs=[hbm] * in_hbm + [v...]
    ppermute x39 -> x40, waiting for transfers between devices: 57.6 us -> 55.7 us  [swap(): return lax.ppermute(values, axis, [(i, i ^ bit) for i in range(count)])]
    ppermute x1 -> x0, starting transfers between devices: 1.59 us -> none  [small_finish(): lax.ppermute(self.send[0][:, -LANES:], ('rows', 'mp'), across)]
    ppermute x39 -> x40, starting transfers between devices: 30.3 us -> 31.3 us  [swap(): return lax.ppermute(values, axis, [(i, i ^ bit) for i in range(count)])]
  transfers between devices with their start and end apart: 40 -> 40, of which waited for: 21 -> 21; matrix products, arithmetic and copies ran while one was open for 0% -> 0% of each run, Pallas kernels for 32% -> 31%
where the time goes in v3:
time: 139 us
  waiting for transfers between devices  55.7 us (40%)
  Pallas kernels  49.8 us (36%)
  starting transfers between devices  31.3 us (23%)
    ppermute x40, waiting for transfers between devices, swap(): return lax.ppermute(values, axis, [(i, i ^ bit) for i in range(count)])  55.7 us
    pallas_call x28, Pallas kernels, whole(): pl.pallas_call(kernel, out_shape=out_shapes, in_specs=[hbm] * in_hbm + [v...  49.8 us
    ppermute x40, starting transfers between devices, swap(): return lax.ppermute(values, axis, [(i, i ^ bit) for i in range(count)])  31.3 us
  transfers between devices with their start and end apart: 40, of which 21 were waited for; matrix products, arithmetic and copies ran while one was open for 0% of the time, Pallas kernels for 31%

profile of v3, /device:TPU:0, one launch (start us, length us, event | category | flops | bytes accessed | tf_op | source)
XLA Modules:
  0.0 138.8 jit_solution(6737596688516452048)
XLA Ops:
  1.6 3.0 %collective-permute-start = (bf16[192,768]{1,0:T(8,128)(2,1)S(1)}, bf16[192,768]{1,0:T(8,128)(2,1)S(1)}, u32[]{:S(2)}, u32[]{:S(2)}) collective-permute-start(bf16[192,768]{1,0:T(8,128)(2,1)S(1)} %constant_dynamic-slice_fusion), channel_id=1, source_target_pairs={{0,1},{1,0},{2,3},{3,2},{4,5},{5,4},{6,7},{7,6},{8,9},{9,8},{10,11... | collective-permute-start | bytes 884744 | tf_op jit(solution)/shard_map/ppermute | solution.py:647
  4.7 10.7 %attention.1 = (bf16[512,768]{1,0:T(8,128)(2,1)}, bf16[512,384]{1,0:T(8,128)(2,1)}, bf16[512,384]{1,0:T(8,128)(2,1)}, bf16[512,384]{1,0:T(8,128)(2,1)}, bf16[6,5...) custom-call(bf16[512,768]{1,0:T(8,128)(2,1)} %bitcast.13, ...), custom_call_target="tpu_custom_call" | custom-call | flops 1 | bytes 1 | tf_op jit(solution)/shard_map/attention/pallas_call | solution.py:627
  15.6 2.0 %collective-permute-start.2 = (bf16[256,384]{1,0:T(8,128)(2,1)S(1)}, bf16[256,384]{1,0:T(8,128)(2,1)S(1)}, u32[]{:S(2)}, u32[]{:S(2)}) collective-permute-start(bf16[256,384]{1,0:T(8,128)(2,1)S(1)} %get-tuple-element.134.mix_own), channel_id=1, source_target_pairs={{0,1},{1,0},{2,3},{3,2},{4,5},{5,4},{6,7},{7,6},{8,9},{9,8},{10,11... | collective-permute-start | bytes 589832 | tf_op jit(solution)/shard_map/ppermute | solution.py:647
  17.6 3.1 %load.1 = (bf16[768,768]{1,0:T(8,128)(2,1)S(1)}, bf16[768,1536]{1,0:T(8,128)(2,1)S(1)}, bf16[1536,768]{1,0:T(8,128)(2,1)S(1)}, bf16[768,768]{1,0:T(8,128)(2,1)S(1)}) custom-call(bf16[384,768]{1,0:T(8,128)(2,1)} %wo_hbm.1, bf16[768,1536]{1,0:T(8,128)(2,1)} %up_hbm.1, bf16[1536,768]{1,0:T(8,128)(2,1)} %down_hbm.1, bf16[768,768]{1,0:T(8,128)(2,1)} %proj_hbm.1, ...), custom_call_target="tpu_custom_call" | custom-call | flops 1 | bytes 1 | tf_op jit(solution)/shard_map/load/pallas_call | solution.py:627
  20.7 2.6 %collective-permute-done.4.mix_other = bf16[256,384]{1,0:T(8,128)(2,1)S(1)} collective-permute-done((bf16[256,384]{1,0:T(8,128)(2,1)S(1)}, bf16[256,384]{1,0:T(8,128)(2,1)S(1)}, u32[]{:S(2)}, u32[]{:S(2)}) %collective-permute-start.4) | collective-permute-done | bytes 196640 | tf_op jit(solution)/shard_map/ppermute | solution.py:647
  23.3 3.3 %feed_forward.3 = (f32[256,768]{1,0:T(8,128)S(1)}, bf16[256,768]{1,0:T(8,128)(2,1)S(1)}, bf16[256,1536]{1,0:T(8,128)(2,1)S(1)}, f32[256,1536]{1,0:T(8,128)S(1)}, bf16[256,768]{1,0:T(8,128)(2,1)S(1)}) custom-call(bf16[512,768]{1,0:T(8,128)(2,1)S(1)} %get-tuple-element.138.tok_ref, bf16[768,768]{1,0:T(8,128)(2,1)S(1)} %get-tuple-element.139.wo_ref.refs_4_, ...), custom_call_target="tpu_custom_call" | custom-call | flops 1 | bytes 1 | tf_op jit(solution)/shard_map/feed_forward/pallas_call | solution.py:627
  27.0 3.3 %feed_forward.2 = (f32[256,768]{1,0:T(8,128)S(1)}, bf16[256,768]{1,0:T(8,128)(2,1)S(1)}, bf16[256,1536]{1,0:T(8,128)(2,1)S(1)}, f32[256,1536]{1,0:T(8,128)S(1)}, bf16[256,768]{1,0:T(8,128)(2,1)S(1)}) custom-call(bf16[512,768]{1,0:T(8,128)(2,1)S(1)} %get-tuple-element.138.tok_ref, bf16[768,768]{1,0:T(8,128)(2,1)S(1)} %get-tuple-element.139.wo_ref.refs_4_, ...), custom_call_target="tpu_custom_call" | custom-call | flops 1 | bytes 1 | tf_op jit(solution)/shard_map/feed_forward/pallas_call | solution.py:627
  30.3 1.7 %collective-permute-start.3 = (bf16[256,768]{1,0:T(8,128)(2,1)S(1)}, bf16[256,768]{1,0:T(8,128)(2,1)S(1)}, u32[]{:S(2)}, u32[]{:S(2)}) collective-permute-start(bf16[256,768]{1,0:T(8,128)(2,1)S(1)} %get-tuple-element.143.own_ref), channel_id=1, source_target_pairs={{0,1},{1,0},{2,3},{3,2},{4,5},{5,4},{6,7},{7,6},{8,9},{9,8},{10,11... | collective-permute-start | bytes 1179656 | tf_op jit(solution)/shard_map/ppermute | solution.py:647
  32.0 6.7 %collective-permute-done.5.rec_ref = bf16[256,768]{1,0:T(8,128)(2,1)S(1)} collective-permute-done((bf16[256,768]{1,0:T(8,128)(2,1)S(1)}, bf16[256,768]{1,0:T(8,128)(2,1)S(1)}, u32[]{:S(2)}, u32[]{:S(2)}) %collective-permute-start.5) | collective-permute-done | bytes 393248 | tf_op jit(solution)/shard_map/ppermute | solution.py:647
  39.1 6.2 %collective-permute-done.3.rec_ref = bf16[256,768]{1,0:T(8,128)(2,1)S(1)} collective-permute-done((bf16[256,768]{1,0:T(8,128)(2,1)S(1)}, bf16[256,768]{1,0:T(8,128)(2,1)S(1)}, u32[]{:S(2)}, u32[]{:S(2)}) %collective-permute-start.3) | collective-permute-done | bytes 393248 | tf_op jit(solution)/shard_map/ppermute | solution.py:647
  45.7 1.6 %collective-permute-start.6 = (bf16[8,768]{1,0:T(8,128)(2,1)S(1)}, bf16[8,768]{1,0:T(8,128)(2,1)S(1)}, u32[]{:S(2)}, u32[]{:S(2)}) collective-permute-start(bf16[8,768]{1,0:T(8,128)(2,1)S(1)} %get-tuple-element.149), channel_id=1, source_target_pairs={{0,2},{2,0},{4,6},{6,4},{8,10},{10,8},{12,14},{14,12},{1,3},{3,1},... | collective-permute-start | bytes 36872 | tf_op jit(solution)/shard_map/ppermute | solution.py:647
  47.3 2.2 %collective-permute-done.6 = bf16[8,768]{1,0:T(8,128)(2,1)S(1)} collective-permute-done((bf16[8,768]{1,0:T(8,128)(2,1)S(1)}, bf16[8,768]{1,0:T(8,128)(2,1)S(1)}, u32[]{:S(2)}, u32[]{:S(2)}) %collective-permute-start.6) | collective-permute-done | bytes 12320 | tf_op jit(solution)/shard_map/ppermute | solution.py:647
  49.5 1.6 %collective-permute-start.7 = (bf16[16,768]{1,0:T(8,128)(2,1)S(1)}, bf16[16,768]{1,0:T(8,128)(2,1)S(1)}, u32[]{:S(2)}, u32[]{:S(2)}) collective-permute-start(bf16[16,768]{1,0:T(8,128)(2,1)S(1)} %get-tuple-element.263), channel_id=1, source_target_pairs={{0,4},{2,6},{4,0},{6,2},{8,12},{10,14},{12,8},{14,10},{1,5},{3,7},... | collective-permute-start | bytes 73736 | tf_op jit(solution)/shard_map/ppermute | solution.py:647
  51.0 2.5 %collective-permute-start.9 = (bf16[16,768]{1,0:T(8,128)(2,1)S(1)}, bf16[16,768]{1,0:T(8,128)(2,1)S(1)}, u32[]{:S(2)}, u32[]{:S(2)}) collective-permute-start(bf16[16,768]{1,0:T(8,128)(2,1)S(1)} %get-tuple-element.263), channel_id=1, source_target_pairs={{0,12},{2,14},{4,8},{6,10},{8,4},{10,6},{12,0},{14,2},{1,13},{3,15... | collective-permute-start | bytes 73736 | tf_op jit(solution)/shard_map/ppermute | solution.py:647
  53.6 4.9 %collective-permute-done.8 = bf16[16,768]{1,0:T(8,128)(2,1)S(1)} collective-permute-done((bf16[16,768]{1,0:T(8,128)(2,1)S(1)}, bf16[16,768]{1,0:T(8,128)(2,1)S(1)}, u32[]{:S(2)}, u32[]{:S(2)}) %collective-permute-start.8) | collective-permute-done | bytes 24608 | tf_op jit(solution)/shard_map/ppermute | solution.py:647
  59.9 2.0 %contrast.1 = (f32[1,1]{1,0:T(1,128)}, f32[48,768]{1,0:T(8,128)}, f32[8,768]{1,0:T(8,128)S(1)}) custom-call(bf16[768,768]{1,0:T(8,128)(2,1)S(1)} %get-tuple-element.137.proj_ref, bf16[128,768]{1,0:T(8,128)(2,1)S(1)} %constant_dynamic-update-slice_fusion.7.gathered_ref, s32[64]{0:T(128)S(1)} %copy-done.5), custom_call_target="tpu_custom_call" | custom-call | flops 1 | bytes 1 | tf_op jit(solution)/shard_map/contrast/pallas_call | solution.py:627
  61.9 3.9 %feed_forward_back.1 = (bf16[512,768]{1,0:T(8,128)(2,1)S(1)}, f32[512,768]{1,0:T(8,128)S(1)}, bf16[512,768]{1,0:T(8,128)(2,1)S(1)}, bf16[512,1536]{1,0:T(8,128)(2,1)S(1)}, f32[1,768]{1,0:T(1,128)S(1)}) custom-call(bf16[1536,768]{1,0:T(8,128)(2,1)S(1)} %get-tuple-element.141.down_ref, bf16[768,1536]{1,0:T(8,128)(2,1)S(1)} %get-tuple-element.140.up_ref, ...), custom_call_target="tpu_custom_call" | custom-call | flops 1 | bytes 1 | tf_op jit(solution)/shard_map/feed_forward_back/pallas_call | solution.py:627
  66.4 1.8 %down_weight.1 = (bf16[384,384]{1,0:T(8,128)(2,1)S(1)}, bf16[384,384]{1,0:T(8,128)(2,1)S(1)}, bf16[384,384]{1,0:T(8,128)(2,1)S(1)}, bf16[384,384]{1,0:T(8,128)(2,1)S(1)}, bf16[384,1536]{1,0:T(8,128)(2,1)S(1)}) custom-call(bf16[512,768]{1,0:T(8,128)(2,1)S(1)} %get-tuple-element.164.df_ref, bf16[256,1536]{1,0:T(8,128)(2,1)S(1)} %get-tuple-element.165.refs_0_, ...), custom_call_target="tpu_custom_call" | custom-call | flops 1 | bytes 1 | tf_op jit(solution)/shard_map/down_weight/pallas_call | solution.py:627
  69.3 1.8 %up_weight.1 = (bf16[384,192]{1,0:T(8,128)(2,1)S(1)}, bf16[384,192]{1,0:T(8,128)(2,1)S(1)}, bf16[384,192]{1,0:T(8,128)(2,1)S(1)}, bf16[384,192]{1,0:T(8,128)(2,1...) custom-call(bf16[512,1536]{1,0:T(8,128)(2,1)S(1)} %get-tuple-element, ...), custom_call_target="tpu_custom_call" | custom-call | flops 1 | bytes 1 | tf_op jit(solution)/shard_map/up_weight/pallas_call | solution.py:627
  73.0 1.5 %collective-permute-start.24 = (bf16[192,1536]{1,0:T(8,128)(2,1)S(1)}, bf16[192,1536]{1,0:T(8,128)(2,1)S(1)}, u32[]{:S(2)}, u32[]{:S(2)}) collective-permute-start(bf16[192,1536]{1,0:T(8,128)(2,1)S(1)} %get-tuple-element.172), channel_id=1, source_target_pairs={{0,2},{2,0},{4,6},{6,4},{8,10},{10,8},{12,14},{14,12},{1,3},{3,1},... | collective-permute-start | bytes 1769480 | tf_op jit(solution)/shard_map/ppermute | solution.py:647
  77.0 8.5 %collective-permute-done.11.refs_9_ = bf16[512,768]{1,0:T(8,128)(2,1)S(1)} collective-permute-done((bf16[512,768]{1,0:T(8,128)(2,1)S(1)}, bf16[512,768]{1,0:T(8,128)(2,1)S(1)}, u32[]{:S(2)}, u32[]{:S(2)}) %collective-permute-start.11) | collective-permute-done | bytes 786464 | tf_op jit(solution)/shard_map/ppermute | solution.py:647
  85.5 1.5 %collective-permute-start.26 = (bf16[192,1536]{1,0:T(8,128)(2,1)S(1)}, bf16[192,1536]{1,0:T(8,128)(2,1)S(1)}, u32[]{:S(2)}, u32[]{:S(2)}) collective-permute-start(bf16[192,1536]{1,0:T(8,128)(2,1)S(1)} %get-tuple-element.203), channel_id=1, source_target_pairs={{0,2},{2,0},{4,6},{6,4},{8,10},{10,8},{12,14},{14,12},{1,3},{3,1},... | collective-permute-start | bytes 1769480 | tf_op jit(solution)/shard_map/ppermute | solution.py:647
  87.0 2.6 %middle_back.1 = (f32[512,768]{1,0:T(8,128)S(1)}, bf16[512,768]{1,0:T(8,128)(2,1)}, bf16[512,384]{1,0:T(8,128)(2,1)S(1)}, f32[1,768]{1,0:T(1,128)S(1)}, bf16[512...) custom-call(bf16[512,384]{1,0:T(8,128)(2,1)} %get-tuple-element.153., ...), custom_call_target="tpu_custom_call" | custom-call | flops 1 | bytes 1 | tf_op jit(solution)/shard_map/middle_back/pallas_call | solution.py:627
  90.3 10.7 %attention_back.1 = (bf16[512,768]{1,0:T(8,128)(2,1)S(1)}, bf16[384,896]{1,0:T(8,128)(2,1)S(1)}, bf16[384,896]{1,0:T(8,128)(2,1)S(1)}, bf16[384,768]{1,0:T(8,128)(2,1)S(1)}, bf16[384,768]{1,0:T(8,128)(2,1)S(1)}) custom-call(bf16[768,384]{1,0:T(8,128)(2,1)} %wq_hbm.3, bf16[768,384]{1,0:T(8,128)(2,1)} %wk_hbm.3, bf16[768,384]{1,0:T(8,128)(2,1)} %wv_hbm.3, ...), custom_call_target="tpu_custom_call" | custom-call | flops 1 | bytes 1 | tf_op jit(solution)/shard_map/attention_back/pallas_call | solution.py:627
  101.6 1.5 %collective-permute-start.36 = (bf16[512,768]{1,0:T(8,128)(2,1)S(1)}, bf16[512,768]{1,0:T(8,128)(2,1)S(1)}, u32[]{:S(2)}, u32[]{:S(2)}) collective-permute-start(bf16[512,768]{1,0:T(8,128)(2,1)S(1)} %get-tuple-element.226.own_ref), channel_id=1, source_target_pairs={{0,1},{1,0},{2,3},{3,2},{4,5},{5,4},{6,7},{7,6},{8,9},{9,8},{10,11... | collective-permute-start | bytes 2359304 | tf_op jit(solution)/shard_map/ppermute | solution.py:647
  103.6 1.5 %collective-permute-start.29 = (bf16[192,896]{1,0:T(8,128)(2,1)S(1)}, bf16[192,896]{1,0:T(8,128)(2,1)S(1)}, u32[]{:S(2)}, u32[]{:S(2)}) collective-permute-start(bf16[192,896]{1,0:T(8,128)(2,1)S(1)} %get-tuple-element.216), channel_id=1, source_target_pairs={{0,2},{2,0},{4,6},{6,4},{8,10},{10,8},{12,14},{14,12},{1,3},{3,1},... | collective-permute-start | bytes 1032200 | tf_op jit(solution)/shard_map/ppermute | solution.py:647
  107.6 7.9 %collective-permute-done.31.rec_ref = bf16[48,1536]{1,0:T(8,128)(2,1)S(1)} collective-permute-done((bf16[48,1536]{1,0:T(8,128)(2,1)S(1)}, bf16[48,1536]{1,0:T(8,128)(2,1)S(1)}, u32[]{:S(2)}, u32[]{:S(2)}) %collective-permute-start.31) | collective-permute-done | bytes 147488 | tf_op jit(solution)/shard_map/ppermute | solution.py:647
  119.9 5.4 %collective-permute-done.32.refs_0_ = bf16[96,896]{1,0:T(8,128)(2,1)S(1)} collective-permute-done((bf16[96,896]{1,0:T(8,128)(2,1)S(1)}, bf16[96,896]{1,0:T(8,128)(2,1)S(1)}, u32[]{:S(2)}, u32[]{:S(2)}) %collective-permute-start.32) | collective-permute-done | bytes 172064 | tf_op jit(solution)/shard_map/ppermute | solution.py:647
  126.5 1.7 %last.1 = f32[512,768]{1,0:T(8,128)} custom-call(bf16[512,768]{1,0:T(8,128)(2,1)S(1)} %get-tuple-element.138.tok_ref, bf16[512,768]{1,0:T(8,128)(2,1)S(1)} %get-tuple-element.226.own_ref, f32[512,768]{1,0:T(8,128)S(1)} %get-tuple-element.227.dh1_ref, f32[768]{0:T(1024)S(1)} %copy-done.4, bf16[512,768]{1,0:T(8,128)(2,1)S(1)} %collective-permute-done.36.rec_ref), custom_call_target="tpu_custom_call" | custom-call | flops 1 | bytes 1 | tf_op jit(solution)/shard_map/last/pallas_call | solution.py:627
  129.1 2.1 %collective-permute-done.35.rec_ref = bf16[48,896]{1,0:T(8,128)(2,1)S(1)} collective-permute-done((bf16[48,896]{1,0:T(8,128)(2,1)S(1)}, bf16[48,896]{1,0:T(8,128)(2,1)S(1)}, u32[]{:S(2)}, u32[]{:S(2)}) %collective-permute-start.35) | collective-permute-done | bytes 86048 | tf_op jit(solution)/shard_map/ppermute | solution.py:647
  133.5 1.7 %collective-permute-start.39 = (f32[48]{0:T(128)S(1)}, f32[48]{0:T(128)S(1)}, u32[]{:S(2)}, u32[]{:S(2)}) collective-permute-start(f32[48]{0:T(128)S(1)} %get-tuple-element.243.gain_own), channel_id=1, source_target_pairs={{0,1},{1,0},{2,3},{3,2},{4,5},{5,4},{6,7},{7,6},{8,9},{9,8},{10,11... | collective-permute-start | bytes 584 | tf_op jit(solution)/shard_map/ppermute | solution.py:647
  135.2 1.9 %collective-permute-done.39.gain_rec = f32[48]{0:T(128)S(1)} collective-permute-done((f32[48]{0:T(128)S(1)}, f32[48]{0:T(128)S(1)}, u32[]{:S(2)}, u32[]{:S(2)}) %collective-permute-start.39) | collective-permute-done | bytes 224 | tf_op jit(solution)/shard_map/ppermute | solution.py:647
  (95 shorter events, 24.6 us)
Async XLA Ops:
  1.6 13.7 %collective-permute-start = (bf16[192,768]{1,0:T(8,128)(2,1)S(1)}, bf16[192,768]{1,0:T(8,128)(2,1)S(1)}, u32[]{:S(2)}, u32[]{:S(2)}) collective-permute-start(bf16[192,768]{1,0:T(8,128)(2,1)S(1)} %constant_dynamic-slice_fusion), channel_id=1, source_target_pairs={{0,1},{1,0},{2,3},{3,2},{4,5},{5,4},{6,7},{7,6},{8,9},{9,8},{10,11... | collective-permute-start | bytes 884744 | tf_op jit(solution)/shard_map/ppermute | solution.py:647
  15.5 7.8 %collective-permute-start.4 = (bf16[256,384]{1,0:T(8,128)(2,1)S(1)}, bf16[256,384]{1,0:T(8,128)(2,1)S(1)}, u32[]{:S(2)}, u32[]{:S(2)}) collective-permute-start(bf16[256,384]{1,0:T(8,128)(2,1)S(1)} %get-tuple-element.145.mix_own), channel_id=1, source_target_pairs={{0,1},{1,0},{2,3},{3,2},{4,5},{5,4},{6,7},{7,6},{8,9},{9,8},{10,11... | collective-permute-start | bytes 589832 | tf_op jit(solution)/shard_map/ppermute | solution.py:647
  15.6 11.4 %collective-permute-start.2 = (bf16[256,384]{1,0:T(8,128)(2,1)S(1)}, bf16[256,384]{1,0:T(8,128)(2,1)S(1)}, u32[]{:S(2)}, u32[]{:S(2)}) collective-permute-start(bf16[256,384]{1,0:T(8,128)(2,1)S(1)} %get-tuple-element.134.mix_own), channel_id=1, source_target_pairs={{0,1},{1,0},{2,3},{3,2},{4,5},{5,4},{6,7},{7,6},{8,9},{9,8},{10,11... | collective-permute-start | bytes 589832 | tf_op jit(solution)/shard_map/ppermute | solution.py:647
  26.6 12.1 %collective-permute-start.5 = (bf16[256,768]{1,0:T(8,128)(2,1)S(1)}, bf16[256,768]{1,0:T(8,128)(2,1)S(1)}, u32[]{:S(2)}, u32[]{:S(2)}) collective-permute-start(bf16[256,768]{1,0:T(8,128)(2,1)S(1)} %get-tuple-element.147.own_ref), channel_id=1, source_target_pairs={{0,1},{1,0},{2,3},{3,2},{4,5},{5,4},{6,7},{7,6},{8,9},{9,8},{10,11... | collective-permute-start | bytes 1179656 | tf_op jit(solution)/shard_map/ppermute | solution.py:647
  30.3 15.0 %collective-permute-start.3 = (bf16[256,768]{1,0:T(8,128)(2,1)S(1)}, bf16[256,768]{1,0:T(8,128)(2,1)S(1)}, u32[]{:S(2)}, u32[]{:S(2)}) collective-permute-start(bf16[256,768]{1,0:T(8,128)(2,1)S(1)} %get-tuple-element.143.own_ref), channel_id=1, source_target_pairs={{0,1},{1,0},{2,3},{3,2},{4,5},{5,4},{6,7},{7,6},{8,9},{9,8},{10,11... | collective-permute-start | bytes 1179656 | tf_op jit(solution)/shard_map/ppermute | solution.py:647
  45.7 3.8 %collective-permute-start.6 = (bf16[8,768]{1,0:T(8,128)(2,1)S(1)}, bf16[8,768]{1,0:T(8,128)(2,1)S(1)}, u32[]{:S(2)}, u32[]{:S(2)}) collective-permute-start(bf16[8,768]{1,0:T(8,128)(2,1)S(1)} %get-tuple-element.149), channel_id=1, source_target_pairs={{0,2},{2,0},{4,6},{6,4},{8,10},{10,8},{12,14},{14,12},{1,3},{3,1},... | collective-permute-start | bytes 36872 | tf_op jit(solution)/shard_map/ppermute | solution.py:647
  49.5 4.2 %collective-permute-start.7 = (bf16[16,768]{1,0:T(8,128)(2,1)S(1)}, bf16[16,768]{1,0:T(8,128)(2,1)S(1)}, u32[]{:S(2)}, u32[]{:S(2)}) collective-permute-start(bf16[16,768]{1,0:T(8,128)(2,1)S(1)} %get-tuple-element.263), channel_id=1, source_target_pairs={{0,4},{2,6},{4,0},{6,2},{8,12},{10,14},{12,8},{14,10},{1,5},{3,7},... | collective-permute-start | bytes 73736 | tf_op jit(solution)/shard_map/ppermute | solution.py:647
  51.0 7.5 %collective-permute-start.9 = (bf16[16,768]{1,0:T(8,128)(2,1)S(1)}, bf16[16,768]{1,0:T(8,128)(2,1)S(1)}, u32[]{:S(2)}, u32[]{:S(2)}) collective-permute-start(bf16[16,768]{1,0:T(8,128)(2,1)S(1)} %get-tuple-element.263), channel_id=1, source_target_pairs={{0,12},{2,14},{4,8},{6,10},{8,4},{10,6},{12,0},{14,2},{1,13},{3,15... | collective-permute-start | bytes 73736 | tf_op jit(solution)/shard_map/ppermute | solution.py:647
  53.5 5.0 %collective-permute-start.8 = (bf16[16,768]{1,0:T(8,128)(2,1)S(1)}, bf16[16,768]{1,0:T(8,128)(2,1)S(1)}, u32[]{:S(2)}, u32[]{:S(2)}) collective-permute-start(bf16[16,768]{1,0:T(8,128)(2,1)S(1)} %get-tuple-element.263), channel_id=1, source_target_pairs={{0,8},{2,10},{4,12},{6,14},{8,0},{10,2},{12,4},{14,6},{1,9},{3,11}... | collective-permute-start | bytes 73736 | tf_op jit(solution)/shard_map/ppermute | solution.py:647
  65.8 19.6 %collective-permute-start.11 = (bf16[512,768]{1,0:T(8,128)(2,1)S(1)}, bf16[512,768]{1,0:T(8,128)(2,1)S(1)}, u32[]{:S(2)}, u32[]{:S(2)}) collective-permute-start(bf16[512,768]{1,0:T(8,128)(2,1)S(1)} %get-tuple-element.162.refs_5_), channel_id=1, source_target_pairs={{0,1},{1,0},{2,3},{3,2},{4,5},{5,4},{6,7},{7,6},{8,9},{9,8},{10,11... | collective-permute-start | bytes 2359304 | tf_op jit(solution)/shard_map/ppermute | solution.py:647
  68.3 2.9 %collective-permute-start.12 = (bf16[384,384]{1,0:T(8,128)(2,1)S(1)}, bf16[384,384]{1,0:T(8,128)(2,1)S(1)}, u32[]{:S(2)}, u32[]{:S(2)}) collective-permute-start(bf16[384,384]{1,0:T(8,128)(2,1)S(1)} %get-tuple-element.168), channel_id=1, source_target_pairs={{0,16},{16,0},{1,17},{17,1},{2,18},{18,2},{3,19},{19,3},{4,20},{20... | collective-permute-start | bytes 884744 | tf_op jit(solution)/shard_map/ppermute | solution.py:647
  68.3 3.0 %collective-permute-start.13 = (bf16[384,384]{1,0:T(8,128)(2,1)S(1)}, bf16[384,384]{1,0:T(8,128)(2,1)S(1)}, u32[]{:S(2)}, u32[]{:S(2)}) collective-permute-start(bf16[384,384]{1,0:T(8,128)(2,1)S(1)} %get-tuple-element.169), channel_id=1, source_target_pairs={{0,16},{16,0},{1,17},{17,1},{2,18},{18,2},{3,19},{19,3},{4,20},{20... | collective-permute-start | bytes 884744 | tf_op jit(solution)/shard_map/ppermute | solution.py:647
  68.8 2.9 %collective-permute-start.14 = (bf16[384,384]{1,0:T(8,128)(2,1)S(1)}, bf16[384,384]{1,0:T(8,128)(2,1)S(1)}, u32[]{:S(2)}, u32[]{:S(2)}) collective-permute-start(bf16[384,384]{1,0:T(8,128)(2,1)S(1)} %get-tuple-element.170), channel_id=1, source_target_pairs={{0,16},{16,0},{1,17},{17,1},{2,18},{18,2},{3,19},{19,3},{4,20},{20... | collective-permute-start | bytes 884744 | tf_op jit(solution)/shard_map/ppermute | solution.py:647
  68.9 3.0 %collective-permute-start.15 = (bf16[384,384]{1,0:T(8,128)(2,1)S(1)}, bf16[384,384]{1,0:T(8,128)(2,1)S(1)}, u32[]{:S(2)}, u32[]{:S(2)}) collective-permute-start(bf16[384,384]{1,0:T(8,128)(2,1)S(1)} %get-tuple-element.171), channel_id=1, source_target_pairs={{0,16},{16,0},{1,17},{17,1},{2,18},{18,2},{3,19},{19,3},{4,20},{20... | collective-permute-start | bytes 884744 | tf_op jit(solution)/shard_map/ppermute | solution.py:647
  71.8 2.7 %collective-permute-start.18 = (bf16[384,192]{1,0:T(8,128)(2,1)S(1)}, bf16[384,192]{1,0:T(8,128)(2,1)S(1)}, u32[]{:S(2)}, u32[]{:S(2)}) collective-permute-start(bf16[384,192]{1,0:T(8,128)(2,1)S(1)} %get-tuple-element.179), channel_id=1, source_target_pairs={{0,16},{16,0},{1,17},{17,1},{2,18},{18,2},{3,19},{19,3},{4,20},{20... | collective-permute-start | bytes 442376 | tf_op jit(solution)/shard_map/ppermute | solution.py:647
  71.9 2.6 %collective-permute-start.19 = (bf16[384,192]{1,0:T(8,128)(2,1)S(1)}, bf16[384,192]{1,0:T(8,128)(2,1)S(1)}, u32[]{:S(2)}, u32[]{:S(2)}) collective-permute-start(bf16[384,192]{1,0:T(8,128)(2,1)S(1)} %get-tuple-element.180), channel_id=1, source_target_pairs={{0,16},{16,0},{1,17},{17,1},{2,18},{18,2},{3,19},{19,3},{4,20},{20... | collective-permute-start | bytes 442376 | tf_op jit(solution)/shard_map/ppermute | solution.py:647
  72.7 2.3 %collective-permute-start.20 = (bf16[384,192]{1,0:T(8,128)(2,1)S(1)}, bf16[384,192]{1,0:T(8,128)(2,1)S(1)}, u32[]{:S(2)}, u32[]{:S(2)}) collective-permute-start(bf16[384,192]{1,0:T(8,128)(2,1)S(1)} %get-tuple-element.181), channel_id=1, source_target_pairs={{0,16},{16,0},{1,17},{17,1},{2,18},{18,2},{3,19},{19,3},{4,20},{20... | collective-permute-start | bytes 442376 | tf_op jit(solution)/shard_map/ppermute | solution.py:647
  73.0 16.6 %collective-permute-start.24 = (bf16[192,1536]{1,0:T(8,128)(2,1)S(1)}, bf16[192,1536]{1,0:T(8,128)(2,1)S(1)}, u32[]{:S(2)}, u32[]{:S(2)}) collective-permute-start(bf16[192,1536]{1,0:T(8,128)(2,1)S(1)} %get-tuple-element.172), channel_id=1, source_target_pairs={{0,2},{2,0},{4,6},{6,4},{8,10},{10,8},{12,14},{14,12},{1,3},{3,1},... | collective-permute-start | bytes 1769480 | tf_op jit(solution)/shard_map/ppermute | solution.py:647
  85.5 15.6 %collective-permute-start.26 = (bf16[192,1536]{1,0:T(8,128)(2,1)S(1)}, bf16[192,1536]{1,0:T(8,128)(2,1)S(1)}, u32[]{:S(2)}, u32[]{:S(2)}) collective-permute-start(bf16[192,1536]{1,0:T(8,128)(2,1)S(1)} %get-tuple-element.203), channel_id=1, source_target_pairs={{0,2},{2,0},{4,6},{6,4},{8,10},{10,8},{12,14},{14,12},{1,3},{3,1},... | collective-permute-start | bytes 1769480 | tf_op jit(solution)/shard_map/ppermute | solution.py:647
  89.7 11.3 %collective-permute-start.25 = (bf16[96,1536]{1,0:T(8,128)(2,1)S(1)}, bf16[96,1536]{1,0:T(8,128)(2,1)S(1)}, u32[]{:S(2)}, u32[]{:S(2)}) collective-permute-start(bf16[96,1536]{1,0:T(8,128)(2,1)S(1)} %get-tuple-element.196), channel_id=1, source_target_pairs={{0,4},{2,6},{4,0},{6,2},{8,12},{10,14},{12,8},{14,10},{1,5},{3,7},... | collective-permute-start | bytes 884744 | tf_op jit(solution)/shard_map/ppermute | solution.py:647
  101.1 5.7 %collective-permute-start.27 = (bf16[384,768]{1,0:T(8,128)(2,1)S(1)}, bf16[384,768]{1,0:T(8,128)(2,1)S(1)}, u32[]{:S(2)}, u32[]{:S(2)}) collective-permute-start(bf16[384,768]{1,0:T(8,128)(2,1)S(1)} %get-tuple-element.204), channel_id=1, source_target_pairs={{0,16},{16,0},{1,17},{17,1},{2,18},{18,2},{3,19},{19,3},{4,20},{20... | collective-permute-start | bytes 1769480 | tf_op jit(solution)/shard_map/ppermute | solution.py:647
  101.6 24.9 %collective-permute-start.36 = (bf16[512,768]{1,0:T(8,128)(2,1)S(1)}, bf16[512,768]{1,0:T(8,128)(2,1)S(1)}, u32[]{:S(2)}, u32[]{:S(2)}) collective-permute-start(bf16[512,768]{1,0:T(8,128)(2,1)S(1)} %get-tuple-element.226.own_ref), channel_id=1, source_target_pairs={{0,1},{1,0},{2,3},{3,2},{4,5},{5,4},{6,7},{7,6},{8,9},{9,8},{10,11... | collective-permute-start | bytes 2359304 | tf_op jit(solution)/shard_map/ppermute | solution.py:647
  103.6 13.3 %collective-permute-start.29 = (bf16[192,896]{1,0:T(8,128)(2,1)S(1)}, bf16[192,896]{1,0:T(8,128)(2,1)S(1)}, u32[]{:S(2)}, u32[]{:S(2)}) collective-permute-start(bf16[192,896]{1,0:T(8,128)(2,1)S(1)} %get-tuple-element.216), channel_id=1, source_target_pairs={{0,2},{2,0},{4,6},{6,4},{8,10},{10,8},{12,14},{14,12},{1,3},{3,1},... | collective-permute-start | bytes 1032200 | tf_op jit(solution)/shard_map/ppermute | solution.py:647
  105.1 11.8 %collective-permute-start.30 = (bf16[96,1536]{1,0:T(8,128)(2,1)S(1)}, bf16[96,1536]{1,0:T(8,128)(2,1)S(1)}, u32[]{:S(2)}, u32[]{:S(2)}) collective-permute-start(bf16[96,1536]{1,0:T(8,128)(2,1)S(1)} %get-tuple-element.210), channel_id=1, source_target_pairs={{0,4},{2,6},{4,0},{6,2},{8,12},{10,14},{12,8},{14,10},{1,5},{3,7},... | collective-permute-start | bytes 884744 | tf_op jit(solution)/shard_map/ppermute | solution.py:647
  106.2 9.3 %collective-permute-start.31 = (bf16[48,1536]{1,0:T(8,128)(2,1)S(1)}, bf16[48,1536]{1,0:T(8,128)(2,1)S(1)}, u32[]{:S(2)}, u32[]{:S(2)}) collective-permute-start(bf16[48,1536]{1,0:T(8,128)(2,1)S(1)} %get-tuple-element.213), channel_id=1, source_target_pairs={{0,8},{2,10},{4,12},{6,14},{8,0},{10,2},{12,4},{14,6},{1,9},{3,11}... | collective-permute-start | bytes 442376 | tf_op jit(solution)/shard_map/ppermute | solution.py:647
  107.0 13.0 %collective-permute-start.33 = (bf16[192,768]{1,0:T(8,128)(2,1)S(1)}, bf16[192,768]{1,0:T(8,128)(2,1)S(1)}, u32[]{:S(2)}, u32[]{:S(2)}) collective-permute-start(bf16[192,768]{1,0:T(8,128)(2,1)S(1)} %get-tuple-element.219), channel_id=1, source_target_pairs={{0,2},{2,0},{4,6},{6,4},{8,10},{10,8},{12,14},{14,12},{1,3},{3,1},... | collective-permute-start | bytes 884744 | tf_op jit(solution)/shard_map/ppermute | solution.py:647
  117.0 8.4 %collective-permute-start.32 = (bf16[96,896]{1,0:T(8,128)(2,1)S(1)}, bf16[96,896]{1,0:T(8,128)(2,1)S(1)}, u32[]{:S(2)}, u32[]{:S(2)}) collective-permute-start(bf16[96,896]{1,0:T(8,128)(2,1)S(1)} %get-tuple-element.218), channel_id=1, source_target_pairs={{0,4},{2,6},{4,0},{6,2},{8,12},{10,14},{12,8},{14,10},{1,5},{3,7},... | collective-permute-start | bytes 516104 | tf_op jit(solution)/shard_map/ppermute | solution.py:647
  117.9 10.3 %collective-permute-start.37 = (bf16[48,1536]{1,0:T(8,128)(2,1)S(1)}, bf16[48,1536]{1,0:T(8,128)(2,1)S(1)}, u32[]{:S(2)}, u32[]{:S(2)}) collective-permute-start(bf16[48,1536]{1,0:T(8,128)(2,1)S(1)} %get-tuple-element.233), channel_id=1, source_target_pairs={{0,8},{2,10},{4,12},{6,14},{8,0},{10,2},{12,4},{14,6},{1,9},{3,11}... | collective-permute-start | bytes 442376 | tf_op jit(solution)/shard_map/ppermute | solution.py:647
  125.4 6.6 %collective-permute-start.34 = (bf16[96,768]{1,0:T(8,128)(2,1)S(1)}, bf16[96,768]{1,0:T(8,128)(2,1)S(1)}, u32[]{:S(2)}, u32[]{:S(2)}) collective-permute-start(bf16[96,768]{1,0:T(8,128)(2,1)S(1)} %get-tuple-element.222), channel_id=1, source_target_pairs={{0,4},{2,6},{4,0},{6,2},{8,12},{10,14},{12,8},{14,10},{1,5},{3,7},... | collective-permute-start | bytes 442376 | tf_op jit(solution)/shard_map/ppermute | solution.py:647
  125.6 5.6 %collective-permute-start.35 = (bf16[48,896]{1,0:T(8,128)(2,1)S(1)}, bf16[48,896]{1,0:T(8,128)(2,1)S(1)}, u32[]{:S(2)}, u32[]{:S(2)}) collective-permute-start(bf16[48,896]{1,0:T(8,128)(2,1)S(1)} %get-tuple-element.225), channel_id=1, source_target_pairs={{0,8},{2,10},{4,12},{6,14},{8,0},{10,2},{12,4},{14,6},{1,9},{3,11}... | collective-permute-start | bytes 258056 | tf_op jit(solution)/shard_map/ppermute | solution.py:647
  132.1 6.1 %collective-permute-start.38 = (bf16[48,768]{1,0:T(8,128)(2,1)S(1)}, bf16[48,768]{1,0:T(8,128)(2,1)S(1)}, u32[]{:S(2)}, u32[]{:S(2)}) collective-permute-start(bf16[48,768]{1,0:T(8,128)(2,1)S(1)} %get-tuple-element.240), channel_id=1, source_target_pairs={{0,8},{2,10},{4,12},{6,14},{8,0},{10,2},{12,4},{14,6},{1,9},{3,11}... | collective-permute-start | bytes 221192 | tf_op jit(solution)/shard_map/ppermute | solution.py:647
  133.5 3.5 %collective-permute-start.39 = (f32[48]{0:T(128)S(1)}, f32[48]{0:T(128)S(1)}, u32[]{:S(2)}, u32[]{:S(2)}) collective-permute-start(f32[48]{0:T(128)S(1)} %get-tuple-element.243.gain_own), channel_id=1, source_target_pairs={{0,1},{1,0},{2,3},{3,2},{4,5},{5,4},{6,7},{7,6},{8,9},{9,8},{10,11... | collective-permute-start | bytes 584 | tf_op jit(solution)/shard_map/ppermute | solution.py:647
  (14 other events, 90.0 us)

commit v4 on v3

--- a/solution.py
+++ b/solution.py
@@ -133,7 +133,7 @@
     low_lanes = lax.broadcasted_iota(jnp.int32, (BLOCK, BLOCK), 1) < BLOCK // 2
     zero = jnp.zeros((BLOCK, BLOCK), bf16)
 
-    @pl.loop(0, pairs)
+    @pl.loop(0, pairs, unroll=True)
     def _(pair):
         lanes = pl.ds(pl.multiple_of(pair * BLOCK, BLOCK), BLOCK)
         for h in range(2):
@@ -1029,10 +1029,11 @@
     first_scatter.received = tie(first_scatter.received, up_scatter.send, down_scatter.send)[0]
     first_scatter.step()
     second_scatter.step()
-    first_scatter.received, up_scatter.received, down_scatter.received = tie(
-        first_scatter.received, up_scatter.received, down_scatter.received
+    first_scatter.received, down_scatter.received = tie(
+        first_scatter.received, down_scatter.received
     )
     first_scatter.step()
+    first_scatter.send, up_scatter.received = tie(first_scatter.send, up_scatter.received)
     up_scatter.step()
     first_scatter.received, second_scatter.received, down_scatter.received = tie(
         first_scatter.received, second_scatter.received, down_scatter.received
@@ -1052,8 +1053,8 @@
         scratch=[pltpu.VMEM((length, width), f32), pltpu.SemaphoreType.DMA((length // BLOCK,))],
         in_vmem=3,
     )
-    second_scatter.received, first_scatter.received, tokens_grad, down_sum, up_sum = tie(
-        second_scatter.received, first_scatter.received, tokens_grad, down_sum, up_sum
+    second_scatter.received, tokens_grad, down_sum, up_sum = tie(
+        second_scatter.received, tokens_grad, down_sum, up_sum
     )
     second_scatter.step()
     bias_pieces = -(-bucket_count // shard)

time: 139 us -> 136 us (0.978)
  waiting for transfers between devices: 55.7 us -> 49 us
  starting transfers between devices: 31.3 us -> 35.3 us
    ppermute x40, waiting for transfers between devices: 55.7 us -> 49 us  [swap(): return lax.ppermute(values, axis, [(i, i ^ bit) for i in range(count)])]
    ppermute x40, starting transfers between devices: 31.3 us -> 35.3 us  [swap(): return lax.ppermute(values, axis, [(i, i ^ bit) for i in range(count)])]
  transfers between devices with their start and end apart: 40 -> 40, of which waited for: 21 -> 19; matrix products, arithmetic and copies ran while one was open for 0% -> 0% of each run, Pallas kernels for 31% -> 31%
where the time goes in v4:
time: 136 us
  Pallas kernels  49.2 us (36%)
  waiting for transfers between devices  49 us (36%)
  starting transfers between devices  35.3 us (26%)
    pallas_call x28, Pallas kernels, whole(): pl.pallas_call(kernel, out_shape=out_shapes, in_specs=[hbm] * in_hbm + [v...  49.2 us
    ppermute x40, waiting for transfers between devices, swap(): return lax.ppermute(values, axis, [(i, i ^ bit) for i in range(count)])  49 us
    ppermute x40, starting transfers between devices, swap(): return lax.ppermute(values, axis, [(i, i ^ bit) for i in range(count)])  35.3 us
  transfers between devices with their start and end apart: 40, of which 19 were waited for; matrix products, arithmetic and copies ran while one was open for 0% of the time, Pallas kernels for 31%

profile of v4, /device:TPU:0, one launch (start us, length us, event | category | flops | bytes accessed | tf_op | source)
XLA Modules:
  0.0 135.5 jit_solution(10206315890445235510)
XLA Ops:
  1.6 3.0 %collective-permute-start = (bf16[192,768]{1,0:T(8,128)(2,1)S(1)}, bf16[192,768]{1,0:T(8,128)(2,1)S(1)}, u32[]{:S(2)}, u32[]{:S(2)}) collective-permute-start(bf16[192,768]{1,0:T(8,128)(2,1)S(1)} %constant_dynamic-slice_fusion), channel_id=1, source_target_pairs={{0,1},{1,0},{2,3},{3,2},{4,5},{5,4},{6,7},{7,6},{8,9},{9,8},{10,11... | collective-permute-start | bytes 884744 | tf_op jit(solution)/shard_map/ppermute | solution.py:647
  4.7 10.0 %attention.1 = (bf16[512,768]{1,0:T(8,128)(2,1)}, bf16[512,384]{1,0:T(8,128)(2,1)}, bf16[512,384]{1,0:T(8,128)(2,1)}, bf16[512,384]{1,0:T(8,128)(2,1)}, bf16[6,5...) custom-call(bf16[512,768]{1,0:T(8,128)(2,1)} %bitcast.13, ...), custom_call_target="tpu_custom_call" | custom-call | flops 1 | bytes 1 | tf_op jit(solution)/shard_map/attention/pallas_call | solution.py:627
  14.9 2.0 %collective-permute-start.2 = (bf16[256,384]{1,0:T(8,128)(2,1)S(1)}, bf16[256,384]{1,0:T(8,128)(2,1)S(1)}, u32[]{:S(2)}, u32[]{:S(2)}) collective-permute-start(bf16[256,384]{1,0:T(8,128)(2,1)S(1)} %get-tuple-element.133.mix_own), channel_id=1, source_target_pairs={{0,1},{1,0},{2,3},{3,2},{4,5},{5,4},{6,7},{7,6},{8,9},{9,8},{10,11... | collective-permute-start | bytes 589832 | tf_op jit(solution)/shard_map/ppermute | solution.py:647
  16.9 3.1 %load.1 = (bf16[768,768]{1,0:T(8,128)(2,1)S(1)}, bf16[768,1536]{1,0:T(8,128)(2,1)S(1)}, bf16[1536,768]{1,0:T(8,128)(2,1)S(1)}, bf16[768,768]{1,0:T(8,128)(2,1)S(1)}) custom-call(bf16[384,768]{1,0:T(8,128)(2,1)} %wo_hbm.1, bf16[768,1536]{1,0:T(8,128)(2,1)} %up_hbm.1, bf16[1536,768]{1,0:T(8,128)(2,1)} %down_hbm.1, bf16[768,768]{1,0:T(8,128)(2,1)} %proj_hbm.1, ...), custom_call_target="tpu_custom_call" | custom-call | flops 1 | bytes 1 | tf_op jit(solution)/shard_map/load/pallas_call | solution.py:627
  20.0 2.6 %collective-permute-done.4.mix_other = bf16[256,384]{1,0:T(8,128)(2,1)S(1)} collective-permute-done((bf16[256,384]{1,0:T(8,128)(2,1)S(1)}, bf16[256,384]{1,0:T(8,128)(2,1)S(1)}, u32[]{:S(2)}, u32[]{:S(2)}) %collective-permute-start.4) | collective-permute-done | bytes 196640 | tf_op jit(solution)/shard_map/ppermute | solution.py:647
  22.6 3.3 %feed_forward.3 = (f32[256,768]{1,0:T(8,128)S(1)}, bf16[256,768]{1,0:T(8,128)(2,1)S(1)}, bf16[256,1536]{1,0:T(8,128)(2,1)S(1)}, f32[256,1536]{1,0:T(8,128)S(1)}, bf16[256,768]{1,0:T(8,128)(2,1)S(1)}) custom-call(bf16[512,768]{1,0:T(8,128)(2,1)S(1)} %get-tuple-element.137.tok_ref, bf16[768,768]{1,0:T(8,128)(2,1)S(1)} %get-tuple-element.138.wo_ref.refs_4_, ...), custom_call_target="tpu_custom_call" | custom-call | flops 1 | bytes 1 | tf_op jit(solution)/shard_map/feed_forward/pallas_call | solution.py:627
  26.3 3.3 %feed_forward.2 = (f32[256,768]{1,0:T(8,128)S(1)}, bf16[256,768]{1,0:T(8,128)(2,1)S(1)}, bf16[256,1536]{1,0:T(8,128)(2,1)S(1)}, f32[256,1536]{1,0:T(8,128)S(1)}, bf16[256,768]{1,0:T(8,128)(2,1)S(1)}) custom-call(bf16[512,768]{1,0:T(8,128)(2,1)S(1)} %get-tuple-element.137.tok_ref, bf16[768,768]{1,0:T(8,128)(2,1)S(1)} %get-tuple-element.138.wo_ref.refs_4_, ...), custom_call_target="tpu_custom_call" | custom-call | flops 1 | bytes 1 | tf_op jit(solution)/shard_map/feed_forward/pallas_call | solution.py:627
  29.6 1.7 %collective-permute-start.3 = (bf16[256,768]{1,0:T(8,128)(2,1)S(1)}, bf16[256,768]{1,0:T(8,128)(2,1)S(1)}, u32[]{:S(2)}, u32[]{:S(2)}) collective-permute-start(bf16[256,768]{1,0:T(8,128)(2,1)S(1)} %get-tuple-element.142.own_ref), channel_id=1, source_target_pairs={{0,1},{1,0},{2,3},{3,2},{4,5},{5,4},{6,7},{7,6},{8,9},{9,8},{10,11... | collective-permute-start | bytes 1179656 | tf_op jit(solution)/shard_map/ppermute | solution.py:647
  31.3 6.7 %collective-permute-done.5.rec_ref = bf16[256,768]{1,0:T(8,128)(2,1)S(1)} collective-permute-done((bf16[256,768]{1,0:T(8,128)(2,1)S(1)}, bf16[256,768]{1,0:T(8,128)(2,1)S(1)}, u32[]{:S(2)}, u32[]{:S(2)}) %collective-permute-start.5) | collective-permute-done | bytes 393248 | tf_op jit(solution)/shard_map/ppermute | solution.py:647
  38.4 6.2 %collective-permute-done.3.rec_ref = bf16[256,768]{1,0:T(8,128)(2,1)S(1)} collective-permute-done((bf16[256,768]{1,0:T(8,128)(2,1)S(1)}, bf16[256,768]{1,0:T(8,128)(2,1)S(1)}, u32[]{:S(2)}, u32[]{:S(2)}) %collective-permute-start.3) | collective-permute-done | bytes 393248 | tf_op jit(solution)/shard_map/ppermute | solution.py:647
  45.0 1.6 %collective-permute-start.6 = (bf16[8,768]{1,0:T(8,128)(2,1)S(1)}, bf16[8,768]{1,0:T(8,128)(2,1)S(1)}, u32[]{:S(2)}, u32[]{:S(2)}) collective-permute-start(bf16[8,768]{1,0:T(8,128)(2,1)S(1)} %get-tuple-element.148), channel_id=1, source_target_pairs={{0,2},{2,0},{4,6},{6,4},{8,10},{10,8},{12,14},{14,12},{1,3},{3,1},... | collective-permute-start | bytes 36872 | tf_op jit(solution)/shard_map/ppermute | solution.py:647
  46.6 2.2 %collective-permute-done.6 = bf16[8,768]{1,0:T(8,128)(2,1)S(1)} collective-permute-done((bf16[8,768]{1,0:T(8,128)(2,1)S(1)}, bf16[8,768]{1,0:T(8,128)(2,1)S(1)}, u32[]{:S(2)}, u32[]{:S(2)}) %collective-permute-start.6) | collective-permute-done | bytes 12320 | tf_op jit(solution)/shard_map/ppermute | solution.py:647
  48.8 1.6 %collective-permute-start.7 = (bf16[16,768]{1,0:T(8,128)(2,1)S(1)}, bf16[16,768]{1,0:T(8,128)(2,1)S(1)}, u32[]{:S(2)}, u32[]{:S(2)}) collective-permute-start(bf16[16,768]{1,0:T(8,128)(2,1)S(1)} %get-tuple-element.261), channel_id=1, source_target_pairs={{0,4},{2,6},{4,0},{6,2},{8,12},{10,14},{12,8},{14,10},{1,5},{3,7},... | collective-permute-start | bytes 73736 | tf_op jit(solution)/shard_map/ppermute | solution.py:647
  50.3 2.5 %collective-permute-start.9 = (bf16[16,768]{1,0:T(8,128)(2,1)S(1)}, bf16[16,768]{1,0:T(8,128)(2,1)S(1)}, u32[]{:S(2)}, u32[]{:S(2)}) collective-permute-start(bf16[16,768]{1,0:T(8,128)(2,1)S(1)} %get-tuple-element.261), channel_id=1, source_target_pairs={{0,12},{2,14},{4,8},{6,10},{8,4},{10,6},{12,0},{14,2},{1,13},{3,15... | collective-permute-start | bytes 73736 | tf_op jit(solution)/shard_map/ppermute | solution.py:647
  53.0 4.9 %collective-permute-done.8 = bf16[16,768]{1,0:T(8,128)(2,1)S(1)} collective-permute-done((bf16[16,768]{1,0:T(8,128)(2,1)S(1)}, bf16[16,768]{1,0:T(8,128)(2,1)S(1)}, u32[]{:S(2)}, u32[]{:S(2)}) %collective-permute-start.8) | collective-permute-done | bytes 24608 | tf_op jit(solution)/shard_map/ppermute | solution.py:647
  59.2 2.0 %contrast.1 = (f32[1,1]{1,0:T(1,128)}, f32[48,768]{1,0:T(8,128)}, f32[8,768]{1,0:T(8,128)S(1)}) custom-call(bf16[768,768]{1,0:T(8,128)(2,1)S(1)} %get-tuple-element.136.proj_ref, bf16[128,768]{1,0:T(8,128)(2,1)S(1)} %constant_dynamic-update-slice_fusion.7.gathered_ref, s32[64]{0:T(128)S(1)} %copy-done.5), custom_call_target="tpu_custom_call" | custom-call | flops 1 | bytes 1 | tf_op jit(solution)/shard_map/contrast/pallas_call | solution.py:627
  61.3 3.9 %feed_forward_back.1 = (bf16[512,768]{1,0:T(8,128)(2,1)S(1)}, f32[512,768]{1,0:T(8,128)S(1)}, bf16[512,768]{1,0:T(8,128)(2,1)S(1)}, bf16[512,1536]{1,0:T(8,128)(2,1)S(1)}, f32[1,768]{1,0:T(1,128)S(1)}) custom-call(bf16[1536,768]{1,0:T(8,128)(2,1)S(1)} %get-tuple-element.140.down_ref, bf16[768,1536]{1,0:T(8,128)(2,1)S(1)} %get-tuple-element.139.up_ref, ...), custom_call_target="tpu_custom_call" | custom-call | flops 1 | bytes 1 | tf_op jit(solution)/shard_map/feed_forward_back/pallas_call | solution.py:627
  65.7 1.8 %down_weight.1 = (bf16[384,384]{1,0:T(8,128)(2,1)S(1)}, bf16[384,384]{1,0:T(8,128)(2,1)S(1)}, bf16[384,384]{1,0:T(8,128)(2,1)S(1)}, bf16[384,384]{1,0:T(8,128)(2,1)S(1)}, bf16[384,1536]{1,0:T(8,128)(2,1)S(1)}) custom-call(bf16[512,768]{1,0:T(8,128)(2,1)S(1)} %get-tuple-element.163.df_ref, bf16[256,1536]{1,0:T(8,128)(2,1)S(1)} %get-tuple-element.164.refs_0_, ...), custom_call_target="tpu_custom_call" | custom-call | flops 1 | bytes 1 | tf_op jit(solution)/shard_map/down_weight/pallas_call | solution.py:627
  68.6 1.8 %up_weight.1 = (bf16[384,192]{1,0:T(8,128)(2,1)S(1)}, bf16[384,192]{1,0:T(8,128)(2,1)S(1)}, bf16[384,192]{1,0:T(8,128)(2,1)S(1)}, bf16[384,192]{1,0:T(8,128)(2,1...) custom-call(bf16[512,1536]{1,0:T(8,128)(2,1)S(1)} %get-tuple-element, ...), custom_call_target="tpu_custom_call" | custom-call | flops 1 | bytes 1 | tf_op jit(solution)/shard_map/up_weight/pallas_call | solution.py:627
  72.3 1.5 %collective-permute-start.24 = (bf16[192,1536]{1,0:T(8,128)(2,1)S(1)}, bf16[192,1536]{1,0:T(8,128)(2,1)S(1)}, u32[]{:S(2)}, u32[]{:S(2)}) collective-permute-start(bf16[192,1536]{1,0:T(8,128)(2,1)S(1)} %get-tuple-element.171), channel_id=1, source_target_pairs={{0,2},{2,0},{4,6},{6,4},{8,10},{10,8},{12,14},{14,12},{1,3},{3,1},... | collective-permute-start | bytes 1769480 | tf_op jit(solution)/shard_map/ppermute | solution.py:647
  76.3 8.5 %collective-permute-done.11.refs_9_ = bf16[512,768]{1,0:T(8,128)(2,1)S(1)} collective-permute-done((bf16[512,768]{1,0:T(8,128)(2,1)S(1)}, bf16[512,768]{1,0:T(8,128)(2,1)S(1)}, u32[]{:S(2)}, u32[]{:S(2)}) %collective-permute-start.11) | collective-permute-done | bytes 786464 | tf_op jit(solution)/shard_map/ppermute | solution.py:647
  86.3 2.6 %middle_back.1 = (f32[512,768]{1,0:T(8,128)S(1)}, bf16[512,768]{1,0:T(8,128)(2,1)}, bf16[512,384]{1,0:T(8,128)(2,1)S(1)}, f32[1,768]{1,0:T(1,128)S(1)}, bf16[512...) custom-call(bf16[512,384]{1,0:T(8,128)(2,1)} %get-tuple-element.152., ...), custom_call_target="tpu_custom_call" | custom-call | flops 1 | bytes 1 | tf_op jit(solution)/shard_map/middle_back/pallas_call | solution.py:627
  89.7 10.7 %attention_back.1 = (bf16[512,768]{1,0:T(8,128)(2,1)S(1)}, bf16[384,896]{1,0:T(8,128)(2,1)S(1)}, bf16[384,896]{1,0:T(8,128)(2,1)S(1)}, bf16[384,768]{1,0:T(8,128)(2,1)S(1)}, bf16[384,768]{1,0:T(8,128)(2,1)S(1)}) custom-call(bf16[768,384]{1,0:T(8,128)(2,1)} %wq_hbm.3, bf16[768,384]{1,0:T(8,128)(2,1)} %wk_hbm.3, bf16[768,384]{1,0:T(8,128)(2,1)} %wv_hbm.3, ...), custom_call_target="tpu_custom_call" | custom-call | flops 1 | bytes 1 | tf_op jit(solution)/shard_map/attention_back/pallas_call | solution.py:627
  102.9 1.6 %collective-permute-start.29 = (bf16[192,896]{1,0:T(8,128)(2,1)S(1)}, bf16[192,896]{1,0:T(8,128)(2,1)S(1)}, u32[]{:S(2)}, u32[]{:S(2)}) collective-permute-start(bf16[192,896]{1,0:T(8,128)(2,1)S(1)} %get-tuple-element.215), channel_id=1, source_target_pairs={{0,2},{2,0},{4,6},{6,4},{8,10},{10,8},{12,14},{14,12},{1,3},{3,1},... | collective-permute-start | bytes 1032200 | tf_op jit(solution)/shard_map/ppermute | solution.py:647
  106.9 7.1 %collective-permute-done.30.rec_ref = bf16[48,1536]{1,0:T(8,128)(2,1)S(1)} collective-permute-done((bf16[48,1536]{1,0:T(8,128)(2,1)S(1)}, bf16[48,1536]{1,0:T(8,128)(2,1)S(1)}, u32[]{:S(2)}, u32[]{:S(2)}) %collective-permute-start.30) | collective-permute-done | bytes 147488 | tf_op jit(solution)/shard_map/ppermute | solution.py:647
  115.4 1.8 %collective-permute-done.35.refs_0_ = bf16[96,1536]{1,0:T(8,128)(2,1)S(1)} collective-permute-done((bf16[96,1536]{1,0:T(8,128)(2,1)S(1)}, bf16[96,1536]{1,0:T(8,128)(2,1)S(1)}, u32[]{:S(2)}, u32[]{:S(2)}) %collective-permute-start.35) | collective-permute-done | bytes 294944 | tf_op jit(solution)/shard_map/ppermute | solution.py:647
  117.3 2.4 %collective-permute-start.36 = (bf16[48,1536]{1,0:T(8,128)(2,1)S(1)}, bf16[48,1536]{1,0:T(8,128)(2,1)S(1)}, u32[]{:S(2)}, u32[]{:S(2)}) collective-permute-start(bf16[48,1536]{1,0:T(8,128)(2,1)S(1)} %get-tuple-element.229), channel_id=1, source_target_pairs={{0,8},{2,10},{4,12},{6,14},{8,0},{10,2},{12,4},{14,6},{1,9},{3,11}... | collective-permute-start | bytes 442376 | tf_op jit(solution)/shard_map/ppermute | solution.py:647
  119.6 2.3 %collective-permute-done.31.refs_0_ = bf16[96,896]{1,0:T(8,128)(2,1)S(1)} collective-permute-done((bf16[96,896]{1,0:T(8,128)(2,1)S(1)}, bf16[96,896]{1,0:T(8,128)(2,1)S(1)}, u32[]{:S(2)}, u32[]{:S(2)}) %collective-permute-start.31) | collective-permute-done | bytes 172064 | tf_op jit(solution)/shard_map/ppermute | solution.py:647
  122.2 2.6 %collective-permute-start.38 = (bf16[48,896]{1,0:T(8,128)(2,1)S(1)}, bf16[48,896]{1,0:T(8,128)(2,1)S(1)}, u32[]{:S(2)}, u32[]{:S(2)}) collective-permute-start(bf16[48,896]{1,0:T(8,128)(2,1)S(1)} %get-tuple-element.240), channel_id=1, source_target_pairs={{0,8},{2,10},{4,12},{6,14},{8,0},{10,2},{12,4},{14,6},{1,9},{3,11}... | collective-permute-start | bytes 258056 | tf_op jit(solution)/shard_map/ppermute | solution.py:647
  124.8 1.7 %last.1 = f32[512,768]{1,0:T(8,128)} custom-call(bf16[512,768]{1,0:T(8,128)(2,1)S(1)} %get-tuple-element.137.tok_ref, bf16[512,768]{1,0:T(8,128)(2,1)S(1)} %get-tuple-element.222.own_ref, f32[512,768]{1,0:T(8,128)S(1)} %get-tuple-element.223.dh1_ref, f32[768]{0:T(1024)S(1)} %copy-done.4, bf16[512,768]{1,0:T(8,128)(2,1)S(1)} %collective-permute-done.34.rec_ref), custom_call_target="tpu_custom_call" | custom-call | flops 1 | bytes 1 | tf_op jit(solution)/shard_map/last/pallas_call | solution.py:627
  130.2 3.1 %collective-permute-start.39 = (f32[48]{0:T(128)S(1)}, f32[48]{0:T(128)S(1)}, u32[]{:S(2)}, u32[]{:S(2)}) collective-permute-start(f32[48]{0:T(128)S(1)} %get-tuple-element.241.gain_own), channel_id=1, source_target_pairs={{0,1},{1,0},{2,3},{3,2},{4,5},{5,4},{6,7},{7,6},{8,9},{9,8},{10,11... | collective-permute-start | bytes 584 | tf_op jit(solution)/shard_map/ppermute | solution.py:647
  133.3 1.5 %collective-permute-done.39.gain_rec = f32[48]{0:T(128)S(1)} collective-permute-done((f32[48]{0:T(128)S(1)}, f32[48]{0:T(128)S(1)}, u32[]{:S(2)}, u32[]{:S(2)}) %collective-permute-start.39) | collective-permute-done | bytes 224 | tf_op jit(solution)/shard_map/ppermute | solution.py:647
  (95 shorter events, 23.0 us)
Async XLA Ops:
  1.6 13.1 %collective-permute-start = (bf16[192,768]{1,0:T(8,128)(2,1)S(1)}, bf16[192,768]{1,0:T(8,128)(2,1)S(1)}, u32[]{:S(2)}, u32[]{:S(2)}) collective-permute-start(bf16[192,768]{1,0:T(8,128)(2,1)S(1)} %constant_dynamic-slice_fusion), channel_id=1, source_target_pairs={{0,1},{1,0},{2,3},{3,2},{4,5},{5,4},{6,7},{7,6},{8,9},{9,8},{10,11... | collective-permute-start | bytes 884744 | tf_op jit(solution)/shard_map/ppermute | solution.py:647
  14.8 7.8 %collective-permute-start.4 = (bf16[256,384]{1,0:T(8,128)(2,1)S(1)}, bf16[256,384]{1,0:T(8,128)(2,1)S(1)}, u32[]{:S(2)}, u32[]{:S(2)}) collective-permute-start(bf16[256,384]{1,0:T(8,128)(2,1)S(1)} %get-tuple-element.144.mix_own), channel_id=1, source_target_pairs={{0,1},{1,0},{2,3},{3,2},{4,5},{5,4},{6,7},{7,6},{8,9},{9,8},{10,11... | collective-permute-start | bytes 589832 | tf_op jit(solution)/shard_map/ppermute | solution.py:647
  14.9 11.4 %collective-permute-start.2 = (bf16[256,384]{1,0:T(8,128)(2,1)S(1)}, bf16[256,384]{1,0:T(8,128)(2,1)S(1)}, u32[]{:S(2)}, u32[]{:S(2)}) collective-permute-start(bf16[256,384]{1,0:T(8,128)(2,1)S(1)} %get-tuple-element.133.mix_own), channel_id=1, source_target_pairs={{0,1},{1,0},{2,3},{3,2},{4,5},{5,4},{6,7},{7,6},{8,9},{9,8},{10,11... | collective-permute-start | bytes 589832 | tf_op jit(solution)/shard_map/ppermute | solution.py:647
  25.9 12.1 %collective-permute-start.5 = (bf16[256,768]{1,0:T(8,128)(2,1)S(1)}, bf16[256,768]{1,0:T(8,128)(2,1)S(1)}, u32[]{:S(2)}, u32[]{:S(2)}) collective-permute-start(bf16[256,768]{1,0:T(8,128)(2,1)S(1)} %get-tuple-element.146.own_ref), channel_id=1, source_target_pairs={{0,1},{1,0},{2,3},{3,2},{4,5},{5,4},{6,7},{7,6},{8,9},{9,8},{10,11... | collective-permute-start | bytes 1179656 | tf_op jit(solution)/shard_map/ppermute | solution.py:647
  29.6 15.0 %collective-permute-start.3 = (bf16[256,768]{1,0:T(8,128)(2,1)S(1)}, bf16[256,768]{1,0:T(8,128)(2,1)S(1)}, u32[]{:S(2)}, u32[]{:S(2)}) collective-permute-start(bf16[256,768]{1,0:T(8,128)(2,1)S(1)} %get-tuple-element.142.own_ref), channel_id=1, source_target_pairs={{0,1},{1,0},{2,3},{3,2},{4,5},{5,4},{6,7},{7,6},{8,9},{9,8},{10,11... | collective-permute-start | bytes 1179656 | tf_op jit(solution)/shard_map/ppermute | solution.py:647
  45.0 3.8 %collective-permute-start.6 = (bf16[8,768]{1,0:T(8,128)(2,1)S(1)}, bf16[8,768]{1,0:T(8,128)(2,1)S(1)}, u32[]{:S(2)}, u32[]{:S(2)}) collective-permute-start(bf16[8,768]{1,0:T(8,128)(2,1)S(1)} %get-tuple-element.148), channel_id=1, source_target_pairs={{0,2},{2,0},{4,6},{6,4},{8,10},{10,8},{12,14},{14,12},{1,3},{3,1},... | collective-permute-start | bytes 36872 | tf_op jit(solution)/shard_map/ppermute | solution.py:647
  48.8 4.2 %collective-permute-start.7 = (bf16[16,768]{1,0:T(8,128)(2,1)S(1)}, bf16[16,768]{1,0:T(8,128)(2,1)S(1)}, u32[]{:S(2)}, u32[]{:S(2)}) collective-permute-start(bf16[16,768]{1,0:T(8,128)(2,1)S(1)} %get-tuple-element.261), channel_id=1, source_target_pairs={{0,4},{2,6},{4,0},{6,2},{8,12},{10,14},{12,8},{14,10},{1,5},{3,7},... | collective-permute-start | bytes 73736 | tf_op jit(solution)/shard_map/ppermute | solution.py:647
  50.3 7.5 %collective-permute-start.9 = (bf16[16,768]{1,0:T(8,128)(2,1)S(1)}, bf16[16,768]{1,0:T(8,128)(2,1)S(1)}, u32[]{:S(2)}, u32[]{:S(2)}) collective-permute-start(bf16[16,768]{1,0:T(8,128)(2,1)S(1)} %get-tuple-element.261), channel_id=1, source_target_pairs={{0,12},{2,14},{4,8},{6,10},{8,4},{10,6},{12,0},{14,2},{1,13},{3,15... | collective-permute-start | bytes 73736 | tf_op jit(solution)/shard_map/ppermute | solution.py:647
  52.8 5.0 %collective-permute-start.8 = (bf16[16,768]{1,0:T(8,128)(2,1)S(1)}, bf16[16,768]{1,0:T(8,128)(2,1)S(1)}, u32[]{:S(2)}, u32[]{:S(2)}) collective-permute-start(bf16[16,768]{1,0:T(8,128)(2,1)S(1)} %get-tuple-element.261), channel_id=1, source_target_pairs={{0,8},{2,10},{4,12},{6,14},{8,0},{10,2},{12,4},{14,6},{1,9},{3,11}... | collective-permute-start | bytes 73736 | tf_op jit(solution)/shard_map/ppermute | solution.py:647
  65.1 19.6 %collective-permute-start.11 = (bf16[512,768]{1,0:T(8,128)(2,1)S(1)}, bf16[512,768]{1,0:T(8,128)(2,1)S(1)}, u32[]{:S(2)}, u32[]{:S(2)}) collective-permute-start(bf16[512,768]{1,0:T(8,128)(2,1)S(1)} %get-tuple-element.161.refs_5_), channel_id=1, source_target_pairs={{0,1},{1,0},{2,3},{3,2},{4,5},{5,4},{6,7},{7,6},{8,9},{9,8},{10,11... | collective-permute-start | bytes 2359304 | tf_op jit(solution)/shard_map/ppermute | solution.py:647
  67.6 2.9 %collective-permute-start.12 = (bf16[384,384]{1,0:T(8,128)(2,1)S(1)}, bf16[384,384]{1,0:T(8,128)(2,1)S(1)}, u32[]{:S(2)}, u32[]{:S(2)}) collective-permute-start(bf16[384,384]{1,0:T(8,128)(2,1)S(1)} %get-tuple-element.167), channel_id=1, source_target_pairs={{0,16},{16,0},{1,17},{17,1},{2,18},{18,2},{3,19},{19,3},{4,20},{20... | collective-permute-start | bytes 884744 | tf_op jit(solution)/shard_map/ppermute | solution.py:647
  67.6 3.0 %collective-permute-start.13 = (bf16[384,384]{1,0:T(8,128)(2,1)S(1)}, bf16[384,384]{1,0:T(8,128)(2,1)S(1)}, u32[]{:S(2)}, u32[]{:S(2)}) collective-permute-start(bf16[384,384]{1,0:T(8,128)(2,1)S(1)} %get-tuple-element.168), channel_id=1, source_target_pairs={{0,16},{16,0},{1,17},{17,1},{2,18},{18,2},{3,19},{19,3},{4,20},{20... | collective-permute-start | bytes 884744 | tf_op jit(solution)/shard_map/ppermute | solution.py:647
  68.1 2.9 %collective-permute-start.14 = (bf16[384,384]{1,0:T(8,128)(2,1)S(1)}, bf16[384,384]{1,0:T(8,128)(2,1)S(1)}, u32[]{:S(2)}, u32[]{:S(2)}) collective-permute-start(bf16[384,384]{1,0:T(8,128)(2,1)S(1)} %get-tuple-element.169), channel_id=1, source_target_pairs={{0,16},{16,0},{1,17},{17,1},{2,18},{18,2},{3,19},{19,3},{4,20},{20... | collective-permute-start | bytes 884744 | tf_op jit(solution)/shard_map/ppermute | solution.py:647
  68.2 3.0 %collective-permute-start.15 = (bf16[384,384]{1,0:T(8,128)(2,1)S(1)}, bf16[384,384]{1,0:T(8,128)(2,1)S(1)}, u32[]{:S(2)}, u32[]{:S(2)}) collective-permute-start(bf16[384,384]{1,0:T(8,128)(2,1)S(1)} %get-tuple-element.170), channel_id=1, source_target_pairs={{0,16},{16,0},{1,17},{17,1},{2,18},{18,2},{3,19},{19,3},{4,20},{20... | collective-permute-start | bytes 884744 | tf_op jit(solution)/shard_map/ppermute | solution.py:647
  71.1 2.7 %collective-permute-start.18 = (bf16[384,192]{1,0:T(8,128)(2,1)S(1)}, bf16[384,192]{1,0:T(8,128)(2,1)S(1)}, u32[]{:S(2)}, u32[]{:S(2)}) collective-permute-start(bf16[384,192]{1,0:T(8,128)(2,1)S(1)} %get-tuple-element.178), channel_id=1, source_target_pairs={{0,16},{16,0},{1,17},{17,1},{2,18},{18,2},{3,19},{19,3},{4,20},{20... | collective-permute-start | bytes 442376 | tf_op jit(solution)/shard_map/ppermute | solution.py:647
  71.2 2.6 %collective-permute-start.19 = (bf16[384,192]{1,0:T(8,128)(2,1)S(1)}, bf16[384,192]{1,0:T(8,128)(2,1)S(1)}, u32[]{:S(2)}, u32[]{:S(2)}) collective-permute-start(bf16[384,192]{1,0:T(8,128)(2,1)S(1)} %get-tuple-element.179), channel_id=1, source_target_pairs={{0,16},{16,0},{1,17},{17,1},{2,18},{18,2},{3,19},{19,3},{4,20},{20... | collective-permute-start | bytes 442376 | tf_op jit(solution)/shard_map/ppermute | solution.py:647
  72.0 2.3 %collective-permute-start.20 = (bf16[384,192]{1,0:T(8,128)(2,1)S(1)}, bf16[384,192]{1,0:T(8,128)(2,1)S(1)}, u32[]{:S(2)}, u32[]{:S(2)}) collective-permute-start(bf16[384,192]{1,0:T(8,128)(2,1)S(1)} %get-tuple-element.180), channel_id=1, source_target_pairs={{0,16},{16,0},{1,17},{17,1},{2,18},{18,2},{3,19},{19,3},{4,20},{20... | collective-permute-start | bytes 442376 | tf_op jit(solution)/shard_map/ppermute | solution.py:647
  72.3 16.6 %collective-permute-start.24 = (bf16[192,1536]{1,0:T(8,128)(2,1)S(1)}, bf16[192,1536]{1,0:T(8,128)(2,1)S(1)}, u32[]{:S(2)}, u32[]{:S(2)}) collective-permute-start(bf16[192,1536]{1,0:T(8,128)(2,1)S(1)} %get-tuple-element.171), channel_id=1, source_target_pairs={{0,2},{2,0},{4,6},{6,4},{8,10},{10,8},{12,14},{14,12},{1,3},{3,1},... | collective-permute-start | bytes 1769480 | tf_op jit(solution)/shard_map/ppermute | solution.py:647
  84.8 15.6 %collective-permute-start.26 = (bf16[192,1536]{1,0:T(8,128)(2,1)S(1)}, bf16[192,1536]{1,0:T(8,128)(2,1)S(1)}, u32[]{:S(2)}, u32[]{:S(2)}) collective-permute-start(bf16[192,1536]{1,0:T(8,128)(2,1)S(1)} %get-tuple-element.202), channel_id=1, source_target_pairs={{0,2},{2,0},{4,6},{6,4},{8,10},{10,8},{12,14},{14,12},{1,3},{3,1},... | collective-permute-start | bytes 1769480 | tf_op jit(solution)/shard_map/ppermute | solution.py:647
  89.1 11.3 %collective-permute-start.25 = (bf16[96,1536]{1,0:T(8,128)(2,1)S(1)}, bf16[96,1536]{1,0:T(8,128)(2,1)S(1)}, u32[]{:S(2)}, u32[]{:S(2)}) collective-permute-start(bf16[96,1536]{1,0:T(8,128)(2,1)S(1)} %get-tuple-element.195), channel_id=1, source_target_pairs={{0,4},{2,6},{4,0},{6,2},{8,12},{10,14},{12,8},{14,10},{1,5},{3,7},... | collective-permute-start | bytes 884744 | tf_op jit(solution)/shard_map/ppermute | solution.py:647
  100.5 5.7 %collective-permute-start.27 = (bf16[384,768]{1,0:T(8,128)(2,1)S(1)}, bf16[384,768]{1,0:T(8,128)(2,1)S(1)}, u32[]{:S(2)}, u32[]{:S(2)}) collective-permute-start(bf16[384,768]{1,0:T(8,128)(2,1)S(1)} %get-tuple-element.203), channel_id=1, source_target_pairs={{0,16},{16,0},{1,17},{17,1},{2,18},{18,2},{3,19},{19,3},{4,20},{20... | collective-permute-start | bytes 1769480 | tf_op jit(solution)/shard_map/ppermute | solution.py:647
  101.0 23.9 %collective-permute-start.34 = (bf16[512,768]{1,0:T(8,128)(2,1)S(1)}, bf16[512,768]{1,0:T(8,128)(2,1)S(1)}, u32[]{:S(2)}, u32[]{:S(2)}) collective-permute-start(bf16[512,768]{1,0:T(8,128)(2,1)S(1)} %get-tuple-element.222.own_ref), channel_id=1, source_target_pairs={{0,1},{1,0},{2,3},{3,2},{4,5},{5,4},{6,7},{7,6},{8,9},{9,8},{10,11... | collective-permute-start | bytes 2359304 | tf_op jit(solution)/shard_map/ppermute | solution.py:647
  102.9 11.2 %collective-permute-start.29 = (bf16[192,896]{1,0:T(8,128)(2,1)S(1)}, bf16[192,896]{1,0:T(8,128)(2,1)S(1)}, u32[]{:S(2)}, u32[]{:S(2)}) collective-permute-start(bf16[192,896]{1,0:T(8,128)(2,1)S(1)} %get-tuple-element.215), channel_id=1, source_target_pairs={{0,2},{2,0},{4,6},{6,4},{8,10},{10,8},{12,14},{14,12},{1,3},{3,1},... | collective-permute-start | bytes 1032200 | tf_op jit(solution)/shard_map/ppermute | solution.py:647
  104.4 9.6 %collective-permute-start.30 = (bf16[48,1536]{1,0:T(8,128)(2,1)S(1)}, bf16[48,1536]{1,0:T(8,128)(2,1)S(1)}, u32[]{:S(2)}, u32[]{:S(2)}) collective-permute-start(bf16[48,1536]{1,0:T(8,128)(2,1)S(1)} %get-tuple-element.212), channel_id=1, source_target_pairs={{0,8},{2,10},{4,12},{6,14},{8,0},{10,2},{12,4},{14,6},{1,9},{3,11}... | collective-permute-start | bytes 442376 | tf_op jit(solution)/shard_map/ppermute | solution.py:647
  105.2 12.0 %collective-permute-start.35 = (bf16[96,1536]{1,0:T(8,128)(2,1)S(1)}, bf16[96,1536]{1,0:T(8,128)(2,1)S(1)}, u32[]{:S(2)}, u32[]{:S(2)}) collective-permute-start(bf16[96,1536]{1,0:T(8,128)(2,1)S(1)} %get-tuple-element.209), channel_id=1, source_target_pairs={{0,4},{2,6},{4,0},{6,2},{8,12},{10,14},{12,8},{14,10},{1,5},{3,7},... | collective-permute-start | bytes 884744 | tf_op jit(solution)/shard_map/ppermute | solution.py:647
  106.3 13.3 %collective-permute-start.32 = (bf16[192,768]{1,0:T(8,128)(2,1)S(1)}, bf16[192,768]{1,0:T(8,128)(2,1)S(1)}, u32[]{:S(2)}, u32[]{:S(2)}) collective-permute-start(bf16[192,768]{1,0:T(8,128)(2,1)S(1)} %get-tuple-element.218), channel_id=1, source_target_pairs={{0,2},{2,0},{4,6},{6,4},{8,10},{10,8},{12,14},{14,12},{1,3},{3,1},... | collective-permute-start | bytes 884744 | tf_op jit(solution)/shard_map/ppermute | solution.py:647
  114.1 7.8 %collective-permute-start.31 = (bf16[96,896]{1,0:T(8,128)(2,1)S(1)}, bf16[96,896]{1,0:T(8,128)(2,1)S(1)}, u32[]{:S(2)}, u32[]{:S(2)}) collective-permute-start(bf16[96,896]{1,0:T(8,128)(2,1)S(1)} %get-tuple-element.217), channel_id=1, source_target_pairs={{0,4},{2,6},{4,0},{6,2},{8,12},{10,14},{12,8},{14,10},{1,5},{3,7},... | collective-permute-start | bytes 516104 | tf_op jit(solution)/shard_map/ppermute | solution.py:647
  117.3 10.3 %collective-permute-start.36 = (bf16[48,1536]{1,0:T(8,128)(2,1)S(1)}, bf16[48,1536]{1,0:T(8,128)(2,1)S(1)}, u32[]{:S(2)}, u32[]{:S(2)}) collective-permute-start(bf16[48,1536]{1,0:T(8,128)(2,1)S(1)} %get-tuple-element.229), channel_id=1, source_target_pairs={{0,8},{2,10},{4,12},{6,14},{8,0},{10,2},{12,4},{14,6},{1,9},{3,11}... | collective-permute-start | bytes 442376 | tf_op jit(solution)/shard_map/ppermute | solution.py:647
  122.0 7.3 %collective-permute-start.33 = (bf16[96,768]{1,0:T(8,128)(2,1)S(1)}, bf16[96,768]{1,0:T(8,128)(2,1)S(1)}, u32[]{:S(2)}, u32[]{:S(2)}) collective-permute-start(bf16[96,768]{1,0:T(8,128)(2,1)S(1)} %get-tuple-element.221), channel_id=1, source_target_pairs={{0,4},{2,6},{4,0},{6,2},{8,12},{10,14},{12,8},{14,10},{1,5},{3,7},... | collective-permute-start | bytes 442376 | tf_op jit(solution)/shard_map/ppermute | solution.py:647
  122.2 7.2 %collective-permute-start.38 = (bf16[48,896]{1,0:T(8,128)(2,1)S(1)}, bf16[48,896]{1,0:T(8,128)(2,1)S(1)}, u32[]{:S(2)}, u32[]{:S(2)}) collective-permute-start(bf16[48,896]{1,0:T(8,128)(2,1)S(1)} %get-tuple-element.240), channel_id=1, source_target_pairs={{0,8},{2,10},{4,12},{6,14},{8,0},{10,2},{12,4},{14,6},{1,9},{3,11}... | collective-permute-start | bytes 258056 | tf_op jit(solution)/shard_map/ppermute | solution.py:647
  129.3 5.5 %collective-permute-start.37 = (bf16[48,768]{1,0:T(8,128)(2,1)S(1)}, bf16[48,768]{1,0:T(8,128)(2,1)S(1)}, u32[]{:S(2)}, u32[]{:S(2)}) collective-permute-start(bf16[48,768]{1,0:T(8,128)(2,1)S(1)} %get-tuple-element.236), channel_id=1, source_target_pairs={{0,8},{2,10},{4,12},{6,14},{8,0},{10,2},{12,4},{14,6},{1,9},{3,11}... | collective-permute-start | bytes 221192 | tf_op jit(solution)/shard_map/ppermute | solution.py:647
  130.2 4.6 %collective-permute-start.39 = (f32[48]{0:T(128)S(1)}, f32[48]{0:T(128)S(1)}, u32[]{:S(2)}, u32[]{:S(2)}) collective-permute-start(f32[48]{0:T(128)S(1)} %get-tuple-element.241.gain_own), channel_id=1, source_target_pairs={{0,1},{1,0},{2,3},{3,2},{4,5},{5,4},{6,7},{7,6},{8,9},{9,8},{10,11... | collective-permute-start | bytes 584 | tf_op jit(solution)/shard_map/ppermute | solution.py:647
  (14 other events, 88.9 us)

commit v5 on v4

--- a/solution.py
+++ b/solution.py
@@ -214,7 +214,7 @@
     size, width = h1_ref.shape
     inner = mix_own.shape[1]
     hidden = up_ref.shape[1]
-    step = 256
+    step = 512
     me = lax.axis_index("mp")
     mix_ref[:, pl.ds(pl.multiple_of(me * inner, inner), inner)] = mix_own[...]
     mix_ref[:, pl.ds(pl.multiple_of((1 - me) * inner, inner), inner)] = mix_other[...]
@@ -311,7 +311,7 @@
     length, width = dh2_ref.shape
     size = length // CHUNKS
     hidden = down_ref.shape[0]
-    step = 256
+    step = 512
     gain = row_gain(gain_ref)
     number = lax.broadcasted_iota(jnp.int32, (SEGS_ROW, 1), 0)
     counts = jnp.sum((seg_ref[...] == number).astype(f32), -1, keepdims=True)

time: 136 us -> 136 us (level)
  no operation moved by 1% of the time
where the time goes in v5:
time: 136 us
  Pallas kernels  49.2 us (36%)
  waiting for transfers between devices  49 us (36%)
  starting transfers between devices  35.3 us (26%)
    pallas_call x28, Pallas kernels, whole(): pl.pallas_call(kernel, out_shape=out_shapes, in_specs=[hbm] * in_hbm + [v...  49.2 us
    ppermute x40, waiting for transfers between devices, swap(): return lax.ppermute(values, axis, [(i, i ^ bit) for i in range(count)])  49 us
    ppermute x40, starting transfers between devices, swap(): return lax.ppermute(values, axis, [(i, i ^ bit) for i in range(count)])  35.3 us
  transfers between devices with their start and end apart: 40, of which 19 were waited for; matrix products, arithmetic and copies ran while one was open for 0% of the time, Pallas kernels for 31%

profile of v5, /device:TPU:0, one launch (start us, length us, event | category | flops | bytes accessed | tf_op | source)
XLA Modules:
  0.0 135.5 jit_solution(10206315890445235510)
XLA Ops:
  1.6 3.0 %collective-permute-start = (bf16[192,768]{1,0:T(8,128)(2,1)S(1)}, bf16[192,768]{1,0:T(8,128)(2,1)S(1)}, u32[]{:S(2)}, u32[]{:S(2)}) collective-permute-start(bf16[192,768]{1,0:T(8,128)(2,1)S(1)} %constant_dynamic-slice_fusion), channel_id=1, source_target_pairs={{0,1},{1,0},{2,3},{3,2},{4,5},{5,4},{6,7},{7,6},{8,9},{9,8},{10,11... | collective-permute-start | bytes 884744 | tf_op jit(solution)/shard_map/ppermute | solution.py:647
  4.7 10.0 %attention.1 = (bf16[512,768]{1,0:T(8,128)(2,1)}, bf16[512,384]{1,0:T(8,128)(2,1)}, bf16[512,384]{1,0:T(8,128)(2,1)}, bf16[512,384]{1,0:T(8,128)(2,1)}, bf16[6,5...) custom-call(bf16[512,768]{1,0:T(8,128)(2,1)} %bitcast.13, ...), custom_call_target="tpu_custom_call" | custom-call | flops 1 | bytes 1 | tf_op jit(solution)/shard_map/attention/pallas_call | solution.py:627
  14.9 2.0 %collective-permute-start.2 = (bf16[256,384]{1,0:T(8,128)(2,1)S(1)}, bf16[256,384]{1,0:T(8,128)(2,1)S(1)}, u32[]{:S(2)}, u32[]{:S(2)}) collective-permute-start(bf16[256,384]{1,0:T(8,128)(2,1)S(1)} %get-tuple-element.133.mix_own), channel_id=1, source_target_pairs={{0,1},{1,0},{2,3},{3,2},{4,5},{5,4},{6,7},{7,6},{8,9},{9,8},{10,11... | collective-permute-start | bytes 589832 | tf_op jit(solution)/shard_map/ppermute | solution.py:647
  16.9 3.1 %load.1 = (bf16[768,768]{1,0:T(8,128)(2,1)S(1)}, bf16[768,1536]{1,0:T(8,128)(2,1)S(1)}, bf16[1536,768]{1,0:T(8,128)(2,1)S(1)}, bf16[768,768]{1,0:T(8,128)(2,1)S(1)}) custom-call(bf16[384,768]{1,0:T(8,128)(2,1)} %wo_hbm.1, bf16[768,1536]{1,0:T(8,128)(2,1)} %up_hbm.1, bf16[1536,768]{1,0:T(8,128)(2,1)} %down_hbm.1, bf16[768,768]{1,0:T(8,128)(2,1)} %proj_hbm.1, ...), custom_call_target="tpu_custom_call" | custom-call | flops 1 | bytes 1 | tf_op jit(solution)/shard_map/load/pallas_call | solution.py:627
  20.0 2.6 %collective-permute-done.4.mix_other = bf16[256,384]{1,0:T(8,128)(2,1)S(1)} collective-permute-done((bf16[256,384]{1,0:T(8,128)(2,1)S(1)}, bf16[256,384]{1,0:T(8,128)(2,1)S(1)}, u32[]{:S(2)}, u32[]{:S(2)}) %collective-permute-start.4) | collective-permute-done | bytes 196640 | tf_op jit(solution)/shard_map/ppermute | solution.py:647
  22.6 3.3 %feed_forward.3 = (f32[256,768]{1,0:T(8,128)S(1)}, bf16[256,768]{1,0:T(8,128)(2,1)S(1)}, bf16[256,1536]{1,0:T(8,128)(2,1)S(1)}, f32[256,1536]{1,0:T(8,128)S(1)}, bf16[256,768]{1,0:T(8,128)(2,1)S(1)}) custom-call(bf16[512,768]{1,0:T(8,128)(2,1)S(1)} %get-tuple-element.137.tok_ref, bf16[768,768]{1,0:T(8,128)(2,1)S(1)} %get-tuple-element.138.wo_ref.refs_4_, ...), custom_call_target="tpu_custom_call" | custom-call | flops 1 | bytes 1 | tf_op jit(solution)/shard_map/feed_forward/pallas_call | solution.py:627
  26.3 3.3 %feed_forward.2 = (f32[256,768]{1,0:T(8,128)S(1)}, bf16[256,768]{1,0:T(8,128)(2,1)S(1)}, bf16[256,1536]{1,0:T(8,128)(2,1)S(1)}, f32[256,1536]{1,0:T(8,128)S(1)}, bf16[256,768]{1,0:T(8,128)(2,1)S(1)}) custom-call(bf16[512,768]{1,0:T(8,128)(2,1)S(1)} %get-tuple-element.137.tok_ref, bf16[768,768]{1,0:T(8,128)(2,1)S(1)} %get-tuple-element.138.wo_ref.refs_4_, ...), custom_call_target="tpu_custom_call" | custom-call | flops 1 | bytes 1 | tf_op jit(solution)/shard_map/feed_forward/pallas_call | solution.py:627
  29.6 1.7 %collective-permute-start.3 = (bf16[256,768]{1,0:T(8,128)(2,1)S(1)}, bf16[256,768]{1,0:T(8,128)(2,1)S(1)}, u32[]{:S(2)}, u32[]{:S(2)}) collective-permute-start(bf16[256,768]{1,0:T(8,128)(2,1)S(1)} %get-tuple-element.142.own_ref), channel_id=1, source_target_pairs={{0,1},{1,0},{2,3},{3,2},{4,5},{5,4},{6,7},{7,6},{8,9},{9,8},{10,11... | collective-permute-start | bytes 1179656 | tf_op jit(solution)/shard_map/ppermute | solution.py:647
  31.3 6.7 %collective-permute-done.5.rec_ref = bf16[256,768]{1,0:T(8,128)(2,1)S(1)} collective-permute-done((bf16[256,768]{1,0:T(8,128)(2,1)S(1)}, bf16[256,768]{1,0:T(8,128)(2,1)S(1)}, u32[]{:S(2)}, u32[]{:S(2)}) %collective-permute-start.5) | collective-permute-done | bytes 393248 | tf_op jit(solution)/shard_map/ppermute | solution.py:647
  38.4 6.2 %collective-permute-done.3.rec_ref = bf16[256,768]{1,0:T(8,128)(2,1)S(1)} collective-permute-done((bf16[256,768]{1,0:T(8,128)(2,1)S(1)}, bf16[256,768]{1,0:T(8,128)(2,1)S(1)}, u32[]{:S(2)}, u32[]{:S(2)}) %collective-permute-start.3) | collective-permute-done | bytes 393248 | tf_op jit(solution)/shard_map/ppermute | solution.py:647
  45.0 1.6 %collective-permute-start.6 = (bf16[8,768]{1,0:T(8,128)(2,1)S(1)}, bf16[8,768]{1,0:T(8,128)(2,1)S(1)}, u32[]{:S(2)}, u32[]{:S(2)}) collective-permute-start(bf16[8,768]{1,0:T(8,128)(2,1)S(1)} %get-tuple-element.148), channel_id=1, source_target_pairs={{0,2},{2,0},{4,6},{6,4},{8,10},{10,8},{12,14},{14,12},{1,3},{3,1},... | collective-permute-start | bytes 36872 | tf_op jit(solution)/shard_map/ppermute | solution.py:647
  46.6 2.2 %collective-permute-done.6 = bf16[8,768]{1,0:T(8,128)(2,1)S(1)} collective-permute-done((bf16[8,768]{1,0:T(8,128)(2,1)S(1)}, bf16[8,768]{1,0:T(8,128)(2,1)S(1)}, u32[]{:S(2)}, u32[]{:S(2)}) %collective-permute-start.6) | collective-permute-done | bytes 12320 | tf_op jit(solution)/shard_map/ppermute | solution.py:647
  48.8 1.6 %collective-permute-start.7 = (bf16[16,768]{1,0:T(8,128)(2,1)S(1)}, bf16[16,768]{1,0:T(8,128)(2,1)S(1)}, u32[]{:S(2)}, u32[]{:S(2)}) collective-permute-start(bf16[16,768]{1,0:T(8,128)(2,1)S(1)} %get-tuple-element.261), channel_id=1, source_target_pairs={{0,4},{2,6},{4,0},{6,2},{8,12},{10,14},{12,8},{14,10},{1,5},{3,7},... | collective-permute-start | bytes 73736 | tf_op jit(solution)/shard_map/ppermute | solution.py:647
  50.3 2.5 %collective-permute-start.9 = (bf16[16,768]{1,0:T(8,128)(2,1)S(1)}, bf16[16,768]{1,0:T(8,128)(2,1)S(1)}, u32[]{:S(2)}, u32[]{:S(2)}) collective-permute-start(bf16[16,768]{1,0:T(8,128)(2,1)S(1)} %get-tuple-element.261), channel_id=1, source_target_pairs={{0,12},{2,14},{4,8},{6,10},{8,4},{10,6},{12,0},{14,2},{1,13},{3,15... | collective-permute-start | bytes 73736 | tf_op jit(solution)/shard_map/ppermute | solution.py:647
  53.0 4.9 %collective-permute-done.8 = bf16[16,768]{1,0:T(8,128)(2,1)S(1)} collective-permute-done((bf16[16,768]{1,0:T(8,128)(2,1)S(1)}, bf16[16,768]{1,0:T(8,128)(2,1)S(1)}, u32[]{:S(2)}, u32[]{:S(2)}) %collective-permute-start.8) | collective-permute-done | bytes 24608 | tf_op jit(solution)/shard_map/ppermute | solution.py:647
  59.2 2.0 %contrast.1 = (f32[1,1]{1,0:T(1,128)}, f32[48,768]{1,0:T(8,128)}, f32[8,768]{1,0:T(8,128)S(1)}) custom-call(bf16[768,768]{1,0:T(8,128)(2,1)S(1)} %get-tuple-element.136.proj_ref, bf16[128,768]{1,0:T(8,128)(2,1)S(1)} %constant_dynamic-update-slice_fusion.7.gathered_ref, s32[64]{0:T(128)S(1)} %copy-done.5), custom_call_target="tpu_custom_call" | custom-call | flops 1 | bytes 1 | tf_op jit(solution)/shard_map/contrast/pallas_call | solution.py:627
  61.3 3.9 %feed_forward_back.1 = (bf16[512,768]{1,0:T(8,128)(2,1)S(1)}, f32[512,768]{1,0:T(8,128)S(1)}, bf16[512,768]{1,0:T(8,128)(2,1)S(1)}, bf16[512,1536]{1,0:T(8,128)(2,1)S(1)}, f32[1,768]{1,0:T(1,128)S(1)}) custom-call(bf16[1536,768]{1,0:T(8,128)(2,1)S(1)} %get-tuple-element.140.down_ref, bf16[768,1536]{1,0:T(8,128)(2,1)S(1)} %get-tuple-element.139.up_ref, ...), custom_call_target="tpu_custom_call" | custom-call | flops 1 | bytes 1 | tf_op jit(solution)/shard_map/feed_forward_back/pallas_call | solution.py:627
  65.7 1.8 %down_weight.1 = (bf16[384,384]{1,0:T(8,128)(2,1)S(1)}, bf16[384,384]{1,0:T(8,128)(2,1)S(1)}, bf16[384,384]{1,0:T(8,128)(2,1)S(1)}, bf16[384,384]{1,0:T(8,128)(2,1)S(1)}, bf16[384,1536]{1,0:T(8,128)(2,1)S(1)}) custom-call(bf16[512,768]{1,0:T(8,128)(2,1)S(1)} %get-tuple-element.163.df_ref, bf16[256,1536]{1,0:T(8,128)(2,1)S(1)} %get-tuple-element.164.refs_0_, ...), custom_call_target="tpu_custom_call" | custom-call | flops 1 | bytes 1 | tf_op jit(solution)/shard_map/down_weight/pallas_call | solution.py:627
  68.6 1.8 %up_weight.1 = (bf16[384,192]{1,0:T(8,128)(2,1)S(1)}, bf16[384,192]{1,0:T(8,128)(2,1)S(1)}, bf16[384,192]{1,0:T(8,128)(2,1)S(1)}, bf16[384,192]{1,0:T(8,128)(2,1...) custom-call(bf16[512,1536]{1,0:T(8,128)(2,1)S(1)} %get-tuple-element, ...), custom_call_target="tpu_custom_call" | custom-call | flops 1 | bytes 1 | tf_op jit(solution)/shard_map/up_weight/pallas_call | solution.py:627
  72.3 1.5 %collective-permute-start.24 = (bf16[192,1536]{1,0:T(8,128)(2,1)S(1)}, bf16[192,1536]{1,0:T(8,128)(2,1)S(1)}, u32[]{:S(2)}, u32[]{:S(2)}) collective-permute-start(bf16[192,1536]{1,0:T(8,128)(2,1)S(1)} %get-tuple-element.171), channel_id=1, source_target_pairs={{0,2},{2,0},{4,6},{6,4},{8,10},{10,8},{12,14},{14,12},{1,3},{3,1},... | collective-permute-start | bytes 1769480 | tf_op jit(solution)/shard_map/ppermute | solution.py:647
  76.3 8.5 %collective-permute-done.11.refs_9_ = bf16[512,768]{1,0:T(8,128)(2,1)S(1)} collective-permute-done((bf16[512,768]{1,0:T(8,128)(2,1)S(1)}, bf16[512,768]{1,0:T(8,128)(2,1)S(1)}, u32[]{:S(2)}, u32[]{:S(2)}) %collective-permute-start.11) | collective-permute-done | bytes 786464 | tf_op jit(solution)/shard_map/ppermute | solution.py:647
  86.3 2.6 %middle_back.1 = (f32[512,768]{1,0:T(8,128)S(1)}, bf16[512,768]{1,0:T(8,128)(2,1)}, bf16[512,384]{1,0:T(8,128)(2,1)S(1)}, f32[1,768]{1,0:T(1,128)S(1)}, bf16[512...) custom-call(bf16[512,384]{1,0:T(8,128)(2,1)} %get-tuple-element.152., ...), custom_call_target="tpu_custom_call" | custom-call | flops 1 | bytes 1 | tf_op jit(solution)/shard_map/middle_back/pallas_call | solution.py:627
  89.7 10.7 %attention_back.1 = (bf16[512,768]{1,0:T(8,128)(2,1)S(1)}, bf16[384,896]{1,0:T(8,128)(2,1)S(1)}, bf16[384,896]{1,0:T(8,128)(2,1)S(1)}, bf16[384,768]{1,0:T(8,128)(2,1)S(1)}, bf16[384,768]{1,0:T(8,128)(2,1)S(1)}) custom-call(bf16[768,384]{1,0:T(8,128)(2,1)} %wq_hbm.3, bf16[768,384]{1,0:T(8,128)(2,1)} %wk_hbm.3, bf16[768,384]{1,0:T(8,128)(2,1)} %wv_hbm.3, ...), custom_call_target="tpu_custom_call" | custom-call | flops 1 | bytes 1 | tf_op jit(solution)/shard_map/attention_back/pallas_call | solution.py:627
  102.9 1.6 %collective-permute-start.29 = (bf16[192,896]{1,0:T(8,128)(2,1)S(1)}, bf16[192,896]{1,0:T(8,128)(2,1)S(1)}, u32[]{:S(2)}, u32[]{:S(2)}) collective-permute-start(bf16[192,896]{1,0:T(8,128)(2,1)S(1)} %get-tuple-element.215), channel_id=1, source_target_pairs={{0,2},{2,0},{4,6},{6,4},{8,10},{10,8},{12,14},{14,12},{1,3},{3,1},... | collective-permute-start | bytes 1032200 | tf_op jit(solution)/shard_map/ppermute | solution.py:647
  106.9 7.1 %collective-permute-done.30.rec_ref = bf16[48,1536]{1,0:T(8,128)(2,1)S(1)} collective-permute-done((bf16[48,1536]{1,0:T(8,128)(2,1)S(1)}, bf16[48,1536]{1,0:T(8,128)(2,1)S(1)}, u32[]{:S(2)}, u32[]{:S(2)}) %collective-permute-start.30) | collective-permute-done | bytes 147488 | tf_op jit(solution)/shard_map/ppermute | solution.py:647
  115.4 1.8 %collective-permute-done.35.refs_0_ = bf16[96,1536]{1,0:T(8,128)(2,1)S(1)} collective-permute-done((bf16[96,1536]{1,0:T(8,128)(2,1)S(1)}, bf16[96,1536]{1,0:T(8,128)(2,1)S(1)}, u32[]{:S(2)}, u32[]{:S(2)}) %collective-permute-start.35) | collective-permute-done | bytes 294944 | tf_op jit(solution)/shard_map/ppermute | solution.py:647
  117.3 2.4 %collective-permute-start.36 = (bf16[48,1536]{1,0:T(8,128)(2,1)S(1)}, bf16[48,1536]{1,0:T(8,128)(2,1)S(1)}, u32[]{:S(2)}, u32[]{:S(2)}) collective-permute-start(bf16[48,1536]{1,0:T(8,128)(2,1)S(1)} %get-tuple-element.229), channel_id=1, source_target_pairs={{0,8},{2,10},{4,12},{6,14},{8,0},{10,2},{12,4},{14,6},{1,9},{3,11}... | collective-permute-start | bytes 442376 | tf_op jit(solution)/shard_map/ppermute | solution.py:647
  119.6 2.3 %collective-permute-done.31.refs_0_ = bf16[96,896]{1,0:T(8,128)(2,1)S(1)} collective-permute-done((bf16[96,896]{1,0:T(8,128)(2,1)S(1)}, bf16[96,896]{1,0:T(8,128)(2,1)S(1)}, u32[]{:S(2)}, u32[]{:S(2)}) %collective-permute-start.31) | collective-permute-done | bytes 172064 | tf_op jit(solution)/shard_map/ppermute | solution.py:647
  122.2 2.6 %collective-permute-start.38 = (bf16[48,896]{1,0:T(8,128)(2,1)S(1)}, bf16[48,896]{1,0:T(8,128)(2,1)S(1)}, u32[]{:S(2)}, u32[]{:S(2)}) collective-permute-start(bf16[48,896]{1,0:T(8,128)(2,1)S(1)} %get-tuple-element.240), channel_id=1, source_target_pairs={{0,8},{2,10},{4,12},{6,14},{8,0},{10,2},{12,4},{14,6},{1,9},{3,11}... | collective-permute-start | bytes 258056 | tf_op jit(solution)/shard_map/ppermute | solution.py:647
  124.8 1.7 %last.1 = f32[512,768]{1,0:T(8,128)} custom-call(bf16[512,768]{1,0:T(8,128)(2,1)S(1)} %get-tuple-element.137.tok_ref, bf16[512,768]{1,0:T(8,128)(2,1)S(1)} %get-tuple-element.222.own_ref, f32[512,768]{1,0:T(8,128)S(1)} %get-tuple-element.223.dh1_ref, f32[768]{0:T(1024)S(1)} %copy-done.4, bf16[512,768]{1,0:T(8,128)(2,1)S(1)} %collective-permute-done.34.rec_ref), custom_call_target="tpu_custom_call" | custom-call | flops 1 | bytes 1 | tf_op jit(solution)/shard_map/last/pallas_call | solution.py:627
  130.2 3.1 %collective-permute-start.39 = (f32[48]{0:T(128)S(1)}, f32[48]{0:T(128)S(1)}, u32[]{:S(2)}, u32[]{:S(2)}) collective-permute-start(f32[48]{0:T(128)S(1)} %get-tuple-element.241.gain_own), channel_id=1, source_target_pairs={{0,1},{1,0},{2,3},{3,2},{4,5},{5,4},{6,7},{7,6},{8,9},{9,8},{10,11... | collective-permute-start | bytes 584 | tf_op jit(solution)/shard_map/ppermute | solution.py:647
  133.3 1.5 %collective-permute-done.39.gain_rec = f32[48]{0:T(128)S(1)} collective-permute-done((f32[48]{0:T(128)S(1)}, f32[48]{0:T(128)S(1)}, u32[]{:S(2)}, u32[]{:S(2)}) %collective-permute-start.39) | collective-permute-done | bytes 224 | tf_op jit(solution)/shard_map/ppermute | solution.py:647
  (95 shorter events, 23.0 us)
Async XLA Ops:
  1.6 13.1 %collective-permute-start = (bf16[192,768]{1,0:T(8,128)(2,1)S(1)}, bf16[192,768]{1,0:T(8,128)(2,1)S(1)}, u32[]{:S(2)}, u32[]{:S(2)}) collective-permute-start(bf16[192,768]{1,0:T(8,128)(2,1)S(1)} %constant_dynamic-slice_fusion), channel_id=1, source_target_pairs={{0,1},{1,0},{2,3},{3,2},{4,5},{5,4},{6,7},{7,6},{8,9},{9,8},{10,11... | collective-permute-start | bytes 884744 | tf_op jit(solution)/shard_map/ppermute | solution.py:647
  14.8 7.8 %collective-permute-start.4 = (bf16[256,384]{1,0:T(8,128)(2,1)S(1)}, bf16[256,384]{1,0:T(8,128)(2,1)S(1)}, u32[]{:S(2)}, u32[]{:S(2)}) collective-permute-start(bf16[256,384]{1,0:T(8,128)(2,1)S(1)} %get-tuple-element.144.mix_own), channel_id=1, source_target_pairs={{0,1},{1,0},{2,3},{3,2},{4,5},{5,4},{6,7},{7,6},{8,9},{9,8},{10,11... | collective-permute-start | bytes 589832 | tf_op jit(solution)/shard_map/ppermute | solution.py:647
  14.9 11.4 %collective-permute-start.2 = (bf16[256,384]{1,0:T(8,128)(2,1)S(1)}, bf16[256,384]{1,0:T(8,128)(2,1)S(1)}, u32[]{:S(2)}, u32[]{:S(2)}) collective-permute-start(bf16[256,384]{1,0:T(8,128)(2,1)S(1)} %get-tuple-element.133.mix_own), channel_id=1, source_target_pairs={{0,1},{1,0},{2,3},{3,2},{4,5},{5,4},{6,7},{7,6},{8,9},{9,8},{10,11... | collective-permute-start | bytes 589832 | tf_op jit(solution)/shard_map/ppermute | solution.py:647
  25.9 12.1 %collective-permute-start.5 = (bf16[256,768]{1,0:T(8,128)(2,1)S(1)}, bf16[256,768]{1,0:T(8,128)(2,1)S(1)}, u32[]{:S(2)}, u32[]{:S(2)}) collective-permute-start(bf16[256,768]{1,0:T(8,128)(2,1)S(1)} %get-tuple-element.146.own_ref), channel_id=1, source_target_pairs={{0,1},{1,0},{2,3},{3,2},{4,5},{5,4},{6,7},{7,6},{8,9},{9,8},{10,11... | collective-permute-start | bytes 1179656 | tf_op jit(solution)/shard_map/ppermute | solution.py:647
  29.6 15.0 %collective-permute-start.3 = (bf16[256,768]{1,0:T(8,128)(2,1)S(1)}, bf16[256,768]{1,0:T(8,128)(2,1)S(1)}, u32[]{:S(2)}, u32[]{:S(2)}) collective-permute-start(bf16[256,768]{1,0:T(8,128)(2,1)S(1)} %get-tuple-element.142.own_ref), channel_id=1, source_target_pairs={{0,1},{1,0},{2,3},{3,2},{4,5},{5,4},{6,7},{7,6},{8,9},{9,8},{10,11... | collective-permute-start | bytes 1179656 | tf_op jit(solution)/shard_map/ppermute | solution.py:647
  45.0 3.8 %collective-permute-start.6 = (bf16[8,768]{1,0:T(8,128)(2,1)S(1)}, bf16[8,768]{1,0:T(8,128)(2,1)S(1)}, u32[]{:S(2)}, u32[]{:S(2)}) collective-permute-start(bf16[8,768]{1,0:T(8,128)(2,1)S(1)} %get-tuple-element.148), channel_id=1, source_target_pairs={{0,2},{2,0},{4,6},{6,4},{8,10},{10,8},{12,14},{14,12},{1,3},{3,1},... | collective-permute-start | bytes 36872 | tf_op jit(solution)/shard_map/ppermute | solution.py:647
  48.8 4.2 %collective-permute-start.7 = (bf16[16,768]{1,0:T(8,128)(2,1)S(1)}, bf16[16,768]{1,0:T(8,128)(2,1)S(1)}, u32[]{:S(2)}, u32[]{:S(2)}) collective-permute-start(bf16[16,768]{1,0:T(8,128)(2,1)S(1)} %get-tuple-element.261), channel_id=1, source_target_pairs={{0,4},{2,6},{4,0},{6,2},{8,12},{10,14},{12,8},{14,10},{1,5},{3,7},... | collective-permute-start | bytes 73736 | tf_op jit(solution)/shard_map/ppermute | solution.py:647
  50.3 7.5 %collective-permute-start.9 = (bf16[16,768]{1,0:T(8,128)(2,1)S(1)}, bf16[16,768]{1,0:T(8,128)(2,1)S(1)}, u32[]{:S(2)}, u32[]{:S(2)}) collective-permute-start(bf16[16,768]{1,0:T(8,128)(2,1)S(1)} %get-tuple-element.261), channel_id=1, source_target_pairs={{0,12},{2,14},{4,8},{6,10},{8,4},{10,6},{12,0},{14,2},{1,13},{3,15... | collective-permute-start | bytes 73736 | tf_op jit(solution)/shard_map/ppermute | solution.py:647
  52.8 5.0 %collective-permute-start.8 = (bf16[16,768]{1,0:T(8,128)(2,1)S(1)}, bf16[16,768]{1,0:T(8,128)(2,1)S(1)}, u32[]{:S(2)}, u32[]{:S(2)}) collective-permute-start(bf16[16,768]{1,0:T(8,128)(2,1)S(1)} %get-tuple-element.261), channel_id=1, source_target_pairs={{0,8},{2,10},{4,12},{6,14},{8,0},{10,2},{12,4},{14,6},{1,9},{3,11}... | collective-permute-start | bytes 73736 | tf_op jit(solution)/shard_map/ppermute | solution.py:647
  65.1 19.6 %collective-permute-start.11 = (bf16[512,768]{1,0:T(8,128)(2,1)S(1)}, bf16[512,768]{1,0:T(8,128)(2,1)S(1)}, u32[]{:S(2)}, u32[]{:S(2)}) collective-permute-start(bf16[512,768]{1,0:T(8,128)(2,1)S(1)} %get-tuple-element.161.refs_5_), channel_id=1, source_target_pairs={{0,1},{1,0},{2,3},{3,2},{4,5},{5,4},{6,7},{7,6},{8,9},{9,8},{10,11... | collective-permute-start | bytes 2359304 | tf_op jit(solution)/shard_map/ppermute | solution.py:647
  67.6 2.9 %collective-permute-start.12 = (bf16[384,384]{1,0:T(8,128)(2,1)S(1)}, bf16[384,384]{1,0:T(8,128)(2,1)S(1)}, u32[]{:S(2)}, u32[]{:S(2)}) collective-permute-start(bf16[384,384]{1,0:T(8,128)(2,1)S(1)} %get-tuple-element.167), channel_id=1, source_target_pairs={{0,16},{16,0},{1,17},{17,1},{2,18},{18,2},{3,19},{19,3},{4,20},{20... | collective-permute-start | bytes 884744 | tf_op jit(solution)/shard_map/ppermute | solution.py:647
  67.6 3.0 %collective-permute-start.13 = (bf16[384,384]{1,0:T(8,128)(2,1)S(1)}, bf16[384,384]{1,0:T(8,128)(2,1)S(1)}, u32[]{:S(2)}, u32[]{:S(2)}) collective-permute-start(bf16[384,384]{1,0:T(8,128)(2,1)S(1)} %get-tuple-element.168), channel_id=1, source_target_pairs={{0,16},{16,0},{1,17},{17,1},{2,18},{18,2},{3,19},{19,3},{4,20},{20... | collective-permute-start | bytes 884744 | tf_op jit(solution)/shard_map/ppermute | solution.py:647
  68.1 2.9 %collective-permute-start.14 = (bf16[384,384]{1,0:T(8,128)(2,1)S(1)}, bf16[384,384]{1,0:T(8,128)(2,1)S(1)}, u32[]{:S(2)}, u32[]{:S(2)}) collective-permute-start(bf16[384,384]{1,0:T(8,128)(2,1)S(1)} %get-tuple-element.169), channel_id=1, source_target_pairs={{0,16},{16,0},{1,17},{17,1},{2,18},{18,2},{3,19},{19,3},{4,20},{20... | collective-permute-start | bytes 884744 | tf_op jit(solution)/shard_map/ppermute | solution.py:647
  68.2 3.0 %collective-permute-start.15 = (bf16[384,384]{1,0:T(8,128)(2,1)S(1)}, bf16[384,384]{1,0:T(8,128)(2,1)S(1)}, u32[]{:S(2)}, u32[]{:S(2)}) collective-permute-start(bf16[384,384]{1,0:T(8,128)(2,1)S(1)} %get-tuple-element.170), channel_id=1, source_target_pairs={{0,16},{16,0},{1,17},{17,1},{2,18},{18,2},{3,19},{19,3},{4,20},{20... | collective-permute-start | bytes 884744 | tf_op jit(solution)/shard_map/ppermute | solution.py:647
  71.1 2.7 %collective-permute-start.18 = (bf16[384,192]{1,0:T(8,128)(2,1)S(1)}, bf16[384,192]{1,0:T(8,128)(2,1)S(1)}, u32[]{:S(2)}, u32[]{:S(2)}) collective-permute-start(bf16[384,192]{1,0:T(8,128)(2,1)S(1)} %get-tuple-element.178), channel_id=1, source_target_pairs={{0,16},{16,0},{1,17},{17,1},{2,18},{18,2},{3,19},{19,3},{4,20},{20... | collective-permute-start | bytes 442376 | tf_op jit(solution)/shard_map/ppermute | solution.py:647
  71.2 2.6 %collective-permute-start.19 = (bf16[384,192]{1,0:T(8,128)(2,1)S(1)}, bf16[384,192]{1,0:T(8,128)(2,1)S(1)}, u32[]{:S(2)}, u32[]{:S(2)}) collective-permute-start(bf16[384,192]{1,0:T(8,128)(2,1)S(1)} %get-tuple-element.179), channel_id=1, source_target_pairs={{0,16},{16,0},{1,17},{17,1},{2,18},{18,2},{3,19},{19,3},{4,20},{20... | collective-permute-start | bytes 442376 | tf_op jit(solution)/shard_map/ppermute | solution.py:647
  72.0 2.3 %collective-permute-start.20 = (bf16[384,192]{1,0:T(8,128)(2,1)S(1)}, bf16[384,192]{1,0:T(8,128)(2,1)S(1)}, u32[]{:S(2)}, u32[]{:S(2)}) collective-permute-start(bf16[384,192]{1,0:T(8,128)(2,1)S(1)} %get-tuple-element.180), channel_id=1, source_target_pairs={{0,16},{16,0},{1,17},{17,1},{2,18},{18,2},{3,19},{19,3},{4,20},{20... | collective-permute-start | bytes 442376 | tf_op jit(solution)/shard_map/ppermute | solution.py:647
  72.3 16.6 %collective-permute-start.24 = (bf16[192,1536]{1,0:T(8,128)(2,1)S(1)}, bf16[192,1536]{1,0:T(8,128)(2,1)S(1)}, u32[]{:S(2)}, u32[]{:S(2)}) collective-permute-start(bf16[192,1536]{1,0:T(8,128)(2,1)S(1)} %get-tuple-element.171), channel_id=1, source_target_pairs={{0,2},{2,0},{4,6},{6,4},{8,10},{10,8},{12,14},{14,12},{1,3},{3,1},... | collective-permute-start | bytes 1769480 | tf_op jit(solution)/shard_map/ppermute | solution.py:647
  84.8 15.6 %collective-permute-start.26 = (bf16[192,1536]{1,0:T(8,128)(2,1)S(1)}, bf16[192,1536]{1,0:T(8,128)(2,1)S(1)}, u32[]{:S(2)}, u32[]{:S(2)}) collective-permute-start(bf16[192,1536]{1,0:T(8,128)(2,1)S(1)} %get-tuple-element.202), channel_id=1, source_target_pairs={{0,2},{2,0},{4,6},{6,4},{8,10},{10,8},{12,14},{14,12},{1,3},{3,1},... | collective-permute-start | bytes 1769480 | tf_op jit(solution)/shard_map/ppermute | solution.py:647
  89.1 11.3 %collective-permute-start.25 = (bf16[96,1536]{1,0:T(8,128)(2,1)S(1)}, bf16[96,1536]{1,0:T(8,128)(2,1)S(1)}, u32[]{:S(2)}, u32[]{:S(2)}) collective-permute-start(bf16[96,1536]{1,0:T(8,128)(2,1)S(1)} %get-tuple-element.195), channel_id=1, source_target_pairs={{0,4},{2,6},{4,0},{6,2},{8,12},{10,14},{12,8},{14,10},{1,5},{3,7},... | collective-permute-start | bytes 884744 | tf_op jit(solution)/shard_map/ppermute | solution.py:647
  100.5 5.7 %collective-permute-start.27 = (bf16[384,768]{1,0:T(8,128)(2,1)S(1)}, bf16[384,768]{1,0:T(8,128)(2,1)S(1)}, u32[]{:S(2)}, u32[]{:S(2)}) collective-permute-start(bf16[384,768]{1,0:T(8,128)(2,1)S(1)} %get-tuple-element.203), channel_id=1, source_target_pairs={{0,16},{16,0},{1,17},{17,1},{2,18},{18,2},{3,19},{19,3},{4,20},{20... | collective-permute-start | bytes 1769480 | tf_op jit(solution)/shard_map/ppermute | solution.py:647
  101.0 23.9 %collective-permute-start.34 = (bf16[512,768]{1,0:T(8,128)(2,1)S(1)}, bf16[512,768]{1,0:T(8,128)(2,1)S(1)}, u32[]{:S(2)}, u32[]{:S(2)}) collective-permute-start(bf16[512,768]{1,0:T(8,128)(2,1)S(1)} %get-tuple-element.222.own_ref), channel_id=1, source_target_pairs={{0,1},{1,0},{2,3},{3,2},{4,5},{5,4},{6,7},{7,6},{8,9},{9,8},{10,11... | collective-permute-start | bytes 2359304 | tf_op jit(solution)/shard_map/ppermute | solution.py:647
  102.9 11.2 %collective-permute-start.29 = (bf16[192,896]{1,0:T(8,128)(2,1)S(1)}, bf16[192,896]{1,0:T(8,128)(2,1)S(1)}, u32[]{:S(2)}, u32[]{:S(2)}) collective-permute-start(bf16[192,896]{1,0:T(8,128)(2,1)S(1)} %get-tuple-element.215), channel_id=1, source_target_pairs={{0,2},{2,0},{4,6},{6,4},{8,10},{10,8},{12,14},{14,12},{1,3},{3,1},... | collective-permute-start | bytes 1032200 | tf_op jit(solution)/shard_map/ppermute | solution.py:647
  104.4 9.6 %collective-permute-start.30 = (bf16[48,1536]{1,0:T(8,128)(2,1)S(1)}, bf16[48,1536]{1,0:T(8,128)(2,1)S(1)}, u32[]{:S(2)}, u32[]{:S(2)}) collective-permute-start(bf16[48,1536]{1,0:T(8,128)(2,1)S(1)} %get-tuple-element.212), channel_id=1, source_target_pairs={{0,8},{2,10},{4,12},{6,14},{8,0},{10,2},{12,4},{14,6},{1,9},{3,11}... | collective-permute-start | bytes 442376 | tf_op jit(solution)/shard_map/ppermute | solution.py:647
  105.2 12.0 %collective-permute-start.35 = (bf16[96,1536]{1,0:T(8,128)(2,1)S(1)}, bf16[96,1536]{1,0:T(8,128)(2,1)S(1)}, u32[]{:S(2)}, u32[]{:S(2)}) collective-permute-start(bf16[96,1536]{1,0:T(8,128)(2,1)S(1)} %get-tuple-element.209), channel_id=1, source_target_pairs={{0,4},{2,6},{4,0},{6,2},{8,12},{10,14},{12,8},{14,10},{1,5},{3,7},... | collective-permute-start | bytes 884744 | tf_op jit(solution)/shard_map/ppermute | solution.py:647
  106.3 13.3 %collective-permute-start.32 = (bf16[192,768]{1,0:T(8,128)(2,1)S(1)}, bf16[192,768]{1,0:T(8,128)(2,1)S(1)}, u32[]{:S(2)}, u32[]{:S(2)}) collective-permute-start(bf16[192,768]{1,0:T(8,128)(2,1)S(1)} %get-tuple-element.218), channel_id=1, source_target_pairs={{0,2},{2,0},{4,6},{6,4},{8,10},{10,8},{12,14},{14,12},{1,3},{3,1},... | collective-permute-start | bytes 884744 | tf_op jit(solution)/shard_map/ppermute | solution.py:647
  114.1 7.8 %collective-permute-start.31 = (bf16[96,896]{1,0:T(8,128)(2,1)S(1)}, bf16[96,896]{1,0:T(8,128)(2,1)S(1)}, u32[]{:S(2)}, u32[]{:S(2)}) collective-permute-start(bf16[96,896]{1,0:T(8,128)(2,1)S(1)} %get-tuple-element.217), channel_id=1, source_target_pairs={{0,4},{2,6},{4,0},{6,2},{8,12},{10,14},{12,8},{14,10},{1,5},{3,7},... | collective-permute-start | bytes 516104 | tf_op jit(solution)/shard_map/ppermute | solution.py:647
  117.3 10.3 %collective-permute-start.36 = (bf16[48,1536]{1,0:T(8,128)(2,1)S(1)}, bf16[48,1536]{1,0:T(8,128)(2,1)S(1)}, u32[]{:S(2)}, u32[]{:S(2)}) collective-permute-start(bf16[48,1536]{1,0:T(8,128)(2,1)S(1)} %get-tuple-element.229), channel_id=1, source_target_pairs={{0,8},{2,10},{4,12},{6,14},{8,0},{10,2},{12,4},{14,6},{1,9},{3,11}... | collective-permute-start | bytes 442376 | tf_op jit(solution)/shard_map/ppermute | solution.py:647
  122.0 7.3 %collective-permute-start.33 = (bf16[96,768]{1,0:T(8,128)(2,1)S(1)}, bf16[96,768]{1,0:T(8,128)(2,1)S(1)}, u32[]{:S(2)}, u32[]{:S(2)}) collective-permute-start(bf16[96,768]{1,0:T(8,128)(2,1)S(1)} %get-tuple-element.221), channel_id=1, source_target_pairs={{0,4},{2,6},{4,0},{6,2},{8,12},{10,14},{12,8},{14,10},{1,5},{3,7},... | collective-permute-start | bytes 442376 | tf_op jit(solution)/shard_map/ppermute | solution.py:647
  122.2 7.2 %collective-permute-start.38 = (bf16[48,896]{1,0:T(8,128)(2,1)S(1)}, bf16[48,896]{1,0:T(8,128)(2,1)S(1)}, u32[]{:S(2)}, u32[]{:S(2)}) collective-permute-start(bf16[48,896]{1,0:T(8,128)(2,1)S(1)} %get-tuple-element.240), channel_id=1, source_target_pairs={{0,8},{2,10},{4,12},{6,14},{8,0},{10,2},{12,4},{14,6},{1,9},{3,11}... | collective-permute-start | bytes 258056 | tf_op jit(solution)/shard_map/ppermute | solution.py:647
  129.3 5.5 %collective-permute-start.37 = (bf16[48,768]{1,0:T(8,128)(2,1)S(1)}, bf16[48,768]{1,0:T(8,128)(2,1)S(1)}, u32[]{:S(2)}, u32[]{:S(2)}) collective-permute-start(bf16[48,768]{1,0:T(8,128)(2,1)S(1)} %get-tuple-element.236), channel_id=1, source_target_pairs={{0,8},{2,10},{4,12},{6,14},{8,0},{10,2},{12,4},{14,6},{1,9},{3,11}... | collective-permute-start | bytes 221192 | tf_op jit(solution)/shard_map/ppermute | solution.py:647
  130.2 4.6 %collective-permute-start.39 = (f32[48]{0:T(128)S(1)}, f32[48]{0:T(128)S(1)}, u32[]{:S(2)}, u32[]{:S(2)}) collective-permute-start(f32[48]{0:T(128)S(1)} %get-tuple-element.241.gain_own), channel_id=1, source_target_pairs={{0,1},{1,0},{2,3},{3,2},{4,5},{5,4},{6,7},{7,6},{8,9},{9,8},{10,11... | collective-permute-start | bytes 584 | tf_op jit(solution)/shard_map/ppermute | solution.py:647
  (14 other events, 88.9 us)
